TPU v7x, 32 devices: a whole 2x2x4 slice. The times are simulated.
32 devices in a mesh: row: 2 (over core), col: 16 (over z, y, x).
Axes of the slice: x: 2, y: 2, z: 4, core: 2. Of those that a mesh axis runs over, the one named last changes fastest.
Arguments:
- features: bfloat16 [8192, 128], P(('row', 'col')), may hold values from -6 to 6
- weight: bfloat16 [128, 256], replicated, may hold values from -0.5 to 0.5
- bias_vector: float32 [256], replicated, may hold values from -3 to 3
- cotangent: bfloat16 [8192, 256], P(('row', 'col')), may hold values from -6 to 6
- degrees: int32 [8192], P(('row', 'col')), may hold values from 1 to 255
- adjacency_tiles: bfloat16 [2, 16, 128, 128, 128], P('row', 'col'), may hold values from 0 to 1, as said below
- tile_positions: int32 [2, 16, 128], P('row', 'col'), may hold values from 0 to 127, as said below
- tile_counts: int32 [2, 16], P('row', 'col'), may hold values from 16 to 128, as said below
Outputs:
- activations: bfloat16 [8192, 256], P(('row', 'col'))
- grad_features: bfloat16 [8192, 128], P(('row', 'col'))
- grad_weight: float32 [128, 256], replicated
- grad_bias: float32 [256], replicated
Inputs may be any that keep to these rules, and one draw needn't show every extreme that they name: `tile_positions`: the first tile_counts[r, c] positions of device (r, c) are distinct; each position q stands for row block q // 4 and column block q % 4 of that device. `tile_counts`: some device has all 128 slots live. `adjacency_tiles`: entries are 0 or 1.
All inputs are finite; a program needn't handle non-finite values.
Results may differ from a plain program's by a relative error of at most 0.015.
Values may be sent and summed in bfloat16 or wider, within the bound.
No kernel may reach another device: no remote copies, remote signals or barrier semaphores. Data moves between devices by JAX's collectives and lax.ppermute only.
A program may use at most 128 MiB of HBM per device.

v0:
```python
import jax
import jax.numpy as jnp
from jax import lax
from jax.sharding import PartitionSpec as P

BLOCK = 128


def split_three(values):
    upper = values.astype(jnp.bfloat16)
    rest = values - upper.astype(jnp.float32)
    middle = rest.astype(jnp.bfloat16)
    lower = (rest - middle.astype(jnp.float32)).astype(jnp.bfloat16)
    return (upper, middle, lower)


def spread(contrib, targets, active, slots, columns):
    selector = (
        (targets[None, :] == jnp.arange(slots, dtype=jnp.int32)[:, None]).astype(jnp.float32)
        * active[None, :]
    ).astype(jnp.bfloat16)
    flattened = contrib.reshape(contrib.shape[0], -1)
    pieces = split_three(flattened)
    summed = jnp.dot(selector, pieces[0], preferred_element_type=jnp.float32)
    summed = summed + jnp.dot(selector, pieces[1], preferred_element_type=jnp.float32)
    summed = summed + jnp.dot(selector, pieces[2], preferred_element_type=jnp.float32)
    return summed.reshape(slots * BLOCK, columns)


def tile_product(form, tile_data, picked):
    if picked.dtype == jnp.bfloat16:
        return jnp.einsum(form, tile_data, picked, preferred_element_type=jnp.float32)
    pieces = split_three(picked)
    first = jnp.einsum(form, tile_data, pieces[0], preferred_element_type=jnp.float32)
    second = jnp.einsum(form, tile_data, pieces[1], preferred_element_type=jnp.float32)
    third = jnp.einsum(form, tile_data, pieces[2], preferred_element_type=jnp.float32)
    return first + second + third


def per_device(
    features, weight, bias_vector, cotangent, degrees, adjacency_tiles, tile_positions, tile_counts
):
    tile_data = adjacency_tiles[0, 0]
    positions = tile_positions[0, 0]
    tile_total = tile_counts[0, 0]
    row_devices = lax.axis_size("row")
    col_devices = lax.axis_size("col")
    local_rows = features.shape[0]
    per_part = local_rows // BLOCK
    col_slots = row_devices * per_part
    row_slots = col_devices * per_part
    row_block = positions // col_slots
    col_block = positions % col_slots
    capacity = tile_data.shape[0]
    active = (jnp.arange(capacity, dtype=jnp.int32) < tile_total).astype(jnp.float32)
    scale_rows = lax.rsqrt(degrees.astype(jnp.float32))[:, None]
    scaled = (scale_rows * features.astype(jnp.float32)).astype(jnp.bfloat16)
    weight_full = weight.astype(jnp.float32)
    gathered = lax.all_gather(scaled, "row", axis=0, tiled=True)
    picked = jnp.take(gathered.reshape(col_slots, BLOCK, scaled.shape[1]), col_block, axis=0)
    contrib = tile_product("tij,tjf->tif", tile_data, picked)
    partial_value = spread(contrib, row_block, active, row_slots, scaled.shape[1])
    summed = lax.psum_scatter(partial_value, "col", scatter_dimension=0, tiled=True)
    hidden = scale_rows * summed
    preact = jnp.dot(hidden, weight_full, precision=lax.Precision.HIGHEST) + bias_vector[None, :]
    logistic = jax.nn.sigmoid(preact)
    activations = (preact * logistic).astype(jnp.bfloat16)
    grad_pre = cotangent.astype(jnp.float32) * logistic * (1.0 + preact * (1.0 - logistic))
    outgoing = scale_rows * jnp.dot(grad_pre, weight_full.T, precision=lax.Precision.HIGHEST)
    columns = outgoing.shape[1]
    gathered_back = lax.all_gather(outgoing, "col", axis=0, tiled=True)
    picked_back = jnp.take(gathered_back.reshape(row_slots, BLOCK, columns), row_block, axis=0)
    contrib_back = tile_product("tji,tjf->tif", tile_data, picked_back)
    partial_back = spread(contrib_back, col_block, active, col_slots, columns)
    returned = lax.psum_scatter(partial_back, "row", scatter_dimension=0, tiled=True)
    weight_term = jnp.dot(hidden.T, grad_pre, precision=lax.Precision.HIGHEST)
    grad_weight, grad_bias = lax.psum((weight_term, jnp.sum(grad_pre, axis=0)), ("row", "col"))
    grad_features = (scale_rows * returned).astype(jnp.bfloat16)
    return (activations, grad_features, grad_weight, grad_bias)


def solution(mesh):
    placed = (
        P(("row", "col"), None),
        P(),
        P(),
        P(("row", "col"), None),
        P(("row", "col")),
        P("row", "col", None, None, None),
        P("row", "col", None),
        P("row", "col"),
    )
    return jax.shard_map(
        per_device,
        mesh=mesh,
        in_specs=placed,
        out_specs=(P(("row", "col"), None), P(("row", "col"), None), P(), P()),
        check_vma=False,
    )
```

profile of v0, /device:TPU:0, one launch (start us, length us, event | category | flops | bytes accessed | tf_op | source)
XLA Modules:
  0.0 424.1 jit_solution(787410039895026161)
XLA Ops:
  7.2 0.0 copy-start
  7.2 0.0 reduce-scatter.3.cloned.1.call-start
  7.9 0.7 convert_rsqrt_fusion
  8.6 0.7 fusion.54
  9.2 0.7 compare_and_fusion
  9.9 0.9 multiply_convert_fusion.2
  10.9 2.0 all_gather.6
  12.9 3.0 gather_fusion
  15.9 9.9 %fusion.20 = f32[128,128,128]{1,2,0:T(8,128)} fusion(bf16[1,1,128,128,128]{4,3,2,1,0:T(8,128)(2,1)} %param.13, bf16[128,128,128]{2,1,0:T(8,128)(2,1)} %gather_fusion, pred[128]{0:T(512)(128)(4,1)S(1)} %get-tuple-element.17), kind=kOutput, calls=%fused_computation.35 | convolution fusion | flops 538968064 | bytes 16777344 | tf_op jit(solution)/shard_map/tij,tjf->tif/dot_general | solution.py:32
  25.8 9.3 %copy.13 = f32[128,128,128]{0,2,1:T(8,128)} copy(f32[128,128,128]{1,2,0:T(8,128)} %fusion.20) | data formatting | bytes 16777216 | tf_op jit(solution)/shard_map/tij,tjf->tif/dot_general | solution.py:32
  35.1 0.0 copy-start.3
  35.1 3.8 bitcast_convert_fusion.1
  39.0 2.0 copy-done.3
  41.0 1.9 subtract_convert_fusion.2
  42.9 1.5 fusion.33
  44.4 1.6 convolution_add_fusion.1
  46.0 1.6 convolution_add_fusion
  47.5 0.0 copy-start.7
  47.5 0.0 copy-start.8
  47.5 1.5 reshape.216
  49.1 0.0 reduce-scatter.3.cloned.1.call-update
  49.1 0.0 all-gather.2.cloned.1.call-start
  49.1 83.3 %reduce-scatter.3.cloned.1.call-done = f32[256,128]{1,0:T(8,128)} async-done(((f32[4096,128]{1,0:T(8,128)}), f32[256,128]{1,0:T(8,128)}) %reduce-scatter.3.cloned.1.call-update) | async-done | bytes 131088 | tf_op jit(solution)/shard_map/reduce_scatter | solution.py:63
  132.4 0.0 copy-done
  132.4 0.0 copy-done.7
  132.4 0.0 copy-done.8
  132.4 2.0 fusion.65
  134.4 0.9 convolution_multiply_fusion
  135.3 0.0 all-gather.2.cloned.1.call-update
  135.4 0.2 reduce-scatter.5.cloned.1.call-start
  135.6 58.2 %all-gather.2.cloned.1.call-done = f32[4096,128]{1,0:T(8,128)} async-done(((f32[256,128]{1,0:T(8,128)}), f32[4096,128]{1,0:T(8,128)}) %all-gather.2.cloned.1.call-update) | async-done | bytes 2097168 | tf_op jit(solution)/shard_map/all_gather | solution.py:71
  193.8 5.9 %gather_fusion.1 = f32[128,128,128]{2,1,0:T(8,128)} fusion(f32[32,128,128]{2,1,0:T(8,128)} %bitcast.96, s32[1024]{0:T(1024)S(1)} %pad_clamp_fusion), kind=kCustom, calls=%fused_computation.1 | custom fusion | bytes 16777728 | tf_op jit(solution)/shard_map/jit(_take)/gather | solution.py:72
  199.7 0.0 copy-start.2
  199.7 0.0 copy-start.5
  199.7 10.4 %fusion.4 = f32[128,128,128]{2,1,0:T(8,128)} fusion(f32[128,128,128]{2,1,0:T(8,128)} %gather_fusion.1, bf16[1,1,128,128,128]{4,3,2,1,0:T(8,128)(2,1)} %param.13, pred[128]{0:T(512)(128)(4,1)S(1)} %get-tuple-element.6), kind=kOutput, calls=%fused_computation.20 | convolution fusion | flops 547356672 | bytes 20971648 | tf_op jit(solution)/shard_map/tji,tjf->tif/dot_general | solution.py:35
  210.2 0.0 copy-done.2
  210.2 0.0 copy-done.5
  210.2 5.7 %fusion = f32[128,128,128]{2,1,0:T(8,128)} fusion(f32[128,128,128]{2,1,0:T(8,128)S(1)} %copy-done.2, bf16[1,1,128,128,128]{4,3,2,1,0:T(8,128)(2,1)S(1)} %copy-done.5, pred[128]{0:T(512)(128)(4,1)S(1)} %get-tuple-element.6), kind=kOutput, calls=%fused_computation.16 | convolution fusion | flops 538968064 | bytes 20971648 | tf_op jit(solution)/shard_map/tji,tjf->tif/dot_general | solution.py:34
  215.9 15.1 %add_bitcast_fusion = f32[128,128,128]{1,2,0:T(8,128)} fusion(f32[128,128,128]{2,1,0:T(8,128)} %fusion, f32[128,128,128]{2,1,0:T(8,128)} %fusion.4, bf16[1,1,128,128,128]{4,3,2,1,0:T(8,128)(2,1)} %param.13, f32[128,128,128]{2,1,0:T(8,128)} %gather_fusion.1, pred[128]{0:T(512)(128)(4,1)S(1)} %get-tuple-element.6), kind=kOutput, calls=%fused_computation.11 | convolution fusion | flops 557842432 | bytes 37748864 | tf_op jit(solution)/shard_map/tji,tjf->tif/dot_general | solution.py:36
  231.0 9.4 %copy.17 = f32[128,128,128]{0,2,1:T(8,128)} copy(f32[128,128,128]{1,2,0:T(8,128)} %add_bitcast_fusion) | data formatting | bytes 16777216 | tf_op jit(solution)/shard_map/add | solution.py:37
  240.4 0.0 copy-start.4
  240.4 3.8 bitcast_convert_fusion
  244.2 2.0 copy-done.4
  246.2 1.9 subtract_convert_fusion
  248.1 1.2 fusion.43
  249.3 0.0 copy-start.6
  249.3 0.0 copy-start.1
  249.3 1.2 convolution_add_fusion.3
  250.5 1.2 convolution_add_fusion.2
  251.7 0.9 reshape.219
  252.6 0.0 reduce-scatter.5.cloned.1.call-update
  252.6 0.0 all-reduce.2.cloned.1.call-start
  252.7 39.3 %psum.15 = f32[256]{0:T(256)} all-reduce(f32[256]{0:T(256)S(1)} %get-tuple-element.4), channel_id=1, replica_groups=mesh['row'=2,'col'=16] {'row','col'}, use_global_device_ids=true, to_apply=%region_4.5 | all-reduce | flops 256 | bytes 2048 | tf_op jit(solution)/shard_map/psum | solution.py:77
  291.9 0.0 copy-done.6
  291.9 1.1 fusion.28
  293.1 0.0 all-reduce.2.cloned.1.call-update
  293.1 0.0 reduce-scatter.5.cloned.1.call-done
  293.1 1.6 multiply_convert_fusion.1
  294.7 121.2 %all-reduce.2.cloned.1.call-done = f32[128,256]{1,0:T(8,128)} async-done(((f32[128,256]{1,0:T(8,128)}), f32[128,256]{1,0:T(8,128)}) %all-reduce.2.cloned.1.call-update) | async-done | bytes 131088 | tf_op jit(solution)/shard_map/psum | solution.py:77
  416.0 1.6 copy.24
  417.6 0.0 copy-done.1
  (2 shorter events, 0.0 us)
Async XLA Ops:
  7.2 125.3 %copy-start = (bf16[128,256]{1,0:T(8,128)(2,1)S(1)}, bf16[128,256]{1,0:T(8,128)(2,1)}, u32[]{:S(2)}) copy-start(bf16[128,256]{1,0:T(8,128)(2,1)} %param.9) | copy-start | bytes 196612
  7.2 125.3 %reduce-scatter.3.cloned.1.call-start = ((), (), s32[]{:S(2)}) async-start(), calls=%async_computation.2 | async-start | bytes 2228224 | tf_op jit(solution)/shard_map/reduce_scatter | solution.py:63
  35.1 5.8 %copy-start.3 = (f32[128,128,128]{0,2,1:T(8,128)S(1)}, f32[128,128,128]{0,2,1:T(8,128)}, u32[]{:S(2)}) copy-start(f32[128,128,128]{0,2,1:T(8,128)} %copy.13) | copy-start | bytes 25165828
  47.5 84.9 %copy-start.7 = (bf16[256,256]{1,0:T(8,128)(2,1)S(1)}, bf16[256,256]{1,0:T(8,128)(2,1)}, u32[]{:S(2)}) copy-start(bf16[256,256]{1,0:T(8,128)(2,1)} %param.11) | copy-start | bytes 393220
  47.5 84.9 %copy-start.8 = (f32[256]{0:T(256)S(1)}, f32[256]{0:T(256)}, u32[]{:S(2)}) copy-start(f32[256]{0:T(256)} %param.10) | copy-start | bytes 3076
  49.1 144.7 %all-gather.2.cloned.1.call-start = ((), (), s32[]{:S(2)}) async-start(), calls=%async_computation.3 | async-start | bytes 2228224 | tf_op jit(solution)/shard_map/all_gather | solution.py:71
  135.4 157.7 %reduce-scatter.5.cloned.1.call-start = ((), (), s32[]{:S(2)}) async-start(), calls=%async_computation.4 | async-start | bytes 393216 | tf_op jit(solution)/shard_map/reduce_scatter | solution.py:75
  199.7 10.4 %copy-start.2 = (f32[128,128,128]{2,1,0:T(8,128)S(1)}, f32[128,128,128]{2,1,0:T(8,128)}, u32[]{:S(2)}) copy-start(f32[128,128,128]{2,1,0:T(8,128)} %gather_fusion.1) | copy-start | bytes 25165828
  199.7 10.4 %copy-start.5 = (bf16[1,1,128,128,128]{4,3,2,1,0:T(8,128)(2,1)S(1)}, bf16[1,1,128,128,128]{4,3,2,1,0:T(8,128)(2,1)}, u32[]{:S(2)}) copy-start(bf16[1,1,128,128,128]{4,3,2,1,0:T(8,128)(2,1)} %param.13) | copy-start | bytes 12582916
  240.4 5.8 %copy-start.4 = (f32[128,128,128]{0,2,1:T(8,128)S(1)}, f32[128,128,128]{0,2,1:T(8,128)}, u32[]{:S(2)}) copy-start(f32[128,128,128]{0,2,1:T(8,128)} %copy.17) | copy-start | bytes 25165828
  249.3 42.7 %copy-start.6 = (f32[256,128]{1,0:T(8,128)S(1)}, f32[256,128]{1,0:T(8,128)}, u32[]{:S(2)}) copy-start(f32[256,128]{1,0:T(8,128)} %reduce-scatter.3.cloned.1.call-done) | copy-start | bytes 393220
  249.3 168.3 %copy-start.1 = (bf16[128,256]{1,0:T(8,128)(2,1)S(1)}, bf16[128,256]{1,0:T(8,128)(2,1)}, u32[]{:S(2)}) copy-start(bf16[128,256]{1,0:T(8,128)(2,1)} %param.9) | copy-start | bytes 196612
  252.6 163.4 %all-reduce.2.cloned.1.call-start = ((), (), s32[]{:S(2)}) async-start(), calls=%async_computation.5 | async-start | bytes 262144 | tf_op jit(solution)/shard_map/psum | solution.py:77
Sparse Core Ops, SparseCore 0:
  49.2 83.1 reduce-scatter.2
  135.8 57.9 all-gather.1
  252.7 6.2 reduce-scatter.4
  293.2 122.7 all-reduce.1
where the time goes:
time: 425 us; the launch traced here: 424 us
  waiting for transfers between devices  263 us (62%)
  matrix products  53.4 us (13%)
  blocking collectives  41.3 us (10%)
  local copies, waits for them, and re-layouts  35.7 us (8%)
  other arithmetic  16 us (4%)
  between operations  14.5 us (3%)
    psum x1, waiting for transfers between devices, per_device(): lax.psum((weight_term, jnp.sum(grad_pre, axis=0)), ('row', 'col'))  121 us
    reduce_scatter x1, waiting for transfers between devices, per_device(): lax.psum_scatter(partial_value, 'col', scatter_dimension=0, tiled=True)  83.3 us
    all_gather x1, waiting for transfers between devices, per_device(): gathered_back = lax.all_gather(outgoing, 'col', axis=0, tiled=True)  58.2 us
    psum x1, blocking collectives, per_device(): lax.psum((weight_term, jnp.sum(grad_pre, axis=0)), ('row', 'col'))  39.3 us
    dot_general x1, matrix products, tile_product(): jnp.einsum(form, tile_data, pieces[2], preferred_element_type=jnp.float32)  15.1 us
    dot_general x1, matrix products, tile_product(): jnp.einsum(form, tile_data, pieces[1], preferred_element_type=jnp.float32)  10.4 us
    dot_general x1, matrix products, tile_product(): jnp.einsum(form, tile_data, picked, preferred_element_type=jnp.float32)  9.91 us
    add x1, local copies, waits for them, and re-layouts, tile_product(): return first + second + third  9.37 us
  transfers between devices with their start and end apart: 4, of which 3 were waited for; matrix products, arithmetic and copies ran while one was open for 1% of the time, Pallas kernels for 0%

commit v1 on v0

v1 whole, which is shorter than its diff:
```python
import functools

import jax
import jax.numpy as jnp
from jax import lax
from jax.experimental import pallas as pl
from jax.experimental.pallas import tpu as pltpu
from jax.sharding import PartitionSpec as P

BLOCK = 128
VMEM_BYTES = 48 * 1024 * 1024
F32 = jnp.float32
BF16 = jnp.bfloat16


def other(index, step, size):
    if size & (size - 1) == 0:
        return index ^ step
    return (index + step) % size


def source(index, step, size):
    if size & (size - 1) == 0:
        return index ^ step
    return (index - step) % size


def params():
    return pltpu.CompilerParams(vmem_limit_bytes=VMEM_BYTES)


def in_hbm(values):
    return pltpu.with_memory_space_constraint(values, pltpu.HBM)


def dot(left, right, contract=((1,), (0,))):
    return lax.dot_general(left, right, (contract, ((), ())), preferred_element_type=F32)


def split_two(values):
    upper = values.astype(BF16)
    return upper, (values - upper.astype(F32)).astype(BF16)


def scale_columns(degrees_row, columns):
    row = lax.rsqrt(degrees_row.astype(F32))
    return row, jnp.transpose(jnp.broadcast_to(row, (columns, row.shape[1])))


def scale_kernel(degrees_hbm, features_hbm, out_ref, degrees_ref, features_ref, sems):
    copies = [
        pltpu.make_async_copy(degrees_hbm, degrees_ref, sems.at[0]),
        pltpu.make_async_copy(features_hbm, features_ref, sems.at[1]),
    ]
    for copy in copies:
        copy.start()
    for copy in copies:
        copy.wait()
    _, scale = scale_columns(degrees_ref[...], features_ref.shape[1])
    out_ref[...] = (scale * features_ref[...].astype(F32)).astype(BF16)


def scale_features(degrees_row, features):
    return pl.pallas_call(
        scale_kernel,
        out_shape=jax.ShapeDtypeStruct(features.shape, BF16),
        in_specs=[pl.BlockSpec(memory_space=pltpu.HBM)] * 2,
        scratch_shapes=[
            pltpu.VMEM(degrees_row.shape, degrees_row.dtype),
            pltpu.VMEM(features.shape, features.dtype),
            pltpu.SemaphoreType.DMA((2,)),
        ],
        compiler_params=params(),
        name="scale_features",
    )(in_hbm(degrees_row), in_hbm(features))


def densify_kernel(
    col_slots, positions_hbm, counts_ref, tiles_ref, out_ref, positions_ref, taken_ref, zero_ref, sems
):
    places = taken_ref.shape[0]
    live = counts_ref[0, 0]
    fetch = pltpu.make_async_copy(positions_hbm, positions_ref, sems.at[0])
    fetch.start()
    zero_ref[...] = jnp.zeros_like(zero_ref)

    def clear(place, carry):
        taken_ref[place] = 0
        return carry

    lax.fori_loop(0, places, clear, 0, unroll=8)
    fetch.wait()

    def target(place):
        if col_slots & (col_slots - 1) == 0:
            row = lax.shift_right_logical(place, col_slots.bit_length() - 1)
            column = place & (col_slots - 1)
        else:
            row, column = lax.div(place, col_slots), lax.rem(place, col_slots)
        return out_ref.at[row, :, pl.ds(pl.multiple_of(column * BLOCK, BLOCK), BLOCK)]

    def send(slot):
        place = positions_ref[0, 0, slot]
        taken_ref[place] = 1
        pltpu.make_async_copy(tiles_ref.at[slot], target(place), sems.at[1]).start()

    def send_many(group, carry):
        for step in range(8):
            send(group * 8 + step)
        return carry

    def send_one(slot, carry):
        send(slot)
        return carry

    groups = lax.shift_right_logical(live, 3)
    lax.fori_loop(0, groups, send_many, 0)
    lax.fori_loop(groups * 8, live, send_one, 0)

    def blank(place, carry):
        @pl.when(taken_ref[place] == 0)
        def _():
            pltpu.make_async_copy(zero_ref, target(place), sems.at[1]).start()

        return carry

    @pl.when(live < places)
    def _():
        lax.fori_loop(0, places, blank, 0, unroll=8)

    pltpu.make_async_copy(out_ref, out_ref, sems.at[1]).wait()


def densify(positions, counts, tiles, row_slots, col_slots):
    return pl.pallas_call(
        functools.partial(densify_kernel, col_slots),
        out_shape=jax.ShapeDtypeStruct((row_slots, BLOCK, col_slots * BLOCK), BF16),
        in_specs=[
            pl.BlockSpec(memory_space=pltpu.HBM),
            pl.BlockSpec(memory_space=pltpu.SMEM),
            pl.BlockSpec(memory_space=pltpu.HBM),
        ],
        out_specs=pl.BlockSpec(memory_space=pl.ANY),
        scratch_shapes=[
            pltpu.SMEM(positions.shape, jnp.int32),
            pltpu.SMEM((row_slots * col_slots,), jnp.int32),
            pltpu.VMEM((BLOCK, BLOCK), BF16),
            pltpu.SemaphoreType.DMA((2,)),
        ],
        compiler_params=params(),
        name="densify",
    )(in_hbm(positions), counts, tiles)


def spot(low):
    col = lax.axis_index("col")
    if low & (low - 1) == 0:
        return lax.axis_index("row"), lax.shift_right_logical(col, low.bit_length() - 1), col & (low - 1)
    return lax.axis_index("row"), lax.div(col, low), lax.rem(col, low)


def piece_columns(index, nodes):
    return pl.ds(pl.multiple_of(index * nodes, nodes), nodes)


def forward_kernel(steps, pieces, dense_ref, *refs):
    scaled, outs = refs[:pieces], refs[pieces:]
    high, low, nodes, _ = dense_ref.shape
    row, line, plane = spot(low)
    for step, onward_ref, here_ref in zip(steps, outs[::2], outs[1::2]):
        column = other(plane, step, low)
        for hop in (*far_first(high), 0):
            chunk = other(line, hop, high)
            total = None
            for piece in range(pieces):
                columns = piece_columns(source(row, piece, pieces), nodes)
                term = dot(dense_ref[chunk, column, :, columns], scaled[piece][...])
                total = term if total is None else total + term
            if hop:
                onward_ref[hop - 1] = total.astype(onward_ref.dtype)
            else:
                here_ref[...] = total.astype(here_ref.dtype)


def forward(dense, scaled, steps):
    high, _, nodes, _ = dense.shape
    pieces = len(scaled)
    width = scaled[0].shape[1]
    products = pl.pallas_call(
        functools.partial(forward_kernel, steps, pieces),
        out_shape=[
            jax.ShapeDtypeStruct(shape, BF16 if step else F32)
            for step in steps
            for shape in ((high - 1, nodes, width), (nodes, width))
        ],
        in_specs=[pl.BlockSpec(memory_space=pltpu.VMEM)] * (1 + pieces),
        compiler_params=params(),
        name="forward_product",
    )(dense, *scaled)
    return dict(zip(steps, zip(products[::2], products[1::2])))


def combine_kernel(count, *refs):
    arrays, outs = refs[:count], refs[count:]
    for hop, out_ref in enumerate(outs):
        out_ref[...] = tree_sum([array[hop].astype(F32) for array in arrays]).astype(out_ref.dtype)


def combine(arrays):
    hops, nodes, columns = arrays[0].shape
    return pl.pallas_call(
        functools.partial(combine_kernel, len(arrays)),
        out_shape=[jax.ShapeDtypeStruct((nodes, columns), BF16)] * hops,
        in_specs=[pl.BlockSpec(memory_space=pltpu.VMEM)] * len(arrays),
        compiler_params=params(),
        name="combine",
    )(*arrays)


def layer_kernel(count, *refs):
    degrees_ref, weight_ref, bias_ref, cotangent_ref = refs[count : count + 4]
    outgoing_ref, hidden_ref, preact_ref, grad_pre_ref = refs[count + 4 :]
    total = tree_sum([ref[...].astype(F32) for ref in refs[:count]])
    row, scale = scale_columns(degrees_ref[...], total.shape[1])
    hidden = scale * total
    weight = weight_ref[...]
    upper, lower = split_two(hidden)
    preact = dot(upper, weight) + dot(lower, weight) + bias_ref[...]
    logistic = 1.0 / (1.0 + jnp.exp(-preact))
    grad_pre = cotangent_ref[...].astype(F32) * logistic * (1.0 + preact * (1.0 - logistic))
    upper, lower = split_two(grad_pre)
    across = ((1,), (1,))
    back = dot(weight, upper, across) + dot(weight, lower, across)
    outgoing_ref[...] = (row * back).astype(BF16)
    hidden_ref[...] = hidden
    preact_ref[...] = preact
    grad_pre_ref[...] = grad_pre


def layer(shares, degrees_row, weight, bias_row, cotangent):
    nodes = degrees_row.shape[1]
    depth, width = weight.shape
    return pl.pallas_call(
        functools.partial(layer_kernel, len(shares)),
        out_shape=[
            jax.ShapeDtypeStruct((depth, nodes), BF16),
            jax.ShapeDtypeStruct((nodes, depth), F32),
            jax.ShapeDtypeStruct((nodes, width), F32),
            jax.ShapeDtypeStruct((nodes, width), F32),
        ],
        compiler_params=params(),
        name="layer",
    )(*shares, degrees_row, weight, bias_row, cotangent)


def results_kernel(hidden_ref, preact_ref, grad_pre_ref, activations_ref, terms_ref):
    preact = preact_ref[...]
    activations_ref[...] = (preact / (1.0 + jnp.exp(-preact))).astype(BF16)
    grad_pre = grad_pre_ref[...]
    grads = split_two(grad_pre)
    upper, lower = split_two(jnp.transpose(hidden_ref[...]))
    weight_term = dot(upper, grads[0]) + dot(lower, grads[0]) + dot(upper, grads[1])
    depth = weight_term.shape[0]
    terms_ref[0:depth, :] = weight_term.astype(BF16)
    bias_term = jnp.sum(grad_pre, axis=0, keepdims=True)
    terms_ref[depth:, :] = jnp.broadcast_to(bias_term, (16, bias_term.shape[1])).astype(BF16)


def results(hidden, preact, grad_pre):
    return pl.pallas_call(
        results_kernel,
        out_shape=[
            jax.ShapeDtypeStruct(preact.shape, BF16),
            jax.ShapeDtypeStruct((hidden.shape[1] + 16, preact.shape[1]), BF16),
        ],
        compiler_params=params(),
        name="results",
    )(hidden, preact, grad_pre)


def tree_sum(values):
    while len(values) > 1:
        values = [left + right for left, right in zip(values[::2], values[1::2])] + (
            values[-1:] if len(values) % 2 else []
        )
    return values[0]


def sum_kernel(*refs):
    refs[-1][...] = tree_sum([ref[...].astype(F32) for ref in refs[:-1]]).astype(BF16)


def sum_terms(items):
    return pl.pallas_call(
        sum_kernel,
        out_shape=jax.ShapeDtypeStruct(items[0].shape, BF16),
        compiler_params=params(),
        name="sum_terms",
    )(*items)


def stack_kernel(low, *refs):
    items, out_ref = refs[:-1], refs[-1]
    _, line, _ = spot(low)
    for step, item in enumerate(items):
        out_ref[source(line, step, len(items))] = item[...]


def stack_line(low, items):
    return pl.pallas_call(
        functools.partial(stack_kernel, low),
        out_shape=jax.ShapeDtypeStruct((len(items),) + items[0].shape, BF16),
        in_specs=[pl.BlockSpec(memory_space=pltpu.VMEM)] * len(items),
        compiler_params=params(),
        name="stack_line",
    )(*items)


def backward_kernel(steps, pieces, has_totals, dense_ref, *refs):
    stacks, inputs, outs = refs[: len(steps)], refs[len(steps) : -pieces], refs[-pieces:]
    terms = inputs[pieces if has_totals else 0 :]
    high, low, nodes, _ = dense_ref.shape
    row, _, plane = spot(low)
    for piece in range(pieces):
        columns = piece_columns(other(row, piece, pieces), nodes)
        total = inputs[piece][...] if has_totals else None
        for step, stack_ref in zip(steps, stacks):
            origin = source(plane, step, low)
            for chunk in range(high):
                term = dot(stack_ref[chunk], dense_ref[chunk, origin, :, columns])
                total = term if total is None else total + term
        depth = total.shape[0]
        outs[piece][0:depth, :] = total.astype(outs[piece].dtype)
        if terms and piece:
            outs[piece][depth:, :] = tree_sum([ref[...].astype(F32) for ref in terms]).astype(BF16)


def backward(dense, stacks, totals, terms=()):
    nodes, slots = dense.shape[2:]
    pieces = slots // nodes
    depth = next(iter(stacks.values())).shape[1]
    inputs = list(stacks.values()) + list(totals) + list(terms)

    def shape_of(piece):
        if terms and piece:
            return jax.ShapeDtypeStruct((depth + terms[0].shape[0], nodes), BF16)
        return jax.ShapeDtypeStruct((depth, nodes), F32)

    return pl.pallas_call(
        functools.partial(backward_kernel, tuple(stacks), pieces, bool(totals)),
        out_shape=[shape_of(piece) for piece in range(pieces)],
        in_specs=[pl.BlockSpec(memory_space=pltpu.VMEM)] * (1 + len(inputs)),
        compiler_params=params(),
        name="backward_product",
    )(dense, *inputs)


def finish_kernel(pieces, degrees_ref, own_ref, sent_ref, *refs):
    shares, outs = refs[: pieces - 1], refs[pieces - 1 :]
    total = own_ref[...]
    depth = total.shape[0]
    for share in shares:
        total = total + share[0:depth, :].astype(F32)
    row = lax.rsqrt(degrees_ref[...].astype(F32))
    outs[0][...] = jnp.transpose(row * total).astype(BF16)
    terms = tree_sum([ref[depth:, :].astype(F32) for ref in (sent_ref, *shares)])
    outs[1][...] = terms[0:depth]
    outs[2][...] = terms[depth : depth + 1]


def finish(degrees_row, own, sent, shares):
    depth, nodes = own.shape
    width = sent.shape[1]
    return pl.pallas_call(
        functools.partial(finish_kernel, len(shares) + 1),
        out_shape=[
            jax.ShapeDtypeStruct((nodes, depth), BF16),
            jax.ShapeDtypeStruct((depth, width), F32),
            jax.ShapeDtypeStruct((1, width), F32),
        ],
        compiler_params=params(),
        name="finish",
    )(degrees_row, own, sent, *shares)


def far_first(size):
    return range(size - 1, 0, -1)


def per_device(
    features, weight, bias_vector, cotangent, degrees, adjacency_tiles, tile_positions, tile_counts
):
    rows = lax.axis_size("row")
    cols = lax.axis_size("col")
    nodes = features.shape[0]
    per_part = nodes // BLOCK
    row_slots = cols * per_part
    col_slots = rows * per_part
    low = 4 if cols % 4 == 0 else 1
    high = cols // low

    degrees_row = degrees[None, :]

    def over_row(values, step):
        pairs = [(index, other(index, step, rows)) for index in range(rows)]
        return lax.ppermute(values, "row", pairs)

    def over_plane(values, step):
        pairs = [
            (index, index // low * low + other(index % low, step, low)) for index in range(cols)
        ]
        return lax.ppermute(values, "col", pairs)

    def over_line(values, step):
        pairs = [
            (index, other(index // low, step, high) * low + index % low) for index in range(cols)
        ]
        return lax.ppermute(values, "col", pairs)

    own = scale_features(degrees_row, features)
    scaled = [own] + [over_row(own, step) for step in range(1, rows)]
    dense = densify(
        tile_positions, tile_counts, adjacency_tiles[0, 0], row_slots, col_slots
    ).reshape(high, low, nodes, col_slots * BLOCK)

    products = forward(dense, scaled, (low - 1,)) | forward(dense, scaled, tuple(range(low - 1))[::-1])
    onward = [products[0][0]] + [over_plane(products[step][0], step) for step in far_first(low)]
    here = [products[0][1]] + [over_plane(products[step][1], step) for step in far_first(low)]
    chunks = combine(onward)
    shares = [over_line(chunks[hop - 1], hop) for hop in far_first(high)]
    outgoing, *kept = layer(here + shares, degrees_row, weight, bias_vector[None, :], cotangent)

    line = {0: outgoing} | {step: over_line(outgoing, step) for step in far_first(high)}
    activations, terms = results(*kept)
    parts = {0: terms} | {step: over_plane(terms, step) for step in far_first(low)}
    line, parts = lax.optimization_barrier((line, parts))
    stacked = stack_line(low, [line[step] for step in range(high)])
    terms = sum_terms([parts[step] for step in range(low)])
    stacks = {0: stacked} | {step: over_plane(stacked, step) for step in far_first(low)}
    parts = {0: terms} | {step: over_line(terms, step) for step in far_first(high)}
    terms = [parts[step] for step in range(high)]
    steps, totals = list(stacks), []
    for group in (steps[: low // 2], steps[low // 2 :]):
        if group:
            arrived = {step: stacks[step] for step in group}
            totals = backward(dense, arrived, totals, terms if group[-1] == steps[-1] else ())
    returned = [over_row(totals[step], step) for step in range(1, rows)]
    grad_features, grad_weight, grad_bias = finish(degrees_row, totals[0], totals[1], returned)
    return activations, grad_features, grad_weight, grad_bias[0]


def solution(mesh):
    placed = (
        P(("row", "col"), None),
        P(),
        P(),
        P(("row", "col"), None),
        P(("row", "col")),
        P("row", "col", None, None, None),
        P("row", "col", None),
        P("row", "col"),
    )
    return jax.shard_map(
        per_device,
        mesh=mesh,
        in_specs=placed,
        out_specs=(P(("row", "col"), None), P(("row", "col"), None), P(), P()),
        check_vma=False,
    )
```

time: 425 us -> 59 us (0.14)
  waiting for transfers between devices: 263 us -> 19.5 us
  matrix products: 53.4 us -> 0 us
  blocking collectives: 41.3 us -> 0 us
  local copies, waits for them, and re-layouts: 35.7 us -> 0.03 us
  starting transfers between devices: 0.34 us -> 29.8 us
  other arithmetic: 16 us -> 0 us
  between operations: 14.5 us -> 1.45 us
  Pallas kernels: 0 us -> 8.21 us
    psum x1 -> x0, waiting for transfers between devices: 121 us -> none  [per_device(): lax.psum((weight_term, jnp.sum(grad_pre, axis=0)), ('row', 'col'))]
    reduce_scatter x2 -> x0, waiting for transfers between devices: 83.3 us -> none  [the longest x1 83.3 us: per_device(): lax.psum_scatter(partial_value, 'col', scatter_dimension=0, tiled=True)]
    all_gather x1 -> x0, waiting for transfers between devices: 58.2 us -> none  [per_device(): gathered_back = lax.all_gather(outgoing, 'col', axis=0, tiled=True)]
    dot_general x13 -> x0, matrix products: 53.4 us -> none  [the longest x1 15.1 us: tile_product(): jnp.einsum(form, tile_data, pieces[2], preferred_element_type=jnp.float32)]
    psum x1 -> x0, blocking collectives: 39.3 us -> none  [per_device(): lax.psum((weight_term, jnp.sum(grad_pre, axis=0)), ('row', 'col'))]
    ppermute x0 -> x23, starting transfers between devices: none -> 29.8 us  [the longest x12 16.5 us: over_plane(): return lax.ppermute(values, 'col', pairs)]
    ppermute x0 -> x23, waiting for transfers between devices: none -> 19.5 us  [the longest x9 10.5 us: over_line(): return lax.ppermute(values, 'col', pairs)]
    convert_element_type x6 -> x0, other arithmetic: 14 us -> none  [the longest x2 7.64 us: split_three(): upper = values.astype(jnp.bfloat16)]
  transfers between devices with their start and end apart: 4 -> 23, of which waited for: 3 -> 10; matrix products, arithmetic and copies ran while one was open for 1% -> 0% of each run, Pallas kernels for 0% -> 8%
where the time goes in v1:
time: 59 us
  starting transfers between devices  29.8 us (51%)
  waiting for transfers between devices  19.5 us (33%)
  Pallas kernels  8.21 us (14%)
  between operations  1.45 us (2%)
    ppermute x12, starting transfers between devices, over_plane(): return lax.ppermute(values, 'col', pairs)  16.5 us
    ppermute x9, starting transfers between devices, over_line(): return lax.ppermute(values, 'col', pairs)  12.7 us
    ppermute x9, waiting for transfers between devices, over_line(): return lax.ppermute(values, 'col', pairs)  10.5 us
    ppermute x12, waiting for transfers between devices, over_plane(): return lax.ppermute(values, 'col', pairs)  7.6 us
    pallas_call x1, Pallas kernels, densify(): pl.pallas_call(functools.partial(densify_kernel, col_slots), out_shape=ja...  2.48 us
    pallas_call x2, Pallas kernels, forward(): pl.pallas_call(functools.partial(forward_kernel, steps, pieces), out_shap...  1.39 us
    ppermute x2, waiting for transfers between devices, over_row(): return lax.ppermute(values, 'row', pairs)  1.35 us
  transfers between devices with their start and end apart: 23, of which 10 were waited for; matrix products, arithmetic and copies ran while one was open for 0% of the time, Pallas kernels for 8%

profile of v1, /device:TPU:0, one launch (start us, length us, event | category | flops | bytes accessed | tf_op | source)
XLA Modules:
  0.0 59.0 jit_solution(1977500987649034398)
XLA Ops:
  0.6 1.0 %scale_features.1.refs_0_ = bf16[256,128]{1,0:T(8,128)(2,1)S(1)} custom-call(s32[1,256]{1,0:T(1,128)} %bitcast.9, bf16[256,128]{1,0:T(8,128)(2,1)} %features_hbm.1), custom_call_target="tpu_custom_call" | custom-call | tf_op jit(solution)/shard_map/scale_features/pallas_call | solution.py:64
  1.6 0.5 collective-permute-start
  2.8 2.5 %densify.1 = bf16[32,128,512]{2,1,0:T(8,128)(2,1)S(1)} custom-call(s32[1,1,128]{2,1,0:T(1,128)} %positions_hbm.1, s32[1,1]{1,0:T(1,128)S(6)} %copy.12.counts_ref, bf16[128,128,128]{2,1,0:T(8,128)(2,1)} %bitcast.13), custom_call_target="tpu_custom_call" | custom-call | tf_op jit(solution)/shard_map/densify/pallas_call | solution.py:135
  5.3 0.0 collective-permute-done.refs_1_
  5.3 0.0 copy-start
  5.3 0.0 copy-start.1
  5.3 0.0 copy-start.2
  5.3 0.0 copy-start.3
  5.3 0.4 forward_product.3
  5.8 3.4 %collective-permute-start.4 = (bf16[3,256,128]{2,1,0:T(8,128)(2,1)S(1)}, bf16[3,256,128]{2,1,0:T(8,128)(2,1)S(1)}, u32[]{:S(2)}, u32[]{:S(2)}) collective-permute-start(bf16[3,256,128]{2,1,0:T(8,128)(2,1)S(1)} %get-tuple-element.41), channel_id=1, source_target_pairs={{0,3},{1,2},{2,1},{3,0},{4,7},{5,6},{6,5},{7,4},{8,11},{9,10},{10,... | collective-permute-start | bytes 589832 | tf_op jit(solution)/shard_map/ppermute | solution.py:412
  9.2 1.0 %forward_product.2 = (bf16[3,256,128]{2,1,0:T(8,128)(2,1)S(1)}, bf16[256,128]{1,0:T(8,128)(2,1)S(1)}, bf16[3,256,128]{2,1,0:T(8,128)(2,1)S(1)}, bf16[256,128]{1,...) custom-call(bf16[4,4,256,512]{3,2,1,0:T(8,128)(2,1)S(1)} %bitcast.6, ...), custom_call_target="tpu_custom_call" | custom-call | tf_op jit(solution)/shard_map/forward_product/pallas_call | solution.py:189
  10.2 0.6 %collective-permute-start.5 = (bf16[3,256,128]{2,1,0:T(8,128)(2,1)S(1)}, bf16[3,256,128]{2,1,0:T(8,128)(2,1)S(1)}, u32[]{:S(2)}, u32[]{:S(2)}) collective-permute-start(bf16[3,256,128]{2,1,0:T(8,128)(2,1)S(1)} %get-tuple-element.42), channel_id=1, source_target_pairs={{0,2},{1,3},{2,0},{3,1},{4,6},{5,7},{6,4},{7,5},{8,10},{9,11},{10,... | collective-permute-start | bytes 589832 | tf_op jit(solution)/shard_map/ppermute | solution.py:412
  10.8 0.5 collective-permute-start.6
  11.3 2.4 %collective-permute-start.1 = (bf16[256,128]{1,0:T(8,128)(2,1)S(1)}, bf16[256,128]{1,0:T(8,128)(2,1)S(1)}, u32[]{:S(2)}, u32[]{:S(2)}) collective-permute-start(bf16[256,128]{1,0:T(8,128)(2,1)S(1)} %get-tuple-element.37), channel_id=1, source_target_pairs={{0,3},{1,2},{2,1},{3,0},{4,7},{5,6},{6,5},{7,4},{8,11},{9,10},{10,... | collective-permute-start | bytes 196616 | tf_op jit(solution)/shard_map/ppermute | solution.py:412
  13.7 0.5 collective-permute-start.2
  14.3 0.7 %collective-permute-done.4.refs_1_ = bf16[3,256,128]{2,1,0:T(8,128)(2,1)S(1)} collective-permute-done((bf16[3,256,128]{2,1,0:T(8,128)(2,1)S(1)}, bf16[3,256,128]{2,1,0:T(8,128)(2,1)S(1)}, u32[]{:S(2)}, u32[]{:S(2)}) %collective-permute-start.4) | collective-permute-done | bytes 196640 | tf_op jit(solution)/shard_map/ppermute | solution.py:412
  15.0 2.0 %collective-permute-start.3 = (bf16[256,128]{1,0:T(8,128)(2,1)S(1)}, bf16[256,128]{1,0:T(8,128)(2,1)S(1)}, u32[]{:S(2)}, u32[]{:S(2)}) collective-permute-start(bf16[256,128]{1,0:T(8,128)(2,1)S(1)} %get-tuple-element.39), channel_id=1, source_target_pairs={{0,1},{1,0},{2,3},{3,2},{4,5},{5,4},{6,7},{7,6},{8,9},{9,8},{10,11... | collective-permute-start | bytes 196616 | tf_op jit(solution)/shard_map/ppermute | solution.py:412
  16.9 2.7 %collective-permute-done.5.refs_2_ = bf16[3,256,128]{2,1,0:T(8,128)(2,1)S(1)} collective-permute-done((bf16[3,256,128]{2,1,0:T(8,128)(2,1)S(1)}, bf16[3,256,128]{2,1,0:T(8,128)(2,1)S(1)}, u32[]{:S(2)}, u32[]{:S(2)}) %collective-permute-start.5) | collective-permute-done | bytes 196640 | tf_op jit(solution)/shard_map/ppermute | solution.py:412
  19.6 0.6 collective-permute-done.6.refs_3_
  20.2 0.1 combine.1
  20.3 3.3 %collective-permute-start.7 = (bf16[256,128]{1,0:T(8,128)(2,1)S(1)}, bf16[256,128]{1,0:T(8,128)(2,1)S(1)}, u32[]{:S(2)}, u32[]{:S(2)}) collective-permute-start(bf16[256,128]{1,0:T(8,128)(2,1)S(1)} %get-tuple-element.44), channel_id=1, source_target_pairs={{0,12},{1,13},{2,14},{3,15},{4,8},{5,9},{6,10},{7,11},{8,4},{9,5},... | collective-permute-start | bytes 196616 | tf_op jit(solution)/shard_map/ppermute | solution.py:418
  23.6 0.0 collective-permute-start.8
  23.6 0.0 collective-permute-done.1.refs_1_
  23.6 1.1 %collective-permute-start.9 = (bf16[256,128]{1,0:T(8,128)(2,1)S(1)}, bf16[256,128]{1,0:T(8,128)(2,1)S(1)}, u32[]{:S(2)}, u32[]{:S(2)}) collective-permute-start(bf16[256,128]{1,0:T(8,128)(2,1)S(1)} %get-tuple-element.46), channel_id=1, source_target_pairs={{0,4},{1,5},{2,6},{3,7},{4,0},{5,1},{6,2},{7,3},{8,12},{9,13},{10,... | collective-permute-start | bytes 196616 | tf_op jit(solution)/shard_map/ppermute | solution.py:418
  24.7 0.0 collective-permute-done.2.refs_2_
  24.8 0.0 collective-permute-done.3.refs_3_
  24.8 2.4 %collective-permute-done.7.refs_4_ = bf16[256,128]{1,0:T(8,128)(2,1)S(1)} collective-permute-done((bf16[256,128]{1,0:T(8,128)(2,1)S(1)}, bf16[256,128]{1,0:T(8,128)(2,1)S(1)}, u32[]{:S(2)}, u32[]{:S(2)}) %collective-permute-start.7) | collective-permute-done | bytes 65568 | tf_op jit(solution)/shard_map/ppermute | solution.py:418
  27.1 2.2 %collective-permute-done.8.refs_5_ = bf16[256,128]{1,0:T(8,128)(2,1)S(1)} collective-permute-done((bf16[256,128]{1,0:T(8,128)(2,1)S(1)}, bf16[256,128]{1,0:T(8,128)(2,1)S(1)}, u32[]{:S(2)}, u32[]{:S(2)}) %collective-permute-start.8) | collective-permute-done | bytes 65568 | tf_op jit(solution)/shard_map/ppermute | solution.py:418
  29.4 0.0 collective-permute-done.9.refs_6_
  29.4 0.0 copy-done
  29.4 0.0 copy-done.1
  29.4 0.0 copy-done.2
  29.4 0.0 copy-done.3
  29.4 0.6 %layer.1 = (bf16[128,256]{1,0:T(8,128)(2,1)S(1)}, f32[256,128]{1,0:T(8,128)S(1)}, f32[256,256]{1,0:T(8,128)S(1)}, f32[256,256]{1,0:T(8,128)S(1)}) custom-call(f32[256,128]{1,0:T(8,128)S(1)} %get-tuple-element.36.refs_0_, bf16[256,128]{1,0:T(8,128)(2,1)S(1)} %collective-permute-done.1.refs_1_, bf16[256,128]{1,0:T(8,128)(2,1)S(1)} %collective-permute-done.2.refs_2_, ...), custom_call_target="tpu_custom_call" | custom-call | tf_op jit(solution)/shard_map/layer/pallas_call | solution.py:243
  30.0 2.6 %collective-permute-start.12 = (bf16[128,256]{1,0:T(8,128)(2,1)S(1)}, bf16[128,256]{1,0:T(8,128)(2,1)S(1)}, u32[]{:S(2)}, u32[]{:S(2)}) collective-permute-start(bf16[128,256]{1,0:T(8,128)(2,1)S(1)} %get-tuple-element.53.refs_0_), channel_id=1, source_target_pairs={{0,12},{1,13},{2,14},{3,15},{4,8},{5,9},{6,10},{7,11},{8,4},{9,5},... | collective-permute-start | bytes 196616 | tf_op jit(solution)/shard_map/ppermute | solution.py:418
  32.6 0.9 %results.1 = (bf16[256,256]{1,0:T(8,128)(2,1)}, bf16[144,256]{1,0:T(8,128)(2,1)S(1)}) custom-call(f32[256,128]{1,0:T(8,128)S(1)} %get-tuple-element.47.hidden_ref, f32[256,256]{1,0:T(8,128)S(1)} %get-tuple-element.48.preact_ref, f32[256,256]{1,0:T(8,128)S(1)} %get-tuple-element.49.grad_pre_ref), custom_call_target="tpu_custom_call" | custom-call | tf_op jit(solution)/shard_map/results/pallas_call | solution.py:270
  33.5 2.4 %collective-permute-start.15 = (bf16[144,256]{1,0:T(8,128)(2,1)S(1)}, bf16[144,256]{1,0:T(8,128)(2,1)S(1)}, u32[]{:S(2)}, u32[]{:S(2)}) collective-permute-start(bf16[144,256]{1,0:T(8,128)(2,1)S(1)} %get-tuple-element.59.refs_0_), channel_id=1, source_target_pairs={{0,3},{1,2},{2,1},{3,0},{4,7},{5,6},{6,5},{7,4},{8,11},{9,10},{10,... | collective-permute-start | bytes 221192 | tf_op jit(solution)/shard_map/ppermute | solution.py:412
  35.9 0.6 collective-permute-start.14
  36.5 0.5 collective-permute-start.13
  37.0 0.0 collective-permute-start.11
  37.0 0.0 collective-permute-done.12.refs_3_
  37.0 1.9 %collective-permute-start.10 = (bf16[128,256]{1,0:T(8,128)(2,1)S(1)}, bf16[128,256]{1,0:T(8,128)(2,1)S(1)}, u32[]{:S(2)}, u32[]{:S(2)}) collective-permute-start(bf16[128,256]{1,0:T(8,128)(2,1)S(1)} %get-tuple-element.53.refs_0_), channel_id=1, source_target_pairs={{0,4},{1,5},{2,6},{3,7},{4,0},{5,1},{6,2},{7,3},{8,12},{9,13},{10,... | collective-permute-start | bytes 196616 | tf_op jit(solution)/shard_map/ppermute | solution.py:418
  38.9 3.3 %collective-permute-done.11.refs_2_ = bf16[128,256]{1,0:T(8,128)(2,1)S(1)} collective-permute-done((bf16[128,256]{1,0:T(8,128)(2,1)S(1)}, bf16[128,256]{1,0:T(8,128)(2,1)S(1)}, u32[]{:S(2)}, u32[]{:S(2)}) %collective-permute-start.11) | collective-permute-done | bytes 65568 | tf_op jit(solution)/shard_map/ppermute | solution.py:418
  42.2 0.0 collective-permute-done.10.refs_1_
  42.2 0.0 collective-permute-done.15.refs_3_
  42.2 0.0 collective-permute-done.14.refs_2_
  42.2 0.0 collective-permute-done.13.refs_1_
  42.2 2.4 %collective-permute-start.18 = (bf16[4,128,256]{2,1,0:T(8,128)(2,1)S(1)}, bf16[4,128,256]{2,1,0:T(8,128)(2,1)S(1)}, u32[]{:S(2)}, u32[]{:S(2)}) collective-permute-start(bf16[4,128,256]{2,1,0:T(8,128)(2,1)S(1)} %stack_line.1.refs_0_), channel_id=1, source_target_pairs={{0,3},{1,2},{2,1},{3,0},{4,7},{5,6},{6,5},{7,4},{8,11},{9,10},{10,... | collective-permute-start | bytes 786440 | tf_op jit(solution)/shard_map/ppermute | solution.py:412
  44.7 0.6 collective-permute-start.17
  45.3 0.5 collective-permute-start.16
  45.8 2.1 %collective-permute-start.21 = (bf16[144,256]{1,0:T(8,128)(2,1)S(1)}, bf16[144,256]{1,0:T(8,128)(2,1)S(1)}, u32[]{:S(2)}, u32[]{:S(2)}) collective-permute-start(bf16[144,256]{1,0:T(8,128)(2,1)S(1)} %sum_terms.1.refs_4_), channel_id=1, source_target_pairs={{0,12},{1,13},{2,14},{3,15},{4,8},{5,9},{6,10},{7,11},{8,4},{9,5},... | collective-permute-start | bytes 221192 | tf_op jit(solution)/shard_map/ppermute | solution.py:418
  47.9 0.4 collective-permute-start.20
  48.3 3.6 %collective-permute-done.18.refs_1_ = bf16[4,128,256]{2,1,0:T(8,128)(2,1)S(1)} collective-permute-done((bf16[4,128,256]{2,1,0:T(8,128)(2,1)S(1)}, bf16[4,128,256]{2,1,0:T(8,128)(2,1)S(1)}, u32[]{:S(2)}, u32[]{:S(2)}) %collective-permute-start.18) | collective-permute-done | bytes 262176 | tf_op jit(solution)/shard_map/ppermute | solution.py:412
  52.0 1.2 %collective-permute-start.19 = (bf16[144,256]{1,0:T(8,128)(2,1)S(1)}, bf16[144,256]{1,0:T(8,128)(2,1)S(1)}, u32[]{:S(2)}, u32[]{:S(2)}) collective-permute-start(bf16[144,256]{1,0:T(8,128)(2,1)S(1)} %sum_terms.1.refs_4_), channel_id=1, source_target_pairs={{0,4},{1,5},{2,6},{3,7},{4,0},{5,1},{6,2},{7,3},{8,12},{9,13},{10,... | collective-permute-start | bytes 221192 | tf_op jit(solution)/shard_map/ppermute | solution.py:418
  53.2 0.4 backward_product.2
  53.7 0.0 collective-permute-done.21.refs_7_
  53.7 0.3 collective-permute-done.20.refs_6_
  54.0 2.4 %collective-permute-done.19.refs_5_ = bf16[144,256]{1,0:T(8,128)(2,1)S(1)} collective-permute-done((bf16[144,256]{1,0:T(8,128)(2,1)S(1)}, bf16[144,256]{1,0:T(8,128)(2,1)S(1)}, u32[]{:S(2)}, u32[]{:S(2)}) %collective-permute-start.19) | collective-permute-done | bytes 73760 | tf_op jit(solution)/shard_map/ppermute | solution.py:418
  56.3 0.0 collective-permute-done.17.refs_1_
  56.3 0.0 collective-permute-done.16.refs_0_
  56.3 0.4 backward_product.3
  56.8 0.1 collective-permute-start.22
  56.9 1.3 %collective-permute-done.22.refs_0_ = bf16[272,256]{1,0:T(8,128)(2,1)S(1)} collective-permute-done((bf16[272,256]{1,0:T(8,128)(2,1)S(1)}, bf16[272,256]{1,0:T(8,128)(2,1)S(1)}, u32[]{:S(2)}, u32[]{:S(2)}) %collective-permute-start.22) | collective-permute-done | bytes 139296 | tf_op jit(solution)/shard_map/ppermute | solution.py:406
  58.2 0.7 %finish.1 = (bf16[256,128]{1,0:T(8,128)(2,1)}, f32[128,256]{1,0:T(8,128)}, f32[1,256]{1,0:T(1,128)}) custom-call(s32[1,256]{1,0:T(1,128)S(1)} %bitcast.11, f32[128,256]{1,0:T(8,128)S(1)} %get-tuple-element.63.own_ref, bf16[272,256]{1,0:T(8,128)(2,1)S(1)} %get-tuple-element.64.sent_ref, bf16[272,256]{1,0:T(8,128)(2,1)S(1)} %collective-permute-done.22.refs_0_), custom_call_target="tpu_custom_call" | custom-call | tf_op jit(solution)/shard_map/finish/pallas_call | solution.py:374
  (2 shorter events, 0.1 us)
Async XLA Ops:
  1.6 3.7 %collective-permute-start = (bf16[256,128]{1,0:T(8,128)(2,1)S(1)}, bf16[256,128]{1,0:T(8,128)(2,1)S(1)}, u32[]{:S(2)}, u32[]{:S(2)}) collective-permute-start(bf16[256,128]{1,0:T(8,128)(2,1)S(1)} %scale_features.1.refs_0_), channel_id=1, source_target_pairs={{0,16},{16,0},{1,17},{17,1},{2,18},{18,2},{3,19},{19,3},{4,20},{20... | collective-permute-start | bytes 196616 | tf_op jit(solution)/shard_map/ppermute | solution.py:406
  5.3 24.1 %copy-start = (bf16[256,256]{1,0:T(8,128)(2,1)S(1)}, bf16[256,256]{1,0:T(8,128)(2,1)}, u32[]{:S(2)}) copy-start(bf16[256,256]{1,0:T(8,128)(2,1)} %refs_10_.1) | copy-start | bytes 393220
  5.3 24.1 %copy-start.1 = (bf16[128,256]{1,0:T(8,128)(2,1)S(1)}, bf16[128,256]{1,0:T(8,128)(2,1)}, u32[]{:S(2)}) copy-start(bf16[128,256]{1,0:T(8,128)(2,1)} %refs_8_.1) | copy-start | bytes 196612
  5.3 24.1 %copy-start.2 = (s32[256]{0:T(256)S(1)}, s32[256]{0:T(256)}, u32[]{:S(2)}) copy-start(s32[256]{0:T(256)} %param.12) | copy-start | bytes 3076
  5.3 24.1 %copy-start.3 = (f32[256]{0:T(256)S(1)}, f32[256]{0:T(256)}, u32[]{:S(2)}) copy-start(f32[256]{0:T(256)} %param.10) | copy-start | bytes 3076
  5.8 9.2 %collective-permute-start.4 = (bf16[3,256,128]{2,1,0:T(8,128)(2,1)S(1)}, bf16[3,256,128]{2,1,0:T(8,128)(2,1)S(1)}, u32[]{:S(2)}, u32[]{:S(2)}) collective-permute-start(bf16[3,256,128]{2,1,0:T(8,128)(2,1)S(1)} %get-tuple-element.41), channel_id=1, source_target_pairs={{0,3},{1,2},{2,1},{3,0},{4,7},{5,6},{6,5},{7,4},{8,11},{9,10},{10,... | collective-permute-start | bytes 589832 | tf_op jit(solution)/shard_map/ppermute | solution.py:412
  10.2 9.4 %collective-permute-start.5 = (bf16[3,256,128]{2,1,0:T(8,128)(2,1)S(1)}, bf16[3,256,128]{2,1,0:T(8,128)(2,1)S(1)}, u32[]{:S(2)}, u32[]{:S(2)}) collective-permute-start(bf16[3,256,128]{2,1,0:T(8,128)(2,1)S(1)} %get-tuple-element.42), channel_id=1, source_target_pairs={{0,2},{1,3},{2,0},{3,1},{4,6},{5,7},{6,4},{7,5},{8,10},{9,11},{10,... | collective-permute-start | bytes 589832 | tf_op jit(solution)/shard_map/ppermute | solution.py:412
  10.8 9.4 %collective-permute-start.6 = (bf16[3,256,128]{2,1,0:T(8,128)(2,1)S(1)}, bf16[3,256,128]{2,1,0:T(8,128)(2,1)S(1)}, u32[]{:S(2)}, u32[]{:S(2)}) collective-permute-start(bf16[3,256,128]{2,1,0:T(8,128)(2,1)S(1)} %get-tuple-element.43), channel_id=1, source_target_pairs={{0,1},{1,0},{2,3},{3,2},{4,5},{5,4},{6,7},{7,6},{8,9},{9,8},{10,11... | collective-permute-start | bytes 589832 | tf_op jit(solution)/shard_map/ppermute | solution.py:412
  11.3 12.3 %collective-permute-start.1 = (bf16[256,128]{1,0:T(8,128)(2,1)S(1)}, bf16[256,128]{1,0:T(8,128)(2,1)S(1)}, u32[]{:S(2)}, u32[]{:S(2)}) collective-permute-start(bf16[256,128]{1,0:T(8,128)(2,1)S(1)} %get-tuple-element.37), channel_id=1, source_target_pairs={{0,3},{1,2},{2,1},{3,0},{4,7},{5,6},{6,5},{7,4},{8,11},{9,10},{10,... | collective-permute-start | bytes 196616 | tf_op jit(solution)/shard_map/ppermute | solution.py:412
  13.7 11.0 %collective-permute-start.2 = (bf16[256,128]{1,0:T(8,128)(2,1)S(1)}, bf16[256,128]{1,0:T(8,128)(2,1)S(1)}, u32[]{:S(2)}, u32[]{:S(2)}) collective-permute-start(bf16[256,128]{1,0:T(8,128)(2,1)S(1)} %get-tuple-element.38), channel_id=1, source_target_pairs={{0,2},{1,3},{2,0},{3,1},{4,6},{5,7},{6,4},{7,5},{8,10},{9,11},{10,... | collective-permute-start | bytes 196616 | tf_op jit(solution)/shard_map/ppermute | solution.py:412
  15.0 9.8 %collective-permute-start.3 = (bf16[256,128]{1,0:T(8,128)(2,1)S(1)}, bf16[256,128]{1,0:T(8,128)(2,1)S(1)}, u32[]{:S(2)}, u32[]{:S(2)}) collective-permute-start(bf16[256,128]{1,0:T(8,128)(2,1)S(1)} %get-tuple-element.39), channel_id=1, source_target_pairs={{0,1},{1,0},{2,3},{3,2},{4,5},{5,4},{6,7},{7,6},{8,9},{9,8},{10,11... | collective-permute-start | bytes 196616 | tf_op jit(solution)/shard_map/ppermute | solution.py:412
  20.3 6.8 %collective-permute-start.7 = (bf16[256,128]{1,0:T(8,128)(2,1)S(1)}, bf16[256,128]{1,0:T(8,128)(2,1)S(1)}, u32[]{:S(2)}, u32[]{:S(2)}) collective-permute-start(bf16[256,128]{1,0:T(8,128)(2,1)S(1)} %get-tuple-element.44), channel_id=1, source_target_pairs={{0,12},{1,13},{2,14},{3,15},{4,8},{5,9},{6,10},{7,11},{8,4},{9,5},... | collective-permute-start | bytes 196616 | tf_op jit(solution)/shard_map/ppermute | solution.py:418
  23.6 5.7 %collective-permute-start.8 = (bf16[256,128]{1,0:T(8,128)(2,1)S(1)}, bf16[256,128]{1,0:T(8,128)(2,1)S(1)}, u32[]{:S(2)}, u32[]{:S(2)}) collective-permute-start(bf16[256,128]{1,0:T(8,128)(2,1)S(1)} %get-tuple-element.45), channel_id=1, source_target_pairs={{0,8},{1,9},{2,10},{3,11},{4,12},{5,13},{6,14},{7,15},{8,0},{9,1},... | collective-permute-start | bytes 196616 | tf_op jit(solution)/shard_map/ppermute | solution.py:418
  23.6 5.7 %collective-permute-start.9 = (bf16[256,128]{1,0:T(8,128)(2,1)S(1)}, bf16[256,128]{1,0:T(8,128)(2,1)S(1)}, u32[]{:S(2)}, u32[]{:S(2)}) collective-permute-start(bf16[256,128]{1,0:T(8,128)(2,1)S(1)} %get-tuple-element.46), channel_id=1, source_target_pairs={{0,4},{1,5},{2,6},{3,7},{4,0},{5,1},{6,2},{7,3},{8,12},{9,13},{10,... | collective-permute-start | bytes 196616 | tf_op jit(solution)/shard_map/ppermute | solution.py:418
  30.0 7.0 %collective-permute-start.12 = (bf16[128,256]{1,0:T(8,128)(2,1)S(1)}, bf16[128,256]{1,0:T(8,128)(2,1)S(1)}, u32[]{:S(2)}, u32[]{:S(2)}) collective-permute-start(bf16[128,256]{1,0:T(8,128)(2,1)S(1)} %get-tuple-element.53.refs_0_), channel_id=1, source_target_pairs={{0,12},{1,13},{2,14},{3,15},{4,8},{5,9},{6,10},{7,11},{8,4},{9,5},... | collective-permute-start | bytes 196616 | tf_op jit(solution)/shard_map/ppermute | solution.py:418
  33.5 8.7 %collective-permute-start.15 = (bf16[144,256]{1,0:T(8,128)(2,1)S(1)}, bf16[144,256]{1,0:T(8,128)(2,1)S(1)}, u32[]{:S(2)}, u32[]{:S(2)}) collective-permute-start(bf16[144,256]{1,0:T(8,128)(2,1)S(1)} %get-tuple-element.59.refs_0_), channel_id=1, source_target_pairs={{0,3},{1,2},{2,1},{3,0},{4,7},{5,6},{6,5},{7,4},{8,11},{9,10},{10,... | collective-permute-start | bytes 221192 | tf_op jit(solution)/shard_map/ppermute | solution.py:412
  35.9 6.3 %collective-permute-start.14 = (bf16[144,256]{1,0:T(8,128)(2,1)S(1)}, bf16[144,256]{1,0:T(8,128)(2,1)S(1)}, u32[]{:S(2)}, u32[]{:S(2)}) collective-permute-start(bf16[144,256]{1,0:T(8,128)(2,1)S(1)} %get-tuple-element.59.refs_0_), channel_id=1, source_target_pairs={{0,2},{1,3},{2,0},{3,1},{4,6},{5,7},{6,4},{7,5},{8,10},{9,11},{10,... | collective-permute-start | bytes 221192 | tf_op jit(solution)/shard_map/ppermute | solution.py:412
  36.5 5.7 %collective-permute-start.13 = (bf16[144,256]{1,0:T(8,128)(2,1)S(1)}, bf16[144,256]{1,0:T(8,128)(2,1)S(1)}, u32[]{:S(2)}, u32[]{:S(2)}) collective-permute-start(bf16[144,256]{1,0:T(8,128)(2,1)S(1)} %get-tuple-element.59.refs_0_), channel_id=1, source_target_pairs={{0,1},{1,0},{2,3},{3,2},{4,5},{5,4},{6,7},{7,6},{8,9},{9,8},{10,11... | collective-permute-start | bytes 221192 | tf_op jit(solution)/shard_map/ppermute | solution.py:412
  37.0 5.2 %collective-permute-start.11 = (bf16[128,256]{1,0:T(8,128)(2,1)S(1)}, bf16[128,256]{1,0:T(8,128)(2,1)S(1)}, u32[]{:S(2)}, u32[]{:S(2)}) collective-permute-start(bf16[128,256]{1,0:T(8,128)(2,1)S(1)} %get-tuple-element.53.refs_0_), channel_id=1, source_target_pairs={{0,8},{1,9},{2,10},{3,11},{4,12},{5,13},{6,14},{7,15},{8,0},{9,1},... | collective-permute-start | bytes 196616 | tf_op jit(solution)/shard_map/ppermute | solution.py:418
  37.0 5.2 %collective-permute-start.10 = (bf16[128,256]{1,0:T(8,128)(2,1)S(1)}, bf16[128,256]{1,0:T(8,128)(2,1)S(1)}, u32[]{:S(2)}, u32[]{:S(2)}) collective-permute-start(bf16[128,256]{1,0:T(8,128)(2,1)S(1)} %get-tuple-element.53.refs_0_), channel_id=1, source_target_pairs={{0,4},{1,5},{2,6},{3,7},{4,0},{5,1},{6,2},{7,3},{8,12},{9,13},{10,... | collective-permute-start | bytes 196616 | tf_op jit(solution)/shard_map/ppermute | solution.py:418
  42.2 9.7 %collective-permute-start.18 = (bf16[4,128,256]{2,1,0:T(8,128)(2,1)S(1)}, bf16[4,128,256]{2,1,0:T(8,128)(2,1)S(1)}, u32[]{:S(2)}, u32[]{:S(2)}) collective-permute-start(bf16[4,128,256]{2,1,0:T(8,128)(2,1)S(1)} %stack_line.1.refs_0_), channel_id=1, source_target_pairs={{0,3},{1,2},{2,1},{3,0},{4,7},{5,6},{6,5},{7,4},{8,11},{9,10},{10,... | collective-permute-start | bytes 786440 | tf_op jit(solution)/shard_map/ppermute | solution.py:412
  44.7 11.6 %collective-permute-start.17 = (bf16[4,128,256]{2,1,0:T(8,128)(2,1)S(1)}, bf16[4,128,256]{2,1,0:T(8,128)(2,1)S(1)}, u32[]{:S(2)}, u32[]{:S(2)}) collective-permute-start(bf16[4,128,256]{2,1,0:T(8,128)(2,1)S(1)} %stack_line.1.refs_0_), channel_id=1, source_target_pairs={{0,1},{1,0},{2,3},{3,2},{4,5},{5,4},{6,7},{7,6},{8,9},{9,8},{10,11... | collective-permute-start | bytes 786440 | tf_op jit(solution)/shard_map/ppermute | solution.py:412
  45.3 11.1 %collective-permute-start.16 = (bf16[4,128,256]{2,1,0:T(8,128)(2,1)S(1)}, bf16[4,128,256]{2,1,0:T(8,128)(2,1)S(1)}, u32[]{:S(2)}, u32[]{:S(2)}) collective-permute-start(bf16[4,128,256]{2,1,0:T(8,128)(2,1)S(1)} %stack_line.1.refs_0_), channel_id=1, source_target_pairs={{0,2},{1,3},{2,0},{3,1},{4,6},{5,7},{6,4},{7,5},{8,10},{9,11},{10,... | collective-permute-start | bytes 786440 | tf_op jit(solution)/shard_map/ppermute | solution.py:412
  45.8 7.8 %collective-permute-start.21 = (bf16[144,256]{1,0:T(8,128)(2,1)S(1)}, bf16[144,256]{1,0:T(8,128)(2,1)S(1)}, u32[]{:S(2)}, u32[]{:S(2)}) collective-permute-start(bf16[144,256]{1,0:T(8,128)(2,1)S(1)} %sum_terms.1.refs_4_), channel_id=1, source_target_pairs={{0,12},{1,13},{2,14},{3,15},{4,8},{5,9},{6,10},{7,11},{8,4},{9,5},... | collective-permute-start | bytes 221192 | tf_op jit(solution)/shard_map/ppermute | solution.py:418
  47.9 6.0 %collective-permute-start.20 = (bf16[144,256]{1,0:T(8,128)(2,1)S(1)}, bf16[144,256]{1,0:T(8,128)(2,1)S(1)}, u32[]{:S(2)}, u32[]{:S(2)}) collective-permute-start(bf16[144,256]{1,0:T(8,128)(2,1)S(1)} %sum_terms.1.refs_4_), channel_id=1, source_target_pairs={{0,8},{1,9},{2,10},{3,11},{4,12},{5,13},{6,14},{7,15},{8,0},{9,1},... | collective-permute-start | bytes 221192 | tf_op jit(solution)/shard_map/ppermute | solution.py:418
  52.0 4.4 %collective-permute-start.19 = (bf16[144,256]{1,0:T(8,128)(2,1)S(1)}, bf16[144,256]{1,0:T(8,128)(2,1)S(1)}, u32[]{:S(2)}, u32[]{:S(2)}) collective-permute-start(bf16[144,256]{1,0:T(8,128)(2,1)S(1)} %sum_terms.1.refs_4_), channel_id=1, source_target_pairs={{0,4},{1,5},{2,6},{3,7},{4,0},{5,1},{6,2},{7,3},{8,12},{9,13},{10,... | collective-permute-start | bytes 221192 | tf_op jit(solution)/shard_map/ppermute | solution.py:418
  56.8 1.4 %collective-permute-start.22 = (bf16[272,256]{1,0:T(8,128)(2,1)S(1)}, bf16[272,256]{1,0:T(8,128)(2,1)S(1)}, u32[]{:S(2)}, u32[]{:S(2)}) collective-permute-start(bf16[272,256]{1,0:T(8,128)(2,1)S(1)} %get-tuple-element.64.sent_ref), channel_id=1, source_target_pairs={{0,16},{16,0},{1,17},{17,1},{2,18},{18,2},{3,19},{19,3},{4,20},{20... | collective-permute-start | bytes 417800 | tf_op jit(solution)/shard_map/ppermute | solution.py:406

commit v2 on v1

--- a/solution.py
+++ b/solution.py
@@ -45,34 +45,6 @@
 def scale_columns(degrees_row, columns):
     row = lax.rsqrt(degrees_row.astype(F32))
     return row, jnp.transpose(jnp.broadcast_to(row, (columns, row.shape[1])))
-
-
-def scale_kernel(degrees_hbm, features_hbm, out_ref, degrees_ref, features_ref, sems):
-    copies = [
-        pltpu.make_async_copy(degrees_hbm, degrees_ref, sems.at[0]),
-        pltpu.make_async_copy(features_hbm, features_ref, sems.at[1]),
-    ]
-    for copy in copies:
-        copy.start()
-    for copy in copies:
-        copy.wait()
-    _, scale = scale_columns(degrees_ref[...], features_ref.shape[1])
-    out_ref[...] = (scale * features_ref[...].astype(F32)).astype(BF16)
-
-
-def scale_features(degrees_row, features):
-    return pl.pallas_call(
-        scale_kernel,
-        out_shape=jax.ShapeDtypeStruct(features.shape, BF16),
-        in_specs=[pl.BlockSpec(memory_space=pltpu.HBM)] * 2,
-        scratch_shapes=[
-            pltpu.VMEM(degrees_row.shape, degrees_row.dtype),
-            pltpu.VMEM(features.shape, features.dtype),
-            pltpu.SemaphoreType.DMA((2,)),
-        ],
-        compiler_params=params(),
-        name="scale_features",
-    )(in_hbm(degrees_row), in_hbm(features))
 
 
 def densify_kernel(
@@ -163,41 +135,54 @@
     return pl.ds(pl.multiple_of(index * nodes, nodes), nodes)
 
 
-def forward_kernel(steps, pieces, dense_ref, *refs):
-    scaled, outs = refs[:pieces], refs[pieces:]
+def forward_kernel(wanted, pieces, scaling, dense_ref, *refs):
+    inputs = refs[: 2 * pieces if scaling else pieces]
+    outs = refs[len(inputs) :]
     high, low, nodes, _ = dense_ref.shape
     row, line, plane = spot(low)
-    for step, onward_ref, here_ref in zip(steps, outs[::2], outs[1::2]):
-        column = other(plane, step, low)
-        for hop in (*far_first(high), 0):
-            chunk = other(line, hop, high)
-            total = None
-            for piece in range(pieces):
-                columns = piece_columns(source(row, piece, pieces), nodes)
-                term = dot(dense_ref[chunk, column, :, columns], scaled[piece][...])
-                total = term if total is None else total + term
-            if hop:
-                onward_ref[hop - 1] = total.astype(onward_ref.dtype)
-            else:
-                here_ref[...] = total.astype(here_ref.dtype)
-
-
-def forward(dense, scaled, steps):
+    if scaling:
+        scaled = outs[len(wanted) :]
+        for degrees_ref, features_ref, out_ref in zip(inputs[:pieces], inputs[pieces:], scaled):
+            _, scale = scale_columns(degrees_ref[...], features_ref.shape[1])
+            out_ref[...] = (scale * features_ref[...].astype(F32)).astype(BF16)
+    else:
+        scaled = inputs
+
+    def product(step, hop):
+        column, chunk = other(plane, step, low), other(line, hop, high)
+        total = None
+        for piece in range(pieces):
+            columns = piece_columns(source(row, piece, pieces), nodes)
+            term = dot(dense_ref[chunk, column, :, columns], scaled[piece][...])
+            total = term if total is None else total + term
+        return total
+
+    for (step, onward), out_ref in zip(wanted, outs):
+        if onward:
+            for hop in far_first(high):
+                out_ref[hop - 1] = product(step, hop).astype(out_ref.dtype)
+        else:
+            out_ref[...] = product(step, 0).astype(out_ref.dtype)
+
+
+def forward(dense, inputs, wanted, scaling=False):
     high, _, nodes, _ = dense.shape
-    pieces = len(scaled)
-    width = scaled[0].shape[1]
-    products = pl.pallas_call(
-        functools.partial(forward_kernel, steps, pieces),
-        out_shape=[
-            jax.ShapeDtypeStruct(shape, BF16 if step else F32)
-            for step in steps
-            for shape in ((high - 1, nodes, width), (nodes, width))
-        ],
-        in_specs=[pl.BlockSpec(memory_space=pltpu.VMEM)] * (1 + pieces),
+    pieces = len(inputs) // 2 if scaling else len(inputs)
+    width = inputs[-1].shape[1]
+
+    def shape_of(step, onward):
+        shape = (high - 1, nodes, width) if onward else (nodes, width)
+        return jax.ShapeDtypeStruct(shape, BF16 if step else F32)
+
+    outs = pl.pallas_call(
+        functools.partial(forward_kernel, wanted, pieces, scaling),
+        out_shape=[shape_of(*item) for item in wanted]
+        + [jax.ShapeDtypeStruct((nodes, width), BF16)] * (pieces if scaling else 0),
+        in_specs=[pl.BlockSpec(memory_space=pltpu.VMEM)] * (1 + len(inputs)),
         compiler_params=params(),
         name="forward_product",
-    )(dense, *scaled)
-    return dict(zip(steps, zip(products[::2], products[1::2])))
+    )(dense, *inputs)
+    return dict(zip(wanted, outs)), outs[len(wanted) :]
 
 
 def combine_kernel(count, *refs):
@@ -253,9 +238,21 @@
     )(*shares, degrees_row, weight, bias_row, cotangent)
 
 
-def results_kernel(hidden_ref, preact_ref, grad_pre_ref, activations_ref, terms_ref):
+def activations_kernel(preact_ref, out_ref):
     preact = preact_ref[...]
-    activations_ref[...] = (preact / (1.0 + jnp.exp(-preact))).astype(BF16)
+    out_ref[...] = (preact / (1.0 + jnp.exp(-preact))).astype(BF16)
+
+
+def activations_of(preact):
+    return pl.pallas_call(
+        activations_kernel,
+        out_shape=jax.ShapeDtypeStruct(preact.shape, BF16),
+        compiler_params=params(),
+        name="activations",
+    )(preact)
+
+
+def terms_kernel(hidden_ref, grad_pre_ref, terms_ref):
     grad_pre = grad_pre_ref[...]
     grads = split_two(grad_pre)
     upper, lower = split_two(jnp.transpose(hidden_ref[...]))
@@ -266,16 +263,13 @@
     terms_ref[depth:, :] = jnp.broadcast_to(bias_term, (16, bias_term.shape[1])).astype(BF16)
 
 
-def results(hidden, preact, grad_pre):
-    return pl.pallas_call(
-        results_kernel,
-        out_shape=[
-            jax.ShapeDtypeStruct(preact.shape, BF16),
-            jax.ShapeDtypeStruct((hidden.shape[1] + 16, preact.shape[1]), BF16),
-        ],
-        compiler_params=params(),
-        name="results",
-    )(hidden, preact, grad_pre)
+def terms_of(hidden, grad_pre):
+    return pl.pallas_call(
+        terms_kernel,
+        out_shape=jax.ShapeDtypeStruct((hidden.shape[1] + 16, grad_pre.shape[1]), BF16),
+        compiler_params=params(),
+        name="weight_terms",
+    )(hidden, grad_pre)
 
 
 def tree_sum(values):
@@ -417,21 +411,29 @@
         ]
         return lax.ppermute(values, "col", pairs)
 
-    own = scale_features(degrees_row, features)
-    scaled = [own] + [over_row(own, step) for step in range(1, rows)]
+    steps = range(1, rows)
+    degrees_all = [degrees] + [over_row(degrees, step) for step in steps]
+    features_all = [features] + [over_row(features, step) for step in steps]
     dense = densify(
         tile_positions, tile_counts, adjacency_tiles[0, 0], row_slots, col_slots
     ).reshape(high, low, nodes, col_slots * BLOCK)
 
-    products = forward(dense, scaled, (low - 1,)) | forward(dense, scaled, tuple(range(low - 1))[::-1])
-    onward = [products[0][0]] + [over_plane(products[step][0], step) for step in far_first(low)]
-    here = [products[0][1]] + [over_plane(products[step][1], step) for step in far_first(low)]
+    inputs = [values[None, :] for values in degrees_all] + features_all
+    products, scaled = forward(dense, inputs, ((low - 1, True),), scaling=True)
+    far_ones = tuple((step, True) for step in far_first(low - 1))
+    rest = ((0, True),) + tuple((step, False) for step in (*far_first(low), 0))
+    for wanted in (far_ones, rest):
+        if wanted:
+            products |= forward(dense, scaled, wanted)[0]
+    onward = [products[0, True]] + [over_plane(products[step, True], step) for step in far_first(low)]
+    here = [products[0, False]] + [over_plane(products[step, False], step) for step in far_first(low)]
     chunks = combine(onward)
     shares = [over_line(chunks[hop - 1], hop) for hop in far_first(high)]
-    outgoing, *kept = layer(here + shares, degrees_row, weight, bias_vector[None, :], cotangent)
+    outgoing, hidden, preact, grad_pre = layer(here + shares, degrees_row, weight, bias_vector[None, :], cotangent)
 
     line = {0: outgoing} | {step: over_line(outgoing, step) for step in far_first(high)}
-    activations, terms = results(*kept)
+    terms = terms_of(hidden, grad_pre)
+    activations = activations_of(preact)
     parts = {0: terms} | {step: over_plane(terms, step) for step in far_first(low)}
     line, parts = lax.optimization_barrier((line, parts))
     stacked = stack_line(low, [line[step] for step in range(high)])

time: 59 us -> 57.9 us (0.981)
  waiting for transfers between devices: 19.5 us -> 18.1 us
    ppermute x12, waiting for transfers between devices: 7.6 us -> 6.41 us  [over_plane(): return lax.ppermute(values, 'col', pairs)]
    ppermute x12, starting transfers between devices: 16.5 us -> 17.3 us  [over_plane(): return lax.ppermute(values, 'col', pairs)]
    ppermute x2 -> x3, waiting for transfers between devices: 1.35 us -> 0.62 us  [over_row(): return lax.ppermute(values, 'row', pairs)]
    pallas_call x4 -> x5, Pallas kernels: 3.3 us -> 2.68 us  [the longest x3 1.69 us: forward(): pl.pallas_call(functools.partial(forward_kernel, wanted, pieces, scaling)...]
  transfers between devices with their start and end apart: 23 -> 24, of which waited for: 10 -> 10; matrix products, arithmetic and copies ran while one was open for 0% -> 0% of each run, Pallas kernels for 8% -> 9%
where the time goes in v2:
time: 57.9 us; the launch traced here: 57.6 us
  starting transfers between devices  30.3 us (52%)
  waiting for transfers between devices  18.1 us (31%)
  Pallas kernels  7.69 us (13%)
  between operations  1.46 us (3%)
    ppermute x12, starting transfers between devices, over_plane(): return lax.ppermute(values, 'col', pairs)  17.3 us
    ppermute x9, starting transfers between devices, over_line(): return lax.ppermute(values, 'col', pairs)  12.4 us
    ppermute x9, waiting for transfers between devices, over_line(): return lax.ppermute(values, 'col', pairs)  11.1 us
    ppermute x12, waiting for transfers between devices, over_plane(): return lax.ppermute(values, 'col', pairs)  6.41 us
    pallas_call x1, Pallas kernels, densify(): pl.pallas_call(functools.partial(densify_kernel, col_slots), out_shape=ja...  2.6 us
    pallas_call x3, Pallas kernels, forward(): pl.pallas_call(functools.partial(forward_kernel, wanted, pieces, scaling)...  1.69 us
  transfers between devices with their start and end apart: 24, of which 10 were waited for; matrix products, arithmetic and copies ran while one was open for 0% of the time, Pallas kernels for 9%

profile of v2, /device:TPU:0, one launch (start us, length us, event | category | flops | bytes accessed | tf_op | source)
XLA Modules:
  0.0 57.6 jit_solution(8993402975807534635)
XLA Ops:
  0.6 0.5 collective-permute-start.1
  1.1 0.1 collective-permute-start
  1.9 0.0 copy-start.1
  1.9 0.0 copy-start.3
  1.9 2.6 %densify.1 = bf16[32,128,512]{2,1,0:T(8,128)(2,1)S(1)} custom-call(s32[1,1,128]{2,1,0:T(1,128)} %positions_hbm.1, s32[1,1]{1,0:T(1,128)S(6)} %copy.12.counts_ref, bf16[128,128,128]{2,1,0:T(8,128)(2,1)} %bitcast.16), custom_call_target="tpu_custom_call" | custom-call | tf_op jit(solution)/shard_map/densify/pallas_call | solution.py:107
  4.5 0.0 collective-permute-done
  4.5 0.0 collective-permute-done.1.refs_3_
  4.5 0.0 copy-done.1
  4.5 0.0 copy-done.3
  4.5 0.5 forward_product.3
  5.1 3.9 %collective-permute-start.5 = (bf16[3,256,128]{2,1,0:T(8,128)(2,1)S(1)}, bf16[3,256,128]{2,1,0:T(8,128)(2,1)S(1)}, u32[]{:S(2)}, u32[]{:S(2)}) collective-permute-start(bf16[3,256,128]{2,1,0:T(8,128)(2,1)S(1)} %get-tuple-element.43), channel_id=1, source_target_pairs={{0,3},{1,2},{2,1},{3,0},{4,7},{5,6},{6,5},{7,4},{8,11},{9,10},{10,... | collective-permute-start | bytes 589832 | tf_op jit(solution)/shard_map/ppermute | solution.py:406
  8.9 0.6 forward_product.5
  9.5 0.6 %collective-permute-start.6 = (bf16[3,256,128]{2,1,0:T(8,128)(2,1)S(1)}, bf16[3,256,128]{2,1,0:T(8,128)(2,1)S(1)}, u32[]{:S(2)}, u32[]{:S(2)}) collective-permute-start(bf16[3,256,128]{2,1,0:T(8,128)(2,1)S(1)} %get-tuple-element.44), channel_id=1, source_target_pairs={{0,2},{1,3},{2,0},{3,1},{4,6},{5,7},{6,4},{7,5},{8,10},{9,11},{10,... | collective-permute-start | bytes 589832 | tf_op jit(solution)/shard_map/ppermute | solution.py:406
  10.2 0.0 collective-permute-start.7
  10.2 0.6 %forward_product.4 = (f32[3,256,128]{2,1,0:T(8,128)S(1)}, bf16[256,128]{1,0:T(8,128)(2,1)S(1)}, bf16[256,128]{1,0:T(8,128)(2,1)S(1)}, bf16[256,128]{1,0:T(8,128)(2,1)S(1)}, f32[256,128]{1,0:T(8,128)S(1)}) custom-call(bf16[4,4,256,512]{3,2,1,0:T(8,128)(2,1)S(1)} %bitcast.8, bf16[256,128]{1,0:T(8,128)(2,1)S(1)} %get-tuple-element.36.refs_0_, ...), custom_call_target="tpu_custom_call" | custom-call | tf_op jit(solution)/shard_map/forward_product/pallas_call | solution.py:177
  10.8 2.9 %collective-permute-start.2 = (bf16[256,128]{1,0:T(8,128)(2,1)S(1)}, bf16[256,128]{1,0:T(8,128)(2,1)S(1)}, u32[]{:S(2)}, u32[]{:S(2)}) collective-permute-start(bf16[256,128]{1,0:T(8,128)(2,1)S(1)} %get-tuple-element.39), channel_id=1, source_target_pairs={{0,3},{1,2},{2,1},{3,0},{4,7},{5,6},{6,5},{7,4},{8,11},{9,10},{10,... | collective-permute-start | bytes 196616 | tf_op jit(solution)/shard_map/ppermute | solution.py:406
  13.8 0.6 collective-permute-start.3
  14.3 0.3 collective-permute-done.5.refs_1_
  14.6 2.1 %collective-permute-start.4 = (bf16[256,128]{1,0:T(8,128)(2,1)S(1)}, bf16[256,128]{1,0:T(8,128)(2,1)S(1)}, u32[]{:S(2)}, u32[]{:S(2)}) collective-permute-start(bf16[256,128]{1,0:T(8,128)(2,1)S(1)} %get-tuple-element.41), channel_id=1, source_target_pairs={{0,1},{1,0},{2,3},{3,2},{4,5},{5,4},{6,7},{7,6},{8,9},{9,8},{10,11... | collective-permute-start | bytes 196616 | tf_op jit(solution)/shard_map/ppermute | solution.py:406
  16.8 2.2 %collective-permute-done.6.refs_2_ = bf16[3,256,128]{2,1,0:T(8,128)(2,1)S(1)} collective-permute-done((bf16[3,256,128]{2,1,0:T(8,128)(2,1)S(1)}, bf16[3,256,128]{2,1,0:T(8,128)(2,1)S(1)}, u32[]{:S(2)}, u32[]{:S(2)}) %collective-permute-start.6) | collective-permute-done | bytes 196640 | tf_op jit(solution)/shard_map/ppermute | solution.py:406
  19.0 0.5 collective-permute-done.7.refs_3_
  19.4 0.1 combine.1
  19.5 3.8 %collective-permute-start.8 = (bf16[256,128]{1,0:T(8,128)(2,1)S(1)}, bf16[256,128]{1,0:T(8,128)(2,1)S(1)}, u32[]{:S(2)}, u32[]{:S(2)}) collective-permute-start(bf16[256,128]{1,0:T(8,128)(2,1)S(1)} %get-tuple-element.46), channel_id=1, source_target_pairs={{0,12},{1,13},{2,14},{3,15},{4,8},{5,9},{6,10},{7,11},{8,4},{9,5},... | collective-permute-start | bytes 196616 | tf_op jit(solution)/shard_map/ppermute | solution.py:412
  23.3 0.0 collective-permute-start.9
  23.3 0.0 collective-permute-done.2.refs_1_
  23.3 0.7 %collective-permute-start.10 = (bf16[256,128]{1,0:T(8,128)(2,1)S(1)}, bf16[256,128]{1,0:T(8,128)(2,1)S(1)}, u32[]{:S(2)}, u32[]{:S(2)}) collective-permute-start(bf16[256,128]{1,0:T(8,128)(2,1)S(1)} %get-tuple-element.48), channel_id=1, source_target_pairs={{0,4},{1,5},{2,6},{3,7},{4,0},{5,1},{6,2},{7,3},{8,12},{9,13},{10,... | collective-permute-start | bytes 196616 | tf_op jit(solution)/shard_map/ppermute | solution.py:412
  24.0 0.0 collective-permute-done.3.refs_2_
  24.0 0.0 collective-permute-done.4.refs_3_
  24.0 2.1 %collective-permute-done.8.refs_4_ = bf16[256,128]{1,0:T(8,128)(2,1)S(1)} collective-permute-done((bf16[256,128]{1,0:T(8,128)(2,1)S(1)}, bf16[256,128]{1,0:T(8,128)(2,1)S(1)}, u32[]{:S(2)}, u32[]{:S(2)}) %collective-permute-start.8) | collective-permute-done | bytes 65568 | tf_op jit(solution)/shard_map/ppermute | solution.py:412
  26.1 2.7 %collective-permute-done.9.refs_5_ = bf16[256,128]{1,0:T(8,128)(2,1)S(1)} collective-permute-done((bf16[256,128]{1,0:T(8,128)(2,1)S(1)}, bf16[256,128]{1,0:T(8,128)(2,1)S(1)}, u32[]{:S(2)}, u32[]{:S(2)}) %collective-permute-start.9) | collective-permute-done | bytes 65568 | tf_op jit(solution)/shard_map/ppermute | solution.py:412
  28.8 0.0 collective-permute-done.10.refs_6_
  28.8 0.0 copy-done
  28.8 0.6 %layer.1 = (bf16[128,256]{1,0:T(8,128)(2,1)S(1)}, f32[256,128]{1,0:T(8,128)S(1)}, f32[256,256]{1,0:T(8,128)S(1)}, f32[256,256]{1,0:T(8,128)S(1)}) custom-call(f32[256,128]{1,0:T(8,128)S(1)} %get-tuple-element.38.refs_0_, bf16[256,128]{1,0:T(8,128)(2,1)S(1)} %collective-permute-done.2.refs_1_, bf16[256,128]{1,0:T(8,128)(2,1)S(1)} %collective-permute-done.3.refs_2_, ...), custom_call_target="tpu_custom_call" | custom-call | tf_op jit(solution)/shard_map/layer/pallas_call | solution.py:228
  29.5 2.7 %collective-permute-start.13 = (bf16[128,256]{1,0:T(8,128)(2,1)S(1)}, bf16[128,256]{1,0:T(8,128)(2,1)S(1)}, u32[]{:S(2)}, u32[]{:S(2)}) collective-permute-start(bf16[128,256]{1,0:T(8,128)(2,1)S(1)} %get-tuple-element.53.refs_0_), channel_id=1, source_target_pairs={{0,12},{1,13},{2,14},{3,15},{4,8},{5,9},{6,10},{7,11},{8,4},{9,5},... | collective-permute-start | bytes 196616 | tf_op jit(solution)/shard_map/ppermute | solution.py:412
  32.2 0.3 weight_terms.1.refs_0_
  32.4 2.5 %collective-permute-start.16 = (bf16[144,256]{1,0:T(8,128)(2,1)S(1)}, bf16[144,256]{1,0:T(8,128)(2,1)S(1)}, u32[]{:S(2)}, u32[]{:S(2)}) collective-permute-start(bf16[144,256]{1,0:T(8,128)(2,1)S(1)} %weight_terms.1.refs_0_), channel_id=1, source_target_pairs={{0,3},{1,2},{2,1},{3,0},{4,7},{5,6},{6,5},{7,4},{8,11},{9,10},{10,... | collective-permute-start | bytes 221192 | tf_op jit(solution)/shard_map/ppermute | solution.py:406
  34.9 0.6 collective-permute-start.15
  35.5 0.5 collective-permute-start.14
  36.0 0.0 collective-permute-start.12
  36.0 0.0 collective-permute-done.13.refs_3_
  36.0 1.8 %collective-permute-start.11 = (bf16[128,256]{1,0:T(8,128)(2,1)S(1)}, bf16[128,256]{1,0:T(8,128)(2,1)S(1)}, u32[]{:S(2)}, u32[]{:S(2)}) collective-permute-start(bf16[128,256]{1,0:T(8,128)(2,1)S(1)} %get-tuple-element.53.refs_0_), channel_id=1, source_target_pairs={{0,4},{1,5},{2,6},{3,7},{4,0},{5,1},{6,2},{7,3},{8,12},{9,13},{10,... | collective-permute-start | bytes 196616 | tf_op jit(solution)/shard_map/ppermute | solution.py:412
  37.8 3.4 %collective-permute-done.12.refs_2_ = bf16[128,256]{1,0:T(8,128)(2,1)S(1)} collective-permute-done((bf16[128,256]{1,0:T(8,128)(2,1)S(1)}, bf16[128,256]{1,0:T(8,128)(2,1)S(1)}, u32[]{:S(2)}, u32[]{:S(2)}) %collective-permute-start.12) | collective-permute-done | bytes 65568 | tf_op jit(solution)/shard_map/ppermute | solution.py:412
  41.2 0.0 collective-permute-done.11.refs_1_
  41.2 0.0 collective-permute-done.16.refs_3_
  41.2 0.0 collective-permute-done.15.refs_2_
  41.2 0.0 collective-permute-done.14.refs_1_
  41.2 2.5 %collective-permute-start.19 = (bf16[4,128,256]{2,1,0:T(8,128)(2,1)S(1)}, bf16[4,128,256]{2,1,0:T(8,128)(2,1)S(1)}, u32[]{:S(2)}, u32[]{:S(2)}) collective-permute-start(bf16[4,128,256]{2,1,0:T(8,128)(2,1)S(1)} %stack_line.1.refs_0_), channel_id=1, source_target_pairs={{0,3},{1,2},{2,1},{3,0},{4,7},{5,6},{6,5},{7,4},{8,11},{9,10},{10,... | collective-permute-start | bytes 786440 | tf_op jit(solution)/shard_map/ppermute | solution.py:406
  43.7 0.6 %collective-permute-start.18 = (bf16[4,128,256]{2,1,0:T(8,128)(2,1)S(1)}, bf16[4,128,256]{2,1,0:T(8,128)(2,1)S(1)}, u32[]{:S(2)}, u32[]{:S(2)}) collective-permute-start(bf16[4,128,256]{2,1,0:T(8,128)(2,1)S(1)} %stack_line.1.refs_0_), channel_id=1, source_target_pairs={{0,1},{1,0},{2,3},{3,2},{4,5},{5,4},{6,7},{7,6},{8,9},{9,8},{10,11... | collective-permute-start | bytes 786440 | tf_op jit(solution)/shard_map/ppermute | solution.py:406
  44.3 0.4 collective-permute-start.17
  44.8 2.3 %collective-permute-start.22 = (bf16[144,256]{1,0:T(8,128)(2,1)S(1)}, bf16[144,256]{1,0:T(8,128)(2,1)S(1)}, u32[]{:S(2)}, u32[]{:S(2)}) collective-permute-start(bf16[144,256]{1,0:T(8,128)(2,1)S(1)} %sum_terms.1.refs_4_), channel_id=1, source_target_pairs={{0,12},{1,13},{2,14},{3,15},{4,8},{5,9},{6,10},{7,11},{8,4},{9,5},... | collective-permute-start | bytes 221192 | tf_op jit(solution)/shard_map/ppermute | solution.py:412
  47.1 0.1 collective-permute-start.21
  47.2 3.4 %collective-permute-done.19.refs_1_ = bf16[4,128,256]{2,1,0:T(8,128)(2,1)S(1)} collective-permute-done((bf16[4,128,256]{2,1,0:T(8,128)(2,1)S(1)}, bf16[4,128,256]{2,1,0:T(8,128)(2,1)S(1)}, u32[]{:S(2)}, u32[]{:S(2)}) %collective-permute-start.19) | collective-permute-done | bytes 262176 | tf_op jit(solution)/shard_map/ppermute | solution.py:406
  50.6 1.1 %collective-permute-start.20 = (bf16[144,256]{1,0:T(8,128)(2,1)S(1)}, bf16[144,256]{1,0:T(8,128)(2,1)S(1)}, u32[]{:S(2)}, u32[]{:S(2)}) collective-permute-start(bf16[144,256]{1,0:T(8,128)(2,1)S(1)} %sum_terms.1.refs_4_), channel_id=1, source_target_pairs={{0,4},{1,5},{2,6},{3,7},{4,0},{5,1},{6,2},{7,3},{8,12},{9,13},{10,... | collective-permute-start | bytes 221192 | tf_op jit(solution)/shard_map/ppermute | solution.py:412
  51.7 0.4 backward_product.2
  52.1 0.0 collective-permute-done.22.refs_7_
  52.2 0.8 %collective-permute-done.21.refs_6_ = bf16[144,256]{1,0:T(8,128)(2,1)S(1)} collective-permute-done((bf16[144,256]{1,0:T(8,128)(2,1)S(1)}, bf16[144,256]{1,0:T(8,128)(2,1)S(1)}, u32[]{:S(2)}, u32[]{:S(2)}) %collective-permute-start.21) | collective-permute-done | bytes 73760 | tf_op jit(solution)/shard_map/ppermute | solution.py:412
  52.9 2.0 %collective-permute-done.20.refs_5_ = bf16[144,256]{1,0:T(8,128)(2,1)S(1)} collective-permute-done((bf16[144,256]{1,0:T(8,128)(2,1)S(1)}, bf16[144,256]{1,0:T(8,128)(2,1)S(1)}, u32[]{:S(2)}, u32[]{:S(2)}) %collective-permute-start.20) | collective-permute-done | bytes 73760 | tf_op jit(solution)/shard_map/ppermute | solution.py:412
  55.0 0.0 collective-permute-done.18.refs_1_
  55.0 0.0 collective-permute-done.17.refs_0_
  55.0 0.4 backward_product.3
  55.4 0.1 collective-permute-start.23
  55.5 0.7 %activations.1 = bf16[256,256]{1,0:T(8,128)(2,1)} custom-call(f32[256,256]{1,0:T(8,128)S(1)} %get-tuple-element.49.preact_ref), custom_call_target="tpu_custom_call" | custom-call | tf_op jit(solution)/shard_map/activations/pallas_call | solution.py:247
  56.3 0.6 %collective-permute-done.23.refs_0_ = bf16[272,256]{1,0:T(8,128)(2,1)S(1)} collective-permute-done((bf16[272,256]{1,0:T(8,128)(2,1)S(1)}, bf16[272,256]{1,0:T(8,128)(2,1)S(1)}, u32[]{:S(2)}, u32[]{:S(2)}) %collective-permute-start.23) | collective-permute-done | bytes 139296 | tf_op jit(solution)/shard_map/ppermute | solution.py:400
  56.9 0.7 %finish.1 = (bf16[256,128]{1,0:T(8,128)(2,1)}, f32[128,256]{1,0:T(8,128)}, f32[1,256]{1,0:T(1,128)}) custom-call(s32[1,256]{1,0:T(1,128)S(1)} %bitcast.13, f32[128,256]{1,0:T(8,128)S(1)} %get-tuple-element.63.own_ref, bf16[272,256]{1,0:T(8,128)(2,1)S(1)} %get-tuple-element.64.sent_ref, bf16[272,256]{1,0:T(8,128)(2,1)S(1)} %collective-permute-done.23.refs_0_), custom_call_target="tpu_custom_call" | custom-call | tf_op jit(solution)/shard_map/finish/pallas_call | solution.py:368
  (7 shorter events, 0.1 us)
Async XLA Ops:
  0.6 3.9 %collective-permute-start.1 = (bf16[256,128]{1,0:T(8,128)(2,1)}, bf16[256,128]{1,0:T(8,128)(2,1)S(1)}, u32[]{:S(2)}, u32[]{:S(2)}) collective-permute-start(bf16[256,128]{1,0:T(8,128)(2,1)} %refs_2_.1), channel_id=1, source_target_pairs={{0,16},{16,0},{1,17},{17,1},{2,18},{18,2},{3,19},{19,3},{4,20},{20... | collective-permute-start | bytes 196616 | tf_op jit(solution)/shard_map/ppermute | solution.py:400
  1.1 3.4 %collective-permute-start = (s32[256]{0:T(256)}, s32[256]{0:T(256)S(1)}, u32[]{:S(2)}, u32[]{:S(2)}) collective-permute-start(s32[256]{0:T(256)} %param.12), channel_id=1, source_target_pairs={{0,16},{16,0},{1,17},{17,1},{2,18},{18,2},{3,19},{19,3},{4,20},{20... | collective-permute-start | bytes 3080 | tf_op jit(solution)/shard_map/ppermute | solution.py:400
  1.9 2.6 %copy-start.1 = (bf16[256,128]{1,0:T(8,128)(2,1)S(1)}, bf16[256,128]{1,0:T(8,128)(2,1)}, u32[]{:S(2)}) copy-start(bf16[256,128]{1,0:T(8,128)(2,1)} %refs_2_.1) | copy-start | bytes 196612
  1.9 2.6 %copy-start.3 = (s32[256]{0:T(256)S(1)}, s32[256]{0:T(256)}, u32[]{:S(2)}) copy-start(s32[256]{0:T(256)} %param.12) | copy-start | bytes 3076
  5.1 9.6 %collective-permute-start.5 = (bf16[3,256,128]{2,1,0:T(8,128)(2,1)S(1)}, bf16[3,256,128]{2,1,0:T(8,128)(2,1)S(1)}, u32[]{:S(2)}, u32[]{:S(2)}) collective-permute-start(bf16[3,256,128]{2,1,0:T(8,128)(2,1)S(1)} %get-tuple-element.43), channel_id=1, source_target_pairs={{0,3},{1,2},{2,1},{3,0},{4,7},{5,6},{6,5},{7,4},{8,11},{9,10},{10,... | collective-permute-start | bytes 589832 | tf_op jit(solution)/shard_map/ppermute | solution.py:406
  8.9 19.9 %copy-start = (bf16[256,256]{1,0:T(8,128)(2,1)S(1)}, bf16[256,256]{1,0:T(8,128)(2,1)}, u32[]{:S(2)}) copy-start(bf16[256,256]{1,0:T(8,128)(2,1)} %refs_10_.1) | copy-start | bytes 393220
  8.9 19.9 %copy-start.2 = (bf16[128,256]{1,0:T(8,128)(2,1)S(1)}, bf16[128,256]{1,0:T(8,128)(2,1)}, u32[]{:S(2)}) copy-start(bf16[128,256]{1,0:T(8,128)(2,1)} %refs_8_.1) | copy-start | bytes 196612
  8.9 19.9 %copy-start.4 = (f32[256]{0:T(256)S(1)}, f32[256]{0:T(256)}, u32[]{:S(2)}) copy-start(f32[256]{0:T(256)} %param.10) | copy-start | bytes 3076
  9.5 9.4 %collective-permute-start.6 = (bf16[3,256,128]{2,1,0:T(8,128)(2,1)S(1)}, bf16[3,256,128]{2,1,0:T(8,128)(2,1)S(1)}, u32[]{:S(2)}, u32[]{:S(2)}) collective-permute-start(bf16[3,256,128]{2,1,0:T(8,128)(2,1)S(1)} %get-tuple-element.44), channel_id=1, source_target_pairs={{0,2},{1,3},{2,0},{3,1},{4,6},{5,7},{6,4},{7,5},{8,10},{9,11},{10,... | collective-permute-start | bytes 589832 | tf_op jit(solution)/shard_map/ppermute | solution.py:406
  10.2 9.3 %collective-permute-start.7 = (bf16[3,256,128]{2,1,0:T(8,128)(2,1)S(1)}, bf16[3,256,128]{2,1,0:T(8,128)(2,1)S(1)}, u32[]{:S(2)}, u32[]{:S(2)}) collective-permute-start(bf16[3,256,128]{2,1,0:T(8,128)(2,1)S(1)} %get-tuple-element.45), channel_id=1, source_target_pairs={{0,1},{1,0},{2,3},{3,2},{4,5},{5,4},{6,7},{7,6},{8,9},{9,8},{10,11... | collective-permute-start | bytes 589832 | tf_op jit(solution)/shard_map/ppermute | solution.py:406
  10.8 12.4 %collective-permute-start.2 = (bf16[256,128]{1,0:T(8,128)(2,1)S(1)}, bf16[256,128]{1,0:T(8,128)(2,1)S(1)}, u32[]{:S(2)}, u32[]{:S(2)}) collective-permute-start(bf16[256,128]{1,0:T(8,128)(2,1)S(1)} %get-tuple-element.39), channel_id=1, source_target_pairs={{0,3},{1,2},{2,1},{3,0},{4,7},{5,6},{6,5},{7,4},{8,11},{9,10},{10,... | collective-permute-start | bytes 196616 | tf_op jit(solution)/shard_map/ppermute | solution.py:406
  13.8 10.2 %collective-permute-start.3 = (bf16[256,128]{1,0:T(8,128)(2,1)S(1)}, bf16[256,128]{1,0:T(8,128)(2,1)S(1)}, u32[]{:S(2)}, u32[]{:S(2)}) collective-permute-start(bf16[256,128]{1,0:T(8,128)(2,1)S(1)} %get-tuple-element.40), channel_id=1, source_target_pairs={{0,2},{1,3},{2,0},{3,1},{4,6},{5,7},{6,4},{7,5},{8,10},{9,11},{10,... | collective-permute-start | bytes 196616 | tf_op jit(solution)/shard_map/ppermute | solution.py:406
  14.6 9.3 %collective-permute-start.4 = (bf16[256,128]{1,0:T(8,128)(2,1)S(1)}, bf16[256,128]{1,0:T(8,128)(2,1)S(1)}, u32[]{:S(2)}, u32[]{:S(2)}) collective-permute-start(bf16[256,128]{1,0:T(8,128)(2,1)S(1)} %get-tuple-element.41), channel_id=1, source_target_pairs={{0,1},{1,0},{2,3},{3,2},{4,5},{5,4},{6,7},{7,6},{8,9},{9,8},{10,11... | collective-permute-start | bytes 196616 | tf_op jit(solution)/shard_map/ppermute | solution.py:406
  19.5 6.6 %collective-permute-start.8 = (bf16[256,128]{1,0:T(8,128)(2,1)S(1)}, bf16[256,128]{1,0:T(8,128)(2,1)S(1)}, u32[]{:S(2)}, u32[]{:S(2)}) collective-permute-start(bf16[256,128]{1,0:T(8,128)(2,1)S(1)} %get-tuple-element.46), channel_id=1, source_target_pairs={{0,12},{1,13},{2,14},{3,15},{4,8},{5,9},{6,10},{7,11},{8,4},{9,5},... | collective-permute-start | bytes 196616 | tf_op jit(solution)/shard_map/ppermute | solution.py:412
  23.3 5.6 %collective-permute-start.9 = (bf16[256,128]{1,0:T(8,128)(2,1)S(1)}, bf16[256,128]{1,0:T(8,128)(2,1)S(1)}, u32[]{:S(2)}, u32[]{:S(2)}) collective-permute-start(bf16[256,128]{1,0:T(8,128)(2,1)S(1)} %get-tuple-element.47), channel_id=1, source_target_pairs={{0,8},{1,9},{2,10},{3,11},{4,12},{5,13},{6,14},{7,15},{8,0},{9,1},... | collective-permute-start | bytes 196616 | tf_op jit(solution)/shard_map/ppermute | solution.py:412
  23.3 5.6 %collective-permute-start.10 = (bf16[256,128]{1,0:T(8,128)(2,1)S(1)}, bf16[256,128]{1,0:T(8,128)(2,1)S(1)}, u32[]{:S(2)}, u32[]{:S(2)}) collective-permute-start(bf16[256,128]{1,0:T(8,128)(2,1)S(1)} %get-tuple-element.48), channel_id=1, source_target_pairs={{0,4},{1,5},{2,6},{3,7},{4,0},{5,1},{6,2},{7,3},{8,12},{9,13},{10,... | collective-permute-start | bytes 196616 | tf_op jit(solution)/shard_map/ppermute | solution.py:412
  29.5 6.5 %collective-permute-start.13 = (bf16[128,256]{1,0:T(8,128)(2,1)S(1)}, bf16[128,256]{1,0:T(8,128)(2,1)S(1)}, u32[]{:S(2)}, u32[]{:S(2)}) collective-permute-start(bf16[128,256]{1,0:T(8,128)(2,1)S(1)} %get-tuple-element.53.refs_0_), channel_id=1, source_target_pairs={{0,12},{1,13},{2,14},{3,15},{4,8},{5,9},{6,10},{7,11},{8,4},{9,5},... | collective-permute-start | bytes 196616 | tf_op jit(solution)/shard_map/ppermute | solution.py:412
  32.4 8.7 %collective-permute-start.16 = (bf16[144,256]{1,0:T(8,128)(2,1)S(1)}, bf16[144,256]{1,0:T(8,128)(2,1)S(1)}, u32[]{:S(2)}, u32[]{:S(2)}) collective-permute-start(bf16[144,256]{1,0:T(8,128)(2,1)S(1)} %weight_terms.1.refs_0_), channel_id=1, source_target_pairs={{0,3},{1,2},{2,1},{3,0},{4,7},{5,6},{6,5},{7,4},{8,11},{9,10},{10,... | collective-permute-start | bytes 221192 | tf_op jit(solution)/shard_map/ppermute | solution.py:406
  34.9 6.2 %collective-permute-start.15 = (bf16[144,256]{1,0:T(8,128)(2,1)S(1)}, bf16[144,256]{1,0:T(8,128)(2,1)S(1)}, u32[]{:S(2)}, u32[]{:S(2)}) collective-permute-start(bf16[144,256]{1,0:T(8,128)(2,1)S(1)} %weight_terms.1.refs_0_), channel_id=1, source_target_pairs={{0,2},{1,3},{2,0},{3,1},{4,6},{5,7},{6,4},{7,5},{8,10},{9,11},{10,... | collective-permute-start | bytes 221192 | tf_op jit(solution)/shard_map/ppermute | solution.py:406
  35.5 5.7 %collective-permute-start.14 = (bf16[144,256]{1,0:T(8,128)(2,1)S(1)}, bf16[144,256]{1,0:T(8,128)(2,1)S(1)}, u32[]{:S(2)}, u32[]{:S(2)}) collective-permute-start(bf16[144,256]{1,0:T(8,128)(2,1)S(1)} %weight_terms.1.refs_0_), channel_id=1, source_target_pairs={{0,1},{1,0},{2,3},{3,2},{4,5},{5,4},{6,7},{7,6},{8,9},{9,8},{10,11... | collective-permute-start | bytes 221192 | tf_op jit(solution)/shard_map/ppermute | solution.py:406
  36.0 5.2 %collective-permute-start.12 = (bf16[128,256]{1,0:T(8,128)(2,1)S(1)}, bf16[128,256]{1,0:T(8,128)(2,1)S(1)}, u32[]{:S(2)}, u32[]{:S(2)}) collective-permute-start(bf16[128,256]{1,0:T(8,128)(2,1)S(1)} %get-tuple-element.53.refs_0_), channel_id=1, source_target_pairs={{0,8},{1,9},{2,10},{3,11},{4,12},{5,13},{6,14},{7,15},{8,0},{9,1},... | collective-permute-start | bytes 196616 | tf_op jit(solution)/shard_map/ppermute | solution.py:412
  36.0 5.2 %collective-permute-start.11 = (bf16[128,256]{1,0:T(8,128)(2,1)S(1)}, bf16[128,256]{1,0:T(8,128)(2,1)S(1)}, u32[]{:S(2)}, u32[]{:S(2)}) collective-permute-start(bf16[128,256]{1,0:T(8,128)(2,1)S(1)} %get-tuple-element.53.refs_0_), channel_id=1, source_target_pairs={{0,4},{1,5},{2,6},{3,7},{4,0},{5,1},{6,2},{7,3},{8,12},{9,13},{10,... | collective-permute-start | bytes 196616 | tf_op jit(solution)/shard_map/ppermute | solution.py:412
  41.2 9.4 %collective-permute-start.19 = (bf16[4,128,256]{2,1,0:T(8,128)(2,1)S(1)}, bf16[4,128,256]{2,1,0:T(8,128)(2,1)S(1)}, u32[]{:S(2)}, u32[]{:S(2)}) collective-permute-start(bf16[4,128,256]{2,1,0:T(8,128)(2,1)S(1)} %stack_line.1.refs_0_), channel_id=1, source_target_pairs={{0,3},{1,2},{2,1},{3,0},{4,7},{5,6},{6,5},{7,4},{8,11},{9,10},{10,... | collective-permute-start | bytes 786440 | tf_op jit(solution)/shard_map/ppermute | solution.py:406
  43.7 11.3 %collective-permute-start.18 = (bf16[4,128,256]{2,1,0:T(8,128)(2,1)S(1)}, bf16[4,128,256]{2,1,0:T(8,128)(2,1)S(1)}, u32[]{:S(2)}, u32[]{:S(2)}) collective-permute-start(bf16[4,128,256]{2,1,0:T(8,128)(2,1)S(1)} %stack_line.1.refs_0_), channel_id=1, source_target_pairs={{0,1},{1,0},{2,3},{3,2},{4,5},{5,4},{6,7},{7,6},{8,9},{9,8},{10,11... | collective-permute-start | bytes 786440 | tf_op jit(solution)/shard_map/ppermute | solution.py:406
  44.3 10.7 %collective-permute-start.17 = (bf16[4,128,256]{2,1,0:T(8,128)(2,1)S(1)}, bf16[4,128,256]{2,1,0:T(8,128)(2,1)S(1)}, u32[]{:S(2)}, u32[]{:S(2)}) collective-permute-start(bf16[4,128,256]{2,1,0:T(8,128)(2,1)S(1)} %stack_line.1.refs_0_), channel_id=1, source_target_pairs={{0,2},{1,3},{2,0},{3,1},{4,6},{5,7},{6,4},{7,5},{8,10},{9,11},{10,... | collective-permute-start | bytes 786440 | tf_op jit(solution)/shard_map/ppermute | solution.py:406
  44.8 7.3 %collective-permute-start.22 = (bf16[144,256]{1,0:T(8,128)(2,1)S(1)}, bf16[144,256]{1,0:T(8,128)(2,1)S(1)}, u32[]{:S(2)}, u32[]{:S(2)}) collective-permute-start(bf16[144,256]{1,0:T(8,128)(2,1)S(1)} %sum_terms.1.refs_4_), channel_id=1, source_target_pairs={{0,12},{1,13},{2,14},{3,15},{4,8},{5,9},{6,10},{7,11},{8,4},{9,5},... | collective-permute-start | bytes 221192 | tf_op jit(solution)/shard_map/ppermute | solution.py:412
  47.1 5.8 %collective-permute-start.21 = (bf16[144,256]{1,0:T(8,128)(2,1)S(1)}, bf16[144,256]{1,0:T(8,128)(2,1)S(1)}, u32[]{:S(2)}, u32[]{:S(2)}) collective-permute-start(bf16[144,256]{1,0:T(8,128)(2,1)S(1)} %sum_terms.1.refs_4_), channel_id=1, source_target_pairs={{0,8},{1,9},{2,10},{3,11},{4,12},{5,13},{6,14},{7,15},{8,0},{9,1},... | collective-permute-start | bytes 221192 | tf_op jit(solution)/shard_map/ppermute | solution.py:412
  50.6 4.4 %collective-permute-start.20 = (bf16[144,256]{1,0:T(8,128)(2,1)S(1)}, bf16[144,256]{1,0:T(8,128)(2,1)S(1)}, u32[]{:S(2)}, u32[]{:S(2)}) collective-permute-start(bf16[144,256]{1,0:T(8,128)(2,1)S(1)} %sum_terms.1.refs_4_), channel_id=1, source_target_pairs={{0,4},{1,5},{2,6},{3,7},{4,0},{5,1},{6,2},{7,3},{8,12},{9,13},{10,... | collective-permute-start | bytes 221192 | tf_op jit(solution)/shard_map/ppermute | solution.py:412
  55.4 1.4 %collective-permute-start.23 = (bf16[272,256]{1,0:T(8,128)(2,1)S(1)}, bf16[272,256]{1,0:T(8,128)(2,1)S(1)}, u32[]{:S(2)}, u32[]{:S(2)}) collective-permute-start(bf16[272,256]{1,0:T(8,128)(2,1)S(1)} %get-tuple-element.64.sent_ref), channel_id=1, source_target_pairs={{0,16},{16,0},{1,17},{17,1},{2,18},{18,2},{3,19},{19,3},{4,20},{20... | collective-permute-start | bytes 417800 | tf_op jit(solution)/shard_map/ppermute | solution.py:400

commit v3 on v2

--- a/solution.py
+++ b/solution.py
@@ -252,24 +252,48 @@
     )(preact)
 
 
-def terms_kernel(hidden_ref, grad_pre_ref, terms_ref):
+def terms_kernel(hidden_ref, grad_pre_ref, *refs):
+    outs, terms_ref = refs[:-1], refs[-1]
     grad_pre = grad_pre_ref[...]
     grads = split_two(grad_pre)
     upper, lower = split_two(jnp.transpose(hidden_ref[...]))
-    weight_term = dot(upper, grads[0]) + dot(lower, grads[0]) + dot(upper, grads[1])
-    depth = weight_term.shape[0]
-    terms_ref[0:depth, :] = weight_term.astype(BF16)
+    terms_ref[...] = dot(upper, grads[0]) + dot(lower, grads[0]) + dot(upper, grads[1])
     bias_term = jnp.sum(grad_pre, axis=0, keepdims=True)
-    terms_ref[depth:, :] = jnp.broadcast_to(bias_term, (16, bias_term.shape[1])).astype(BF16)
+    pieces = len(outs)
+    rows = terms_ref.shape[0] // pieces
+    for step, out_ref in enumerate(outs):
+        start = pl.multiple_of(other(lax.axis_index("row"), step, pieces) * rows, 8)
+        out_ref[0:rows, :] = terms_ref[pl.ds(start, rows), :]
+        out_ref[rows:, :] = jnp.broadcast_to(bias_term, (16, bias_term.shape[1]))
 
 
 def terms_of(hidden, grad_pre):
+    pieces = lax.axis_size("row")
+    depth, width = hidden.shape[1], grad_pre.shape[1]
     return pl.pallas_call(
         terms_kernel,
-        out_shape=jax.ShapeDtypeStruct((hidden.shape[1] + 16, grad_pre.shape[1]), BF16),
+        out_shape=[jax.ShapeDtypeStruct((depth // pieces + 16, width), F32)] * pieces,
+        scratch_shapes=[pltpu.VMEM((depth, width), F32)],
         compiler_params=params(),
         name="weight_terms",
     )(hidden, grad_pre)
+
+
+def pack_kernel(outgoing_ref, *refs):
+    pieces, out_ref = refs[:-1], refs[-1]
+    depth = outgoing_ref.shape[0]
+    out_ref[0:depth, :] = outgoing_ref[...]
+    out_ref[depth:, :] = tree_sum([piece[...] for piece in pieces]).astype(BF16)
+
+
+def pack(outgoing, pieces):
+    depth, nodes = outgoing.shape
+    return pl.pallas_call(
+        pack_kernel,
+        out_shape=jax.ShapeDtypeStruct((depth + pieces[0].shape[0], nodes), BF16),
+        compiler_params=params(),
+        name="pack",
+    )(outgoing, *pieces)
 
 
 def tree_sum(values):
@@ -280,60 +304,61 @@
     return values[0]
 
 
-def sum_kernel(*refs):
-    refs[-1][...] = tree_sum([ref[...].astype(F32) for ref in refs[:-1]]).astype(BF16)
-
-
-def sum_terms(items):
-    return pl.pallas_call(
-        sum_kernel,
-        out_shape=jax.ShapeDtypeStruct(items[0].shape, BF16),
+def sum_kernel(depth, *refs):
+    refs[-1][...] = tree_sum([ref[depth:, :].astype(F32) for ref in refs[:-1]]).astype(BF16)
+
+
+def sum_terms(parcels, depth):
+    rows, width = parcels[0].shape
+    return pl.pallas_call(
+        functools.partial(sum_kernel, depth),
+        out_shape=jax.ShapeDtypeStruct((rows - depth, width), BF16),
         compiler_params=params(),
         name="sum_terms",
-    )(*items)
-
-
-def stack_kernel(low, *refs):
-    items, out_ref = refs[:-1], refs[-1]
-    _, line, _ = spot(low)
-    for step, item in enumerate(items):
-        out_ref[source(line, step, len(items))] = item[...]
-
-
-def stack_line(low, items):
-    return pl.pallas_call(
-        functools.partial(stack_kernel, low),
+    )(*parcels)
+
+
+def stack_kernel(*refs):
+    for step, ref in enumerate(refs[:-1]):
+        refs[-1][step] = ref[...]
+
+
+def stack_line(items):
+    return pl.pallas_call(
+        stack_kernel,
         out_shape=jax.ShapeDtypeStruct((len(items),) + items[0].shape, BF16),
-        in_specs=[pl.BlockSpec(memory_space=pltpu.VMEM)] * len(items),
         compiler_params=params(),
         name="stack_line",
     )(*items)
 
 
 def backward_kernel(steps, pieces, has_totals, dense_ref, *refs):
-    stacks, inputs, outs = refs[: len(steps)], refs[len(steps) : -pieces], refs[-pieces:]
+    count = len(steps)
+    parcels, stacks = refs[:count], refs[count : 2 * count]
+    inputs, outs = refs[2 * count : -pieces], refs[-pieces:]
     terms = inputs[pieces if has_totals else 0 :]
     high, low, nodes, _ = dense_ref.shape
-    row, _, plane = spot(low)
+    row, line, plane = spot(low)
     for piece in range(pieces):
         columns = piece_columns(other(row, piece, pieces), nodes)
         total = inputs[piece][...] if has_totals else None
-        for step, stack_ref in zip(steps, stacks):
+        for step, parcel_ref, stack_ref in zip(steps, parcels, stacks):
             origin = source(plane, step, low)
-            for chunk in range(high):
-                term = dot(stack_ref[chunk], dense_ref[chunk, origin, :, columns])
+            depth = stack_ref.shape[1]
+            for hop in range(high):
+                values = stack_ref[hop - 1] if hop else parcel_ref[0:depth, :]
+                term = dot(values, dense_ref[source(line, hop, high), origin, :, columns])
                 total = term if total is None else total + term
-        depth = total.shape[0]
         outs[piece][0:depth, :] = total.astype(outs[piece].dtype)
         if terms and piece:
             outs[piece][depth:, :] = tree_sum([ref[...].astype(F32) for ref in terms]).astype(BF16)
 
 
-def backward(dense, stacks, totals, terms=()):
+def backward(dense, parcels, stacks, totals, terms=()):
     nodes, slots = dense.shape[2:]
     pieces = slots // nodes
     depth = next(iter(stacks.values())).shape[1]
-    inputs = list(stacks.values()) + list(totals) + list(terms)
+    inputs = list(parcels.values()) + list(stacks.values()) + list(totals) + list(terms)
 
     def shape_of(piece):
         if terms and piece:
@@ -357,9 +382,11 @@
         total = total + share[0:depth, :].astype(F32)
     row = lax.rsqrt(degrees_ref[...].astype(F32))
     outs[0][...] = jnp.transpose(row * total).astype(BF16)
-    terms = tree_sum([ref[depth:, :].astype(F32) for ref in (sent_ref, *shares)])
-    outs[1][...] = terms[0:depth]
-    outs[2][...] = terms[depth : depth + 1]
+    rows = depth // pieces
+    for step, ref in enumerate((sent_ref, *shares)):
+        start = pl.multiple_of(source(lax.axis_index("row"), step, pieces) * rows, 8)
+        outs[1][pl.ds(start, rows), :] = ref[depth : depth + rows, :].astype(F32)
+    outs[2][...] = sent_ref[depth + rows : depth + rows + 16, :].astype(F32)[0:1]
 
 
 def finish(degrees_row, own, sent, shares):
@@ -431,21 +458,27 @@
     shares = [over_line(chunks[hop - 1], hop) for hop in far_first(high)]
     outgoing, hidden, preact, grad_pre = layer(here + shares, degrees_row, weight, bias_vector[None, :], cotangent)
 
-    line = {0: outgoing} | {step: over_line(outgoing, step) for step in far_first(high)}
-    terms = terms_of(hidden, grad_pre)
+    line = [over_line(outgoing, step) for step in far_first(high)][::-1]
+    pieces = terms_of(hidden, grad_pre)
     activations = activations_of(preact)
-    parts = {0: terms} | {step: over_plane(terms, step) for step in far_first(low)}
-    line, parts = lax.optimization_barrier((line, parts))
-    stacked = stack_line(low, [line[step] for step in range(high)])
-    terms = sum_terms([parts[step] for step in range(low)])
+    parcel = pack(outgoing, [pieces[0]] + [over_row(pieces[step], step) for step in range(1, rows)])
+    parcels = {0: parcel} | {step: over_plane(parcel, step) for step in far_first(low)}
+    line, parcels = lax.optimization_barrier((line, parcels))
+    stacked = stack_line(line)
     stacks = {0: stacked} | {step: over_plane(stacked, step) for step in far_first(low)}
+    terms = sum_terms([parcels[step] for step in range(low)], weight.shape[0])
     parts = {0: terms} | {step: over_line(terms, step) for step in far_first(high)}
     terms = [parts[step] for step in range(high)]
     steps, totals = list(stacks), []
     for group in (steps[: low // 2], steps[low // 2 :]):
         if group:
-            arrived = {step: stacks[step] for step in group}
-            totals = backward(dense, arrived, totals, terms if group[-1] == steps[-1] else ())
+            totals = backward(
+                dense,
+                {step: parcels[step] for step in group},
+                {step: stacks[step] for step in group},
+                totals,
+                terms if group[-1] == steps[-1] else (),
+            )
     returned = [over_row(totals[step], step) for step in range(1, rows)]
     grad_features, grad_weight, grad_bias = finish(degrees_row, totals[0], totals[1], returned)
     return activations, grad_features, grad_weight, grad_bias[0]

time: 57.9 us -> 57 us (0.984)
  waiting for transfers between devices: 18.1 us -> 17.2 us
    ppermute x12, waiting for transfers between devices: 6.41 us -> 5.66 us  [over_plane(): return lax.ppermute(values, 'col', pairs)]
  transfers between devices with their start and end apart: 24 -> 25, of which waited for: 10 -> 10; matrix products, arithmetic and copies ran while one was open for 0% -> 0% of each run, Pallas kernels for 9% -> 9%
where the time goes in v3:
time: 57 us; the launch traced here: 56.7 us
  starting transfers between devices  30.4 us (53%)
  waiting for transfers between devices  17.2 us (30%)
  Pallas kernels  7.69 us (13%)
  between operations  1.46 us (3%)
    ppermute x12, starting transfers between devices, over_plane(): return lax.ppermute(values, 'col', pairs)  17.7 us
    ppermute x9, starting transfers between devices, over_line(): return lax.ppermute(values, 'col', pairs)  11.9 us
    ppermute x9, waiting for transfers between devices, over_line(): return lax.ppermute(values, 'col', pairs)  11 us
    ppermute x12, waiting for transfers between devices, over_plane(): return lax.ppermute(values, 'col', pairs)  5.66 us
    pallas_call x1, Pallas kernels, densify(): pl.pallas_call(functools.partial(densify_kernel, col_slots), out_shape=ja...  2.58 us
    pallas_call x3, Pallas kernels, forward(): pl.pallas_call(functools.partial(forward_kernel, wanted, pieces, scaling)...  1.69 us
  transfers between devices with their start and end apart: 25, of which 10 were waited for; matrix products, arithmetic and copies ran while one was open for 0% of the time, Pallas kernels for 9%

profile of v3, /device:TPU:0, one launch (start us, length us, event | category | flops | bytes accessed | tf_op | source)
XLA Modules:
  0.0 56.7 jit_solution(5924533018224322607)
XLA Ops:
  0.6 0.5 collective-permute-start.1
  1.1 0.1 collective-permute-start
  1.9 0.0 copy-start.1
  1.9 2.6 %densify.1 = bf16[32,128,512]{2,1,0:T(8,128)(2,1)S(1)} custom-call(s32[1,1,128]{2,1,0:T(1,128)} %positions_hbm.1, s32[1,1]{1,0:T(1,128)S(6)} %copy.12.counts_ref, bf16[128,128,128]{2,1,0:T(8,128)(2,1)} %bitcast.16), custom_call_target="tpu_custom_call" | custom-call | tf_op jit(solution)/shard_map/densify/pallas_call | solution.py:107
  4.5 0.0 collective-permute-done
  4.5 0.0 collective-permute-done.1.refs_3_
  4.5 0.5 forward_product.3
  5.0 3.9 %collective-permute-start.5 = (bf16[3,256,128]{2,1,0:T(8,128)(2,1)S(1)}, bf16[3,256,128]{2,1,0:T(8,128)(2,1)S(1)}, u32[]{:S(2)}, u32[]{:S(2)}) collective-permute-start(bf16[3,256,128]{2,1,0:T(8,128)(2,1)S(1)} %get-tuple-element.44), channel_id=1, source_target_pairs={{0,3},{1,2},{2,1},{3,0},{4,7},{5,6},{6,5},{7,4},{8,11},{9,10},{10,... | collective-permute-start | bytes 589832 | tf_op jit(solution)/shard_map/ppermute | solution.py:433
  9.0 0.6 forward_product.5
  9.5 0.8 %collective-permute-start.6 = (bf16[3,256,128]{2,1,0:T(8,128)(2,1)S(1)}, bf16[3,256,128]{2,1,0:T(8,128)(2,1)S(1)}, u32[]{:S(2)}, u32[]{:S(2)}) collective-permute-start(bf16[3,256,128]{2,1,0:T(8,128)(2,1)S(1)} %get-tuple-element.45), channel_id=1, source_target_pairs={{0,2},{1,3},{2,0},{3,1},{4,6},{5,7},{6,4},{7,5},{8,10},{9,11},{10,... | collective-permute-start | bytes 589832 | tf_op jit(solution)/shard_map/ppermute | solution.py:433
  10.4 0.0 collective-permute-start.7
  10.4 0.6 %forward_product.4 = (f32[3,256,128]{2,1,0:T(8,128)S(1)}, bf16[256,128]{1,0:T(8,128)(2,1)S(1)}, bf16[256,128]{1,0:T(8,128)(2,1)S(1)}, bf16[256,128]{1,0:T(8,128)(2,1)S(1)}, f32[256,128]{1,0:T(8,128)S(1)}) custom-call(bf16[4,4,256,512]{3,2,1,0:T(8,128)(2,1)S(1)} %bitcast.8, bf16[256,128]{1,0:T(8,128)(2,1)S(1)} %get-tuple-element.37.refs_0_, ...), custom_call_target="tpu_custom_call" | custom-call | tf_op jit(solution)/shard_map/forward_product/pallas_call | solution.py:177
  11.0 2.8 %collective-permute-start.2 = (bf16[256,128]{1,0:T(8,128)(2,1)S(1)}, bf16[256,128]{1,0:T(8,128)(2,1)S(1)}, u32[]{:S(2)}, u32[]{:S(2)}) collective-permute-start(bf16[256,128]{1,0:T(8,128)(2,1)S(1)} %get-tuple-element.40), channel_id=1, source_target_pairs={{0,3},{1,2},{2,1},{3,0},{4,7},{5,6},{6,5},{7,4},{8,11},{9,10},{10,... | collective-permute-start | bytes 196616 | tf_op jit(solution)/shard_map/ppermute | solution.py:433
  13.8 0.8 %collective-permute-start.3 = (bf16[256,128]{1,0:T(8,128)(2,1)S(1)}, bf16[256,128]{1,0:T(8,128)(2,1)S(1)}, u32[]{:S(2)}, u32[]{:S(2)}) collective-permute-start(bf16[256,128]{1,0:T(8,128)(2,1)S(1)} %get-tuple-element.41), channel_id=1, source_target_pairs={{0,2},{1,3},{2,0},{3,1},{4,6},{5,7},{6,4},{7,5},{8,10},{9,11},{10,... | collective-permute-start | bytes 196616 | tf_op jit(solution)/shard_map/ppermute | solution.py:433
  14.6 0.1 collective-permute-done.5.refs_1_
  14.7 2.3 %collective-permute-start.4 = (bf16[256,128]{1,0:T(8,128)(2,1)S(1)}, bf16[256,128]{1,0:T(8,128)(2,1)S(1)}, u32[]{:S(2)}, u32[]{:S(2)}) collective-permute-start(bf16[256,128]{1,0:T(8,128)(2,1)S(1)} %get-tuple-element.42), channel_id=1, source_target_pairs={{0,1},{1,0},{2,3},{3,2},{4,5},{5,4},{6,7},{7,6},{8,9},{9,8},{10,11... | collective-permute-start | bytes 196616 | tf_op jit(solution)/shard_map/ppermute | solution.py:433
  17.0 2.0 %collective-permute-done.6.refs_2_ = bf16[3,256,128]{2,1,0:T(8,128)(2,1)S(1)} collective-permute-done((bf16[3,256,128]{2,1,0:T(8,128)(2,1)S(1)}, bf16[3,256,128]{2,1,0:T(8,128)(2,1)S(1)}, u32[]{:S(2)}, u32[]{:S(2)}) %collective-permute-start.6) | collective-permute-done | bytes 196640 | tf_op jit(solution)/shard_map/ppermute | solution.py:433
  19.0 0.7 %collective-permute-done.7.refs_3_ = bf16[3,256,128]{2,1,0:T(8,128)(2,1)S(1)} collective-permute-done((bf16[3,256,128]{2,1,0:T(8,128)(2,1)S(1)}, bf16[3,256,128]{2,1,0:T(8,128)(2,1)S(1)}, u32[]{:S(2)}, u32[]{:S(2)}) %collective-permute-start.7) | collective-permute-done | bytes 196640 | tf_op jit(solution)/shard_map/ppermute | solution.py:433
  19.7 0.1 combine.1
  19.8 3.4 %collective-permute-start.8 = (bf16[256,128]{1,0:T(8,128)(2,1)S(1)}, bf16[256,128]{1,0:T(8,128)(2,1)S(1)}, u32[]{:S(2)}, u32[]{:S(2)}) collective-permute-start(bf16[256,128]{1,0:T(8,128)(2,1)S(1)} %get-tuple-element.47), channel_id=1, source_target_pairs={{0,12},{1,13},{2,14},{3,15},{4,8},{5,9},{6,10},{7,11},{8,4},{9,5},... | collective-permute-start | bytes 196616 | tf_op jit(solution)/shard_map/ppermute | solution.py:439
  23.2 0.0 collective-permute-start.9
  23.2 0.0 collective-permute-done.2.refs_1_
  23.2 1.0 %collective-permute-start.10 = (bf16[256,128]{1,0:T(8,128)(2,1)S(1)}, bf16[256,128]{1,0:T(8,128)(2,1)S(1)}, u32[]{:S(2)}, u32[]{:S(2)}) collective-permute-start(bf16[256,128]{1,0:T(8,128)(2,1)S(1)} %get-tuple-element.49), channel_id=1, source_target_pairs={{0,4},{1,5},{2,6},{3,7},{4,0},{5,1},{6,2},{7,3},{8,12},{9,13},{10,... | collective-permute-start | bytes 196616 | tf_op jit(solution)/shard_map/ppermute | solution.py:439
  24.2 0.0 collective-permute-done.3.refs_2_
  24.3 0.0 collective-permute-done.4.refs_3_
  24.3 2.4 %collective-permute-done.8.refs_4_ = bf16[256,128]{1,0:T(8,128)(2,1)S(1)} collective-permute-done((bf16[256,128]{1,0:T(8,128)(2,1)S(1)}, bf16[256,128]{1,0:T(8,128)(2,1)S(1)}, u32[]{:S(2)}, u32[]{:S(2)}) %collective-permute-start.8) | collective-permute-done | bytes 65568 | tf_op jit(solution)/shard_map/ppermute | solution.py:439
  26.7 2.1 %collective-permute-done.9.refs_5_ = bf16[256,128]{1,0:T(8,128)(2,1)S(1)} collective-permute-done((bf16[256,128]{1,0:T(8,128)(2,1)S(1)}, bf16[256,128]{1,0:T(8,128)(2,1)S(1)}, u32[]{:S(2)}, u32[]{:S(2)}) %collective-permute-start.9) | collective-permute-done | bytes 65568 | tf_op jit(solution)/shard_map/ppermute | solution.py:439
  28.8 0.0 collective-permute-done.10.refs_6_
  28.8 0.0 copy-done
  28.9 0.0 copy-done.4
  28.9 0.6 %layer.1 = (bf16[128,256]{1,0:T(8,128)(2,1)S(1)}, f32[256,128]{1,0:T(8,128)S(1)}, f32[256,256]{1,0:T(8,128)S(1)}, f32[256,256]{1,0:T(8,128)S(1)}) custom-call(f32[256,128]{1,0:T(8,128)S(1)} %get-tuple-element.39.refs_0_, bf16[256,128]{1,0:T(8,128)(2,1)S(1)} %collective-permute-done.2.refs_1_, bf16[256,128]{1,0:T(8,128)(2,1)S(1)} %collective-permute-done.3.refs_2_, ...), custom_call_target="tpu_custom_call" | custom-call | tf_op jit(solution)/shard_map/layer/pallas_call | solution.py:228
  29.5 0.3 weight_terms.1
  29.8 0.1 collective-permute-start.14
  29.9 2.7 %collective-permute-start.13 = (bf16[128,256]{1,0:T(8,128)(2,1)S(1)}, bf16[128,256]{1,0:T(8,128)(2,1)S(1)}, u32[]{:S(2)}, u32[]{:S(2)}) collective-permute-start(bf16[128,256]{1,0:T(8,128)(2,1)S(1)} %get-tuple-element.51.outgoing_ref), channel_id=1, source_target_pairs={{0,12},{1,13},{2,14},{3,15},{4,8},{5,9},{6,10},{7,11},{8,4},{9,5},... | collective-permute-start | bytes 196616 | tf_op jit(solution)/shard_map/ppermute | solution.py:439
  32.5 0.0 collective-permute-done.14.refs_1_
  32.6 2.2 %collective-permute-start.17 = (bf16[208,256]{1,0:T(8,128)(2,1)S(1)}, bf16[208,256]{1,0:T(8,128)(2,1)S(1)}, u32[]{:S(2)}, u32[]{:S(2)}) collective-permute-start(bf16[208,256]{1,0:T(8,128)(2,1)S(1)} %pack.1.refs_0_), channel_id=1, source_target_pairs={{0,3},{1,2},{2,1},{3,0},{4,7},{5,6},{6,5},{7,4},{8,11},{9,10},{10,... | collective-permute-start | bytes 319496 | tf_op jit(solution)/shard_map/ppermute | solution.py:433
  34.7 0.8 %collective-permute-start.16 = (bf16[208,256]{1,0:T(8,128)(2,1)S(1)}, bf16[208,256]{1,0:T(8,128)(2,1)S(1)}, u32[]{:S(2)}, u32[]{:S(2)}) collective-permute-start(bf16[208,256]{1,0:T(8,128)(2,1)S(1)} %pack.1.refs_0_), channel_id=1, source_target_pairs={{0,2},{1,3},{2,0},{3,1},{4,6},{5,7},{6,4},{7,5},{8,10},{9,11},{10,... | collective-permute-start | bytes 319496 | tf_op jit(solution)/shard_map/ppermute | solution.py:433
  35.6 0.5 collective-permute-start.15
  36.1 0.2 collective-permute-start.12
  36.3 0.0 collective-permute-done.13.refs_2_
  36.3 1.6 %collective-permute-start.11 = (bf16[128,256]{1,0:T(8,128)(2,1)S(1)}, bf16[128,256]{1,0:T(8,128)(2,1)S(1)}, u32[]{:S(2)}, u32[]{:S(2)}) collective-permute-start(bf16[128,256]{1,0:T(8,128)(2,1)S(1)} %get-tuple-element.51.outgoing_ref), channel_id=1, source_target_pairs={{0,4},{1,5},{2,6},{3,7},{4,0},{5,1},{6,2},{7,3},{8,12},{9,13},{10,... | collective-permute-start | bytes 196616 | tf_op jit(solution)/shard_map/ppermute | solution.py:439
  37.9 3.4 %collective-permute-done.12.refs_1_ = bf16[128,256]{1,0:T(8,128)(2,1)S(1)} collective-permute-done((bf16[128,256]{1,0:T(8,128)(2,1)S(1)}, bf16[128,256]{1,0:T(8,128)(2,1)S(1)}, u32[]{:S(2)}, u32[]{:S(2)}) %collective-permute-start.12) | collective-permute-done | bytes 65568 | tf_op jit(solution)/shard_map/ppermute | solution.py:439
  41.3 0.0 collective-permute-done.11.refs_0_
  41.3 0.0 collective-permute-done.17.refs_1_.refs_3_
  41.3 0.0 collective-permute-done.16.refs_2_.refs_0_
  41.3 0.0 collective-permute-done.15.refs_1_
  41.3 2.3 %collective-permute-start.20 = (bf16[3,128,256]{2,1,0:T(8,128)(2,1)S(1)}, bf16[3,128,256]{2,1,0:T(8,128)(2,1)S(1)}, u32[]{:S(2)}, u32[]{:S(2)}) collective-permute-start(bf16[3,128,256]{2,1,0:T(8,128)(2,1)S(1)} %stack_line.1.refs_2_), channel_id=1, source_target_pairs={{0,3},{1,2},{2,1},{3,0},{4,7},{5,6},{6,5},{7,4},{8,11},{9,10},{10,... | collective-permute-start | bytes 589832 | tf_op jit(solution)/shard_map/ppermute | solution.py:433
  43.7 0.7 %collective-permute-start.19 = (bf16[3,128,256]{2,1,0:T(8,128)(2,1)S(1)}, bf16[3,128,256]{2,1,0:T(8,128)(2,1)S(1)}, u32[]{:S(2)}, u32[]{:S(2)}) collective-permute-start(bf16[3,128,256]{2,1,0:T(8,128)(2,1)S(1)} %stack_line.1.refs_2_), channel_id=1, source_target_pairs={{0,1},{1,0},{2,3},{3,2},{4,5},{5,4},{6,7},{7,6},{8,9},{9,8},{10,11... | collective-permute-start | bytes 589832 | tf_op jit(solution)/shard_map/ppermute | solution.py:433
  44.4 0.5 collective-permute-start.18
  44.9 2.4 %collective-permute-start.23 = (bf16[80,256]{1,0:T(8,128)(2,1)S(1)}, bf16[80,256]{1,0:T(8,128)(2,1)S(1)}, u32[]{:S(2)}, u32[]{:S(2)}) collective-permute-start(bf16[80,256]{1,0:T(8,128)(2,1)S(1)} %sum_terms.1.refs_6_), channel_id=1, source_target_pairs={{0,12},{1,13},{2,14},{3,15},{4,8},{5,9},{6,10},{7,11},{8,4},{9,5},... | collective-permute-start | bytes 122888 | tf_op jit(solution)/shard_map/ppermute | solution.py:439
  47.3 0.0 collective-permute-start.22
  47.3 2.8 %collective-permute-done.20.refs_3_ = bf16[3,128,256]{2,1,0:T(8,128)(2,1)S(1)} collective-permute-done((bf16[3,128,256]{2,1,0:T(8,128)(2,1)S(1)}, bf16[3,128,256]{2,1,0:T(8,128)(2,1)S(1)}, u32[]{:S(2)}, u32[]{:S(2)}) %collective-permute-start.20) | collective-permute-done | bytes 196640 | tf_op jit(solution)/shard_map/ppermute | solution.py:433
  50.1 0.6 %collective-permute-start.21 = (bf16[80,256]{1,0:T(8,128)(2,1)S(1)}, bf16[80,256]{1,0:T(8,128)(2,1)S(1)}, u32[]{:S(2)}, u32[]{:S(2)}) collective-permute-start(bf16[80,256]{1,0:T(8,128)(2,1)S(1)} %sum_terms.1.refs_6_), channel_id=1, source_target_pairs={{0,4},{1,5},{2,6},{3,7},{4,0},{5,1},{6,2},{7,3},{8,12},{9,13},{10,... | collective-permute-start | bytes 122888 | tf_op jit(solution)/shard_map/ppermute | solution.py:439
  50.7 0.4 backward_product.2
  51.1 0.0 collective-permute-done.23.refs_9_
  51.2 1.2 %collective-permute-done.22.refs_8_ = bf16[80,256]{1,0:T(8,128)(2,1)S(1)} collective-permute-done((bf16[80,256]{1,0:T(8,128)(2,1)S(1)}, bf16[80,256]{1,0:T(8,128)(2,1)S(1)}, u32[]{:S(2)}, u32[]{:S(2)}) %collective-permute-start.22) | collective-permute-done | bytes 40992 | tf_op jit(solution)/shard_map/ppermute | solution.py:439
  52.3 1.8 %collective-permute-done.21.refs_7_ = bf16[80,256]{1,0:T(8,128)(2,1)S(1)} collective-permute-done((bf16[80,256]{1,0:T(8,128)(2,1)S(1)}, bf16[80,256]{1,0:T(8,128)(2,1)S(1)}, u32[]{:S(2)}, u32[]{:S(2)}) %collective-permute-start.21) | collective-permute-done | bytes 40992 | tf_op jit(solution)/shard_map/ppermute | solution.py:439
  54.1 0.0 collective-permute-done.19.refs_3_
  54.1 0.0 collective-permute-done.18.refs_2_
  54.1 0.4 backward_product.3
  54.6 0.1 collective-permute-start.24
  54.7 0.7 %activations.1 = bf16[256,256]{1,0:T(8,128)(2,1)} custom-call(f32[256,256]{1,0:T(8,128)S(1)} %get-tuple-element.50.preact_ref), custom_call_target="tpu_custom_call" | custom-call | tf_op jit(solution)/shard_map/activations/pallas_call | solution.py:247
  55.4 0.6 collective-permute-done.24.refs_0_
  56.0 0.7 %finish.1 = (bf16[256,128]{1,0:T(8,128)(2,1)}, f32[128,256]{1,0:T(8,128)}, f32[1,256]{1,0:T(1,128)}) custom-call(s32[1,256]{1,0:T(1,128)S(1)} %bitcast.13, f32[128,256]{1,0:T(8,128)S(1)} %get-tuple-element.65.own_ref, bf16[208,256]{1,0:T(8,128)(2,1)S(1)} %get-tuple-element.66.sent_ref, bf16[208,256]{1,0:T(8,128)(2,1)S(1)} %collective-permute-done.24.refs_0_), custom_call_target="tpu_custom_call" | custom-call | tf_op jit(solution)/shard_map/finish/pallas_call | solution.py:395
  (10 shorter events, 0.1 us)
Async XLA Ops:
  0.6 3.9 %collective-permute-start.1 = (bf16[256,128]{1,0:T(8,128)(2,1)}, bf16[256,128]{1,0:T(8,128)(2,1)S(1)}, u32[]{:S(2)}, u32[]{:S(2)}) collective-permute-start(bf16[256,128]{1,0:T(8,128)(2,1)} %refs_2_.1), channel_id=1, source_target_pairs={{0,16},{16,0},{1,17},{17,1},{2,18},{18,2},{3,19},{19,3},{4,20},{20... | collective-permute-start | bytes 196616 | tf_op jit(solution)/shard_map/ppermute | solution.py:427
  1.1 3.3 %collective-permute-start = (s32[256]{0:T(256)}, s32[256]{0:T(256)S(1)}, u32[]{:S(2)}, u32[]{:S(2)}) collective-permute-start(s32[256]{0:T(256)} %param.12), channel_id=1, source_target_pairs={{0,16},{16,0},{1,17},{17,1},{2,18},{18,2},{3,19},{19,3},{4,20},{20... | collective-permute-start | bytes 3080 | tf_op jit(solution)/shard_map/ppermute | solution.py:427
  1.9 2.6 %copy-start.1 = (bf16[256,128]{1,0:T(8,128)(2,1)S(1)}, bf16[256,128]{1,0:T(8,128)(2,1)}, u32[]{:S(2)}) copy-start(bf16[256,128]{1,0:T(8,128)(2,1)} %refs_2_.1) | copy-start | bytes 196612
  1.9 2.6 %copy-start.3 = (s32[256]{0:T(256)S(1)}, s32[256]{0:T(256)}, u32[]{:S(2)}) copy-start(s32[256]{0:T(256)} %param.12) | copy-start | bytes 3076
  5.0 9.6 %collective-permute-start.5 = (bf16[3,256,128]{2,1,0:T(8,128)(2,1)S(1)}, bf16[3,256,128]{2,1,0:T(8,128)(2,1)S(1)}, u32[]{:S(2)}, u32[]{:S(2)}) collective-permute-start(bf16[3,256,128]{2,1,0:T(8,128)(2,1)S(1)} %get-tuple-element.44), channel_id=1, source_target_pairs={{0,3},{1,2},{2,1},{3,0},{4,7},{5,6},{6,5},{7,4},{8,11},{9,10},{10,... | collective-permute-start | bytes 589832 | tf_op jit(solution)/shard_map/ppermute | solution.py:433
  9.0 19.9 %copy-start = (bf16[256,256]{1,0:T(8,128)(2,1)S(1)}, bf16[256,256]{1,0:T(8,128)(2,1)}, u32[]{:S(2)}) copy-start(bf16[256,256]{1,0:T(8,128)(2,1)} %refs_10_.1) | copy-start | bytes 393220
  9.0 19.9 %copy-start.2 = (bf16[128,256]{1,0:T(8,128)(2,1)S(1)}, bf16[128,256]{1,0:T(8,128)(2,1)}, u32[]{:S(2)}) copy-start(bf16[128,256]{1,0:T(8,128)(2,1)} %refs_8_.1) | copy-start | bytes 196612
  9.0 19.9 %copy-start.4 = (f32[256]{0:T(256)S(1)}, f32[256]{0:T(256)}, u32[]{:S(2)}) copy-start(f32[256]{0:T(256)} %param.10) | copy-start | bytes 3076
  9.5 9.4 %collective-permute-start.6 = (bf16[3,256,128]{2,1,0:T(8,128)(2,1)S(1)}, bf16[3,256,128]{2,1,0:T(8,128)(2,1)S(1)}, u32[]{:S(2)}, u32[]{:S(2)}) collective-permute-start(bf16[3,256,128]{2,1,0:T(8,128)(2,1)S(1)} %get-tuple-element.45), channel_id=1, source_target_pairs={{0,2},{1,3},{2,0},{3,1},{4,6},{5,7},{6,4},{7,5},{8,10},{9,11},{10,... | collective-permute-start | bytes 589832 | tf_op jit(solution)/shard_map/ppermute | solution.py:433
  10.4 9.3 %collective-permute-start.7 = (bf16[3,256,128]{2,1,0:T(8,128)(2,1)S(1)}, bf16[3,256,128]{2,1,0:T(8,128)(2,1)S(1)}, u32[]{:S(2)}, u32[]{:S(2)}) collective-permute-start(bf16[3,256,128]{2,1,0:T(8,128)(2,1)S(1)} %get-tuple-element.46), channel_id=1, source_target_pairs={{0,1},{1,0},{2,3},{3,2},{4,5},{5,4},{6,7},{7,6},{8,9},{9,8},{10,11... | collective-permute-start | bytes 589832 | tf_op jit(solution)/shard_map/ppermute | solution.py:433
  11.0 12.2 %collective-permute-start.2 = (bf16[256,128]{1,0:T(8,128)(2,1)S(1)}, bf16[256,128]{1,0:T(8,128)(2,1)S(1)}, u32[]{:S(2)}, u32[]{:S(2)}) collective-permute-start(bf16[256,128]{1,0:T(8,128)(2,1)S(1)} %get-tuple-element.40), channel_id=1, source_target_pairs={{0,3},{1,2},{2,1},{3,0},{4,7},{5,6},{6,5},{7,4},{8,11},{9,10},{10,... | collective-permute-start | bytes 196616 | tf_op jit(solution)/shard_map/ppermute | solution.py:433
  13.8 10.5 %collective-permute-start.3 = (bf16[256,128]{1,0:T(8,128)(2,1)S(1)}, bf16[256,128]{1,0:T(8,128)(2,1)S(1)}, u32[]{:S(2)}, u32[]{:S(2)}) collective-permute-start(bf16[256,128]{1,0:T(8,128)(2,1)S(1)} %get-tuple-element.41), channel_id=1, source_target_pairs={{0,2},{1,3},{2,0},{3,1},{4,6},{5,7},{6,4},{7,5},{8,10},{9,11},{10,... | collective-permute-start | bytes 196616 | tf_op jit(solution)/shard_map/ppermute | solution.py:433
  14.7 9.6 %collective-permute-start.4 = (bf16[256,128]{1,0:T(8,128)(2,1)S(1)}, bf16[256,128]{1,0:T(8,128)(2,1)S(1)}, u32[]{:S(2)}, u32[]{:S(2)}) collective-permute-start(bf16[256,128]{1,0:T(8,128)(2,1)S(1)} %get-tuple-element.42), channel_id=1, source_target_pairs={{0,1},{1,0},{2,3},{3,2},{4,5},{5,4},{6,7},{7,6},{8,9},{9,8},{10,11... | collective-permute-start | bytes 196616 | tf_op jit(solution)/shard_map/ppermute | solution.py:433
  19.8 6.9 %collective-permute-start.8 = (bf16[256,128]{1,0:T(8,128)(2,1)S(1)}, bf16[256,128]{1,0:T(8,128)(2,1)S(1)}, u32[]{:S(2)}, u32[]{:S(2)}) collective-permute-start(bf16[256,128]{1,0:T(8,128)(2,1)S(1)} %get-tuple-element.47), channel_id=1, source_target_pairs={{0,12},{1,13},{2,14},{3,15},{4,8},{5,9},{6,10},{7,11},{8,4},{9,5},... | collective-permute-start | bytes 196616 | tf_op jit(solution)/shard_map/ppermute | solution.py:439
  23.2 5.6 %collective-permute-start.9 = (bf16[256,128]{1,0:T(8,128)(2,1)S(1)}, bf16[256,128]{1,0:T(8,128)(2,1)S(1)}, u32[]{:S(2)}, u32[]{:S(2)}) collective-permute-start(bf16[256,128]{1,0:T(8,128)(2,1)S(1)} %get-tuple-element.48), channel_id=1, source_target_pairs={{0,8},{1,9},{2,10},{3,11},{4,12},{5,13},{6,14},{7,15},{8,0},{9,1},... | collective-permute-start | bytes 196616 | tf_op jit(solution)/shard_map/ppermute | solution.py:439
  23.2 5.6 %collective-permute-start.10 = (bf16[256,128]{1,0:T(8,128)(2,1)S(1)}, bf16[256,128]{1,0:T(8,128)(2,1)S(1)}, u32[]{:S(2)}, u32[]{:S(2)}) collective-permute-start(bf16[256,128]{1,0:T(8,128)(2,1)S(1)} %get-tuple-element.49), channel_id=1, source_target_pairs={{0,4},{1,5},{2,6},{3,7},{4,0},{5,1},{6,2},{7,3},{8,12},{9,13},{10,... | collective-permute-start | bytes 196616 | tf_op jit(solution)/shard_map/ppermute | solution.py:439
  29.8 2.8 %collective-permute-start.14 = (f32[80,256]{1,0:T(8,128)S(1)}, f32[80,256]{1,0:T(8,128)S(1)}, u32[]{:S(2)}, u32[]{:S(2)}) collective-permute-start(f32[80,256]{1,0:T(8,128)S(1)} %get-tuple-element.55), channel_id=1, source_target_pairs={{0,16},{16,0},{1,17},{17,1},{2,18},{18,2},{3,19},{19,3},{4,20},{20... | collective-permute-start | bytes 245768 | tf_op jit(solution)/shard_map/ppermute | solution.py:427
  29.9 6.4 %collective-permute-start.13 = (bf16[128,256]{1,0:T(8,128)(2,1)S(1)}, bf16[128,256]{1,0:T(8,128)(2,1)S(1)}, u32[]{:S(2)}, u32[]{:S(2)}) collective-permute-start(bf16[128,256]{1,0:T(8,128)(2,1)S(1)} %get-tuple-element.51.outgoing_ref), channel_id=1, source_target_pairs={{0,12},{1,13},{2,14},{3,15},{4,8},{5,9},{6,10},{7,11},{8,4},{9,5},... | collective-permute-start | bytes 196616 | tf_op jit(solution)/shard_map/ppermute | solution.py:439
  32.6 8.7 %collective-permute-start.17 = (bf16[208,256]{1,0:T(8,128)(2,1)S(1)}, bf16[208,256]{1,0:T(8,128)(2,1)S(1)}, u32[]{:S(2)}, u32[]{:S(2)}) collective-permute-start(bf16[208,256]{1,0:T(8,128)(2,1)S(1)} %pack.1.refs_0_), channel_id=1, source_target_pairs={{0,3},{1,2},{2,1},{3,0},{4,7},{5,6},{6,5},{7,4},{8,11},{9,10},{10,... | collective-permute-start | bytes 319496 | tf_op jit(solution)/shard_map/ppermute | solution.py:433
  34.7 6.5 %collective-permute-start.16 = (bf16[208,256]{1,0:T(8,128)(2,1)S(1)}, bf16[208,256]{1,0:T(8,128)(2,1)S(1)}, u32[]{:S(2)}, u32[]{:S(2)}) collective-permute-start(bf16[208,256]{1,0:T(8,128)(2,1)S(1)} %pack.1.refs_0_), channel_id=1, source_target_pairs={{0,2},{1,3},{2,0},{3,1},{4,6},{5,7},{6,4},{7,5},{8,10},{9,11},{10,... | collective-permute-start | bytes 319496 | tf_op jit(solution)/shard_map/ppermute | solution.py:433
  35.6 5.7 %collective-permute-start.15 = (bf16[208,256]{1,0:T(8,128)(2,1)S(1)}, bf16[208,256]{1,0:T(8,128)(2,1)S(1)}, u32[]{:S(2)}, u32[]{:S(2)}) collective-permute-start(bf16[208,256]{1,0:T(8,128)(2,1)S(1)} %pack.1.refs_0_), channel_id=1, source_target_pairs={{0,1},{1,0},{2,3},{3,2},{4,5},{5,4},{6,7},{7,6},{8,9},{9,8},{10,11... | collective-permute-start | bytes 319496 | tf_op jit(solution)/shard_map/ppermute | solution.py:433
  36.1 5.2 %collective-permute-start.12 = (bf16[128,256]{1,0:T(8,128)(2,1)S(1)}, bf16[128,256]{1,0:T(8,128)(2,1)S(1)}, u32[]{:S(2)}, u32[]{:S(2)}) collective-permute-start(bf16[128,256]{1,0:T(8,128)(2,1)S(1)} %get-tuple-element.51.outgoing_ref), channel_id=1, source_target_pairs={{0,8},{1,9},{2,10},{3,11},{4,12},{5,13},{6,14},{7,15},{8,0},{9,1},... | collective-permute-start | bytes 196616 | tf_op jit(solution)/shard_map/ppermute | solution.py:439
  36.3 5.0 %collective-permute-start.11 = (bf16[128,256]{1,0:T(8,128)(2,1)S(1)}, bf16[128,256]{1,0:T(8,128)(2,1)S(1)}, u32[]{:S(2)}, u32[]{:S(2)}) collective-permute-start(bf16[128,256]{1,0:T(8,128)(2,1)S(1)} %get-tuple-element.51.outgoing_ref), channel_id=1, source_target_pairs={{0,4},{1,5},{2,6},{3,7},{4,0},{5,1},{6,2},{7,3},{8,12},{9,13},{10,... | collective-permute-start | bytes 196616 | tf_op jit(solution)/shard_map/ppermute | solution.py:439
  41.3 8.8 %collective-permute-start.20 = (bf16[3,128,256]{2,1,0:T(8,128)(2,1)S(1)}, bf16[3,128,256]{2,1,0:T(8,128)(2,1)S(1)}, u32[]{:S(2)}, u32[]{:S(2)}) collective-permute-start(bf16[3,128,256]{2,1,0:T(8,128)(2,1)S(1)} %stack_line.1.refs_2_), channel_id=1, source_target_pairs={{0,3},{1,2},{2,1},{3,0},{4,7},{5,6},{6,5},{7,4},{8,11},{9,10},{10,... | collective-permute-start | bytes 589832 | tf_op jit(solution)/shard_map/ppermute | solution.py:433
  43.7 10.5 %collective-permute-start.19 = (bf16[3,128,256]{2,1,0:T(8,128)(2,1)S(1)}, bf16[3,128,256]{2,1,0:T(8,128)(2,1)S(1)}, u32[]{:S(2)}, u32[]{:S(2)}) collective-permute-start(bf16[3,128,256]{2,1,0:T(8,128)(2,1)S(1)} %stack_line.1.refs_2_), channel_id=1, source_target_pairs={{0,1},{1,0},{2,3},{3,2},{4,5},{5,4},{6,7},{7,6},{8,9},{9,8},{10,11... | collective-permute-start | bytes 589832 | tf_op jit(solution)/shard_map/ppermute | solution.py:433
  44.4 9.8 %collective-permute-start.18 = (bf16[3,128,256]{2,1,0:T(8,128)(2,1)S(1)}, bf16[3,128,256]{2,1,0:T(8,128)(2,1)S(1)}, u32[]{:S(2)}, u32[]{:S(2)}) collective-permute-start(bf16[3,128,256]{2,1,0:T(8,128)(2,1)S(1)} %stack_line.1.refs_2_), channel_id=1, source_target_pairs={{0,2},{1,3},{2,0},{3,1},{4,6},{5,7},{6,4},{7,5},{8,10},{9,11},{10,... | collective-permute-start | bytes 589832 | tf_op jit(solution)/shard_map/ppermute | solution.py:433
  44.9 6.2 %collective-permute-start.23 = (bf16[80,256]{1,0:T(8,128)(2,1)S(1)}, bf16[80,256]{1,0:T(8,128)(2,1)S(1)}, u32[]{:S(2)}, u32[]{:S(2)}) collective-permute-start(bf16[80,256]{1,0:T(8,128)(2,1)S(1)} %sum_terms.1.refs_6_), channel_id=1, source_target_pairs={{0,12},{1,13},{2,14},{3,15},{4,8},{5,9},{6,10},{7,11},{8,4},{9,5},... | collective-permute-start | bytes 122888 | tf_op jit(solution)/shard_map/ppermute | solution.py:439
  47.3 5.0 %collective-permute-start.22 = (bf16[80,256]{1,0:T(8,128)(2,1)S(1)}, bf16[80,256]{1,0:T(8,128)(2,1)S(1)}, u32[]{:S(2)}, u32[]{:S(2)}) collective-permute-start(bf16[80,256]{1,0:T(8,128)(2,1)S(1)} %sum_terms.1.refs_6_), channel_id=1, source_target_pairs={{0,8},{1,9},{2,10},{3,11},{4,12},{5,13},{6,14},{7,15},{8,0},{9,1},... | collective-permute-start | bytes 122888 | tf_op jit(solution)/shard_map/ppermute | solution.py:439
  50.1 4.0 %collective-permute-start.21 = (bf16[80,256]{1,0:T(8,128)(2,1)S(1)}, bf16[80,256]{1,0:T(8,128)(2,1)S(1)}, u32[]{:S(2)}, u32[]{:S(2)}) collective-permute-start(bf16[80,256]{1,0:T(8,128)(2,1)S(1)} %sum_terms.1.refs_6_), channel_id=1, source_target_pairs={{0,4},{1,5},{2,6},{3,7},{4,0},{5,1},{6,2},{7,3},{8,12},{9,13},{10,... | collective-permute-start | bytes 122888 | tf_op jit(solution)/shard_map/ppermute | solution.py:439
  54.6 1.4 %collective-permute-start.24 = (bf16[208,256]{1,0:T(8,128)(2,1)S(1)}, bf16[208,256]{1,0:T(8,128)(2,1)S(1)}, u32[]{:S(2)}, u32[]{:S(2)}) collective-permute-start(bf16[208,256]{1,0:T(8,128)(2,1)S(1)} %get-tuple-element.66.sent_ref), channel_id=1, source_target_pairs={{0,16},{16,0},{1,17},{17,1},{2,18},{18,2},{3,19},{19,3},{4,20},{20... | collective-permute-start | bytes 319496 | tf_op jit(solution)/shard_map/ppermute | solution.py:427

commit v4 on v3

--- a/solution.py
+++ b/solution.py
@@ -449,10 +449,12 @@
     products, scaled = forward(dense, inputs, ((low - 1, True),), scaling=True)
     far_ones = tuple((step, True) for step in far_first(low - 1))
     rest = ((0, True),) + tuple((step, False) for step in (*far_first(low), 0))
-    for wanted in (far_ones, rest):
-        if wanted:
-            products |= forward(dense, scaled, wanted)[0]
-    onward = [products[0, True]] + [over_plane(products[step, True], step) for step in far_first(low)]
+    if far_ones:
+        products |= forward(dense, scaled, far_ones)[0]
+    onward = [over_plane(products[step, True], step) for step in far_first(low)]
+    scaled, onward[:1] = lax.optimization_barrier((scaled, onward[:1]))
+    products |= forward(dense, scaled, rest)[0]
+    onward = [products[0, True]] + onward
     here = [products[0, False]] + [over_plane(products[step, False], step) for step in far_first(low)]
     chunks = combine(onward)
     shares = [over_line(chunks[hop - 1], hop) for hop in far_first(high)]
@@ -463,7 +465,6 @@
     activations = activations_of(preact)
     parcel = pack(outgoing, [pieces[0]] + [over_row(pieces[step], step) for step in range(1, rows)])
     parcels = {0: parcel} | {step: over_plane(parcel, step) for step in far_first(low)}
-    line, parcels = lax.optimization_barrier((line, parcels))
     stacked = stack_line(line)
     stacks = {0: stacked} | {step: over_plane(stacked, step) for step in far_first(low)}
     terms = sum_terms([parcels[step] for step in range(low)], weight.shape[0])

time: 57 us -> 63.8 us (1.12)
  waiting for transfers between devices: 17.2 us -> 22.8 us
  starting transfers between devices: 30.4 us -> 31.5 us
    ppermute x12, waiting for transfers between devices: 5.66 us -> 12.7 us  [over_plane(): return lax.ppermute(values, 'col', pairs)]
    ppermute x9, starting transfers between devices: 11.9 us -> 13.4 us  [over_line(): return lax.ppermute(values, 'col', pairs)]
    ppermute x9, waiting for transfers between devices: 11 us -> 9.52 us  [over_line(): return lax.ppermute(values, 'col', pairs)]
  transfers between devices with their start and end apart: 25 -> 25, of which waited for: 10 -> 9; matrix products, arithmetic and copies ran while one was open for 0% -> 0% of each run, Pallas kernels for 9% -> 8%
where the time goes in v4:
time: 63.8 us; the launch traced here: 63.4 us
  starting transfers between devices  31.5 us (49%)
  waiting for transfers between devices  22.8 us (36%)
  Pallas kernels  7.66 us (12%)
  between operations  1.45 us (2%)
    ppermute x12, starting transfers between devices, over_plane(): return lax.ppermute(values, 'col', pairs)  17.4 us
    ppermute x9, starting transfers between devices, over_line(): return lax.ppermute(values, 'col', pairs)  13.4 us
    ppermute x12, waiting for transfers between devices, over_plane(): return lax.ppermute(values, 'col', pairs)  12.7 us
    ppermute x9, waiting for transfers between devices, over_line(): return lax.ppermute(values, 'col', pairs)  9.52 us
    pallas_call x1, Pallas kernels, densify(): pl.pallas_call(functools.partial(densify_kernel, col_slots), out_shape=ja...  2.53 us
    pallas_call x3, Pallas kernels, forward(): pl.pallas_call(functools.partial(forward_kernel, wanted, pieces, scaling)...  1.69 us
  transfers between devices with their start and end apart: 25, of which 9 were waited for; matrix products, arithmetic and copies ran while one was open for 0% of the time, Pallas kernels for 8%

profile of v4, /device:TPU:0, one launch (start us, length us, event | category | flops | bytes accessed | tf_op | source)
XLA Modules:
  0.0 63.4 jit_solution(1245658472992889834)
XLA Ops:
  0.6 0.5 collective-permute-start.1
  1.1 0.1 collective-permute-start
  1.9 0.0 copy-start.1
  1.9 0.0 copy-start.3
  1.9 2.5 %densify.1 = bf16[32,128,512]{2,1,0:T(8,128)(2,1)S(1)} custom-call(s32[1,1,128]{2,1,0:T(1,128)} %positions_hbm.1, s32[1,1]{1,0:T(1,128)S(6)} %copy.12.counts_ref, bf16[128,128,128]{2,1,0:T(8,128)(2,1)} %bitcast.16), custom_call_target="tpu_custom_call" | custom-call | tf_op jit(solution)/shard_map/densify/pallas_call | solution.py:107
  4.4 0.0 collective-permute-done
  4.4 0.0 collective-permute-done.1.refs_3_
  4.5 0.5 forward_product.3
  5.0 4.0 %collective-permute-start.2 = (bf16[3,256,128]{2,1,0:T(8,128)(2,1)S(1)}, bf16[3,256,128]{2,1,0:T(8,128)(2,1)S(1)}, u32[]{:S(2)}, u32[]{:S(2)}) collective-permute-start(bf16[3,256,128]{2,1,0:T(8,128)(2,1)S(1)} %get-tuple-element.35), channel_id=1, source_target_pairs={{0,3},{1,2},{2,1},{3,0},{4,7},{5,6},{6,5},{7,4},{8,11},{9,10},{10,... | collective-permute-start | bytes 589832 | tf_op jit(solution)/shard_map/ppermute | solution.py:433
  9.0 0.6 forward_product.5
  9.6 0.5 collective-permute-start.6
  10.1 0.1 collective-permute-start.7
  10.2 4.5 %collective-permute-done.2.refs_1_ = bf16[3,256,128]{2,1,0:T(8,128)(2,1)S(1)} collective-permute-done((bf16[3,256,128]{2,1,0:T(8,128)(2,1)S(1)}, bf16[3,256,128]{2,1,0:T(8,128)(2,1)S(1)}, u32[]{:S(2)}, u32[]{:S(2)}) %collective-permute-start.2) | collective-permute-done | bytes 196640 | tf_op jit(solution)/shard_map/ppermute | solution.py:433
  14.7 0.6 forward_product.4
  15.3 3.1 %collective-permute-start.3 = (bf16[256,128]{1,0:T(8,128)(2,1)S(1)}, bf16[256,128]{1,0:T(8,128)(2,1)S(1)}, u32[]{:S(2)}, u32[]{:S(2)}) collective-permute-start(bf16[256,128]{1,0:T(8,128)(2,1)S(1)} %get-tuple-element.39), channel_id=1, source_target_pairs={{0,3},{1,2},{2,1},{3,0},{4,7},{5,6},{6,5},{7,4},{8,11},{9,10},{10,... | collective-permute-start | bytes 196616 | tf_op jit(solution)/shard_map/ppermute | solution.py:433
  18.4 0.5 collective-permute-start.4
  18.9 0.2 collective-permute-start.5
  19.0 0.0 collective-permute-done.6.refs_2_
  19.0 0.3 collective-permute-done.7.refs_3_
  19.3 0.1 combine.1
  19.4 3.8 %collective-permute-start.8 = (bf16[256,128]{1,0:T(8,128)(2,1)S(1)}, bf16[256,128]{1,0:T(8,128)(2,1)S(1)}, u32[]{:S(2)}, u32[]{:S(2)}) collective-permute-start(bf16[256,128]{1,0:T(8,128)(2,1)S(1)} %get-tuple-element.46), channel_id=1, source_target_pairs={{0,12},{1,13},{2,14},{3,15},{4,8},{5,9},{6,10},{7,11},{8,4},{9,5},... | collective-permute-start | bytes 196616 | tf_op jit(solution)/shard_map/ppermute | solution.py:439
  23.2 0.0 collective-permute-start.9
  23.2 0.0 collective-permute-done.3.refs_1_
  23.2 0.7 %collective-permute-start.10 = (bf16[256,128]{1,0:T(8,128)(2,1)S(1)}, bf16[256,128]{1,0:T(8,128)(2,1)S(1)}, u32[]{:S(2)}, u32[]{:S(2)}) collective-permute-start(bf16[256,128]{1,0:T(8,128)(2,1)S(1)} %get-tuple-element.48), channel_id=1, source_target_pairs={{0,4},{1,5},{2,6},{3,7},{4,0},{5,1},{6,2},{7,3},{8,12},{9,13},{10,... | collective-permute-start | bytes 196616 | tf_op jit(solution)/shard_map/ppermute | solution.py:439
  23.9 0.0 collective-permute-done.4.refs_2_
  23.9 0.0 collective-permute-done.5.refs_3_
  23.9 2.2 %collective-permute-done.8.refs_4_ = bf16[256,128]{1,0:T(8,128)(2,1)S(1)} collective-permute-done((bf16[256,128]{1,0:T(8,128)(2,1)S(1)}, bf16[256,128]{1,0:T(8,128)(2,1)S(1)}, u32[]{:S(2)}, u32[]{:S(2)}) %collective-permute-start.8) | collective-permute-done | bytes 65568 | tf_op jit(solution)/shard_map/ppermute | solution.py:439
  26.0 2.7 %collective-permute-done.9.refs_5_ = bf16[256,128]{1,0:T(8,128)(2,1)S(1)} collective-permute-done((bf16[256,128]{1,0:T(8,128)(2,1)S(1)}, bf16[256,128]{1,0:T(8,128)(2,1)S(1)}, u32[]{:S(2)}, u32[]{:S(2)}) %collective-permute-start.9) | collective-permute-done | bytes 65568 | tf_op jit(solution)/shard_map/ppermute | solution.py:439
  28.7 0.0 collective-permute-done.10.refs_6_
  28.7 0.0 copy-done
  28.7 0.6 layer.1
  29.4 0.3 weight_terms.1
  29.7 0.1 collective-permute-start.11
  29.7 2.7 %collective-permute-start.16 = (bf16[128,256]{1,0:T(8,128)(2,1)S(1)}, bf16[128,256]{1,0:T(8,128)(2,1)S(1)}, u32[]{:S(2)}, u32[]{:S(2)}) collective-permute-start(bf16[128,256]{1,0:T(8,128)(2,1)S(1)} %get-tuple-element.50.outgoing_ref), channel_id=1, source_target_pairs={{0,12},{1,13},{2,14},{3,15},{4,8},{5,9},{6,10},{7,11},{8,4},{9,5},... | collective-permute-start | bytes 196616 | tf_op jit(solution)/shard_map/ppermute | solution.py:439
  32.5 0.0 collective-permute-start.15
  32.5 1.7 %collective-permute-start.14 = (bf16[128,256]{1,0:T(8,128)(2,1)S(1)}, bf16[128,256]{1,0:T(8,128)(2,1)S(1)}, u32[]{:S(2)}, u32[]{:S(2)}) collective-permute-start(bf16[128,256]{1,0:T(8,128)(2,1)S(1)} %get-tuple-element.50.outgoing_ref), channel_id=1, source_target_pairs={{0,4},{1,5},{2,6},{3,7},{4,0},{5,1},{6,2},{7,3},{8,12},{9,13},{10,... | collective-permute-start | bytes 196616 | tf_op jit(solution)/shard_map/ppermute | solution.py:439
  34.2 0.0 collective-permute-done.11.refs_1_
  34.2 2.5 %collective-permute-start.19 = (bf16[208,256]{1,0:T(8,128)(2,1)S(1)}, bf16[208,256]{1,0:T(8,128)(2,1)S(1)}, u32[]{:S(2)}, u32[]{:S(2)}) collective-permute-start(bf16[208,256]{1,0:T(8,128)(2,1)S(1)} %pack.1.refs_0_), channel_id=1, source_target_pairs={{0,3},{1,2},{2,1},{3,0},{4,7},{5,6},{6,5},{7,4},{8,11},{9,10},{10,... | collective-permute-start | bytes 319496 | tf_op jit(solution)/shard_map/ppermute | solution.py:433
  36.7 0.0 collective-permute-done.16.refs_2_
  36.7 2.2 %collective-permute-done.15.refs_1_ = bf16[128,256]{1,0:T(8,128)(2,1)S(1)} collective-permute-done((bf16[128,256]{1,0:T(8,128)(2,1)S(1)}, bf16[128,256]{1,0:T(8,128)(2,1)S(1)}, u32[]{:S(2)}, u32[]{:S(2)}) %collective-permute-start.15) | collective-permute-done | bytes 65568 | tf_op jit(solution)/shard_map/ppermute | solution.py:439
  38.9 0.0 collective-permute-done.14.refs_0_
  38.9 2.5 %collective-permute-start.20 = (bf16[3,128,256]{2,1,0:T(8,128)(2,1)S(1)}, bf16[3,128,256]{2,1,0:T(8,128)(2,1)S(1)}, u32[]{:S(2)}, u32[]{:S(2)}) collective-permute-start(bf16[3,128,256]{2,1,0:T(8,128)(2,1)S(1)} %stack_line.1.refs_2_), channel_id=1, source_target_pairs={{0,3},{1,2},{2,1},{3,0},{4,7},{5,6},{6,5},{7,4},{8,11},{9,10},{10,... | collective-permute-start | bytes 589832 | tf_op jit(solution)/shard_map/ppermute | solution.py:433
  41.4 0.6 collective-permute-start.18
  42.0 0.5 collective-permute-start.17
  42.5 1.7 %collective-permute-start.13 = (bf16[208,256]{1,0:T(8,128)(2,1)S(1)}, bf16[208,256]{1,0:T(8,128)(2,1)S(1)}, u32[]{:S(2)}, u32[]{:S(2)}) collective-permute-start(bf16[208,256]{1,0:T(8,128)(2,1)S(1)} %pack.1.refs_0_), channel_id=1, source_target_pairs={{0,1},{1,0},{2,3},{3,2},{4,5},{5,4},{6,7},{7,6},{8,9},{9,8},{10,11... | collective-permute-start | bytes 319496 | tf_op jit(solution)/shard_map/ppermute | solution.py:433
  44.2 0.0 collective-permute-done.19.refs_1_.refs_3_
  44.2 1.3 %collective-permute-start.12 = (bf16[208,256]{1,0:T(8,128)(2,1)S(1)}, bf16[208,256]{1,0:T(8,128)(2,1)S(1)}, u32[]{:S(2)}, u32[]{:S(2)}) collective-permute-start(bf16[208,256]{1,0:T(8,128)(2,1)S(1)} %pack.1.refs_0_), channel_id=1, source_target_pairs={{0,2},{1,3},{2,0},{3,1},{4,6},{5,7},{6,4},{7,5},{8,10},{9,11},{10,... | collective-permute-start | bytes 319496 | tf_op jit(solution)/shard_map/ppermute | solution.py:433
  45.5 8.0 %collective-permute-done.13.refs_1_ = bf16[208,256]{1,0:T(8,128)(2,1)S(1)} collective-permute-done((bf16[208,256]{1,0:T(8,128)(2,1)S(1)}, bf16[208,256]{1,0:T(8,128)(2,1)S(1)}, u32[]{:S(2)}, u32[]{:S(2)}) %collective-permute-start.13) | collective-permute-done | bytes 106528 | tf_op jit(solution)/shard_map/ppermute | solution.py:433
  53.5 0.0 collective-permute-done.12.refs_2_.refs_0_
  53.5 2.4 %collective-permute-start.23 = (bf16[80,256]{1,0:T(8,128)(2,1)S(1)}, bf16[80,256]{1,0:T(8,128)(2,1)S(1)}, u32[]{:S(2)}, u32[]{:S(2)}) collective-permute-start(bf16[80,256]{1,0:T(8,128)(2,1)S(1)} %sum_terms.1.refs_6_), channel_id=1, source_target_pairs={{0,12},{1,13},{2,14},{3,15},{4,8},{5,9},{6,10},{7,11},{8,4},{9,5},... | collective-permute-start | bytes 122888 | tf_op jit(solution)/shard_map/ppermute | solution.py:439
  55.9 0.0 collective-permute-start.22
  55.9 0.0 collective-permute-done.20.refs_3_
  55.9 2.0 %collective-permute-start.21 = (bf16[80,256]{1,0:T(8,128)(2,1)S(1)}, bf16[80,256]{1,0:T(8,128)(2,1)S(1)}, u32[]{:S(2)}, u32[]{:S(2)}) collective-permute-start(bf16[80,256]{1,0:T(8,128)(2,1)S(1)} %sum_terms.1.refs_6_), channel_id=1, source_target_pairs={{0,4},{1,5},{2,6},{3,7},{4,0},{5,1},{6,2},{7,3},{8,12},{9,13},{10,... | collective-permute-start | bytes 122888 | tf_op jit(solution)/shard_map/ppermute | solution.py:439
  57.9 0.4 backward_product.2
  58.4 1.0 %collective-permute-done.23.refs_9_ = bf16[80,256]{1,0:T(8,128)(2,1)S(1)} collective-permute-done((bf16[80,256]{1,0:T(8,128)(2,1)S(1)}, bf16[80,256]{1,0:T(8,128)(2,1)S(1)}, u32[]{:S(2)}, u32[]{:S(2)}) %collective-permute-start.23) | collective-permute-done | bytes 40992 | tf_op jit(solution)/shard_map/ppermute | solution.py:439
  59.4 1.5 %collective-permute-done.22.refs_8_ = bf16[80,256]{1,0:T(8,128)(2,1)S(1)} collective-permute-done((bf16[80,256]{1,0:T(8,128)(2,1)S(1)}, bf16[80,256]{1,0:T(8,128)(2,1)S(1)}, u32[]{:S(2)}, u32[]{:S(2)}) %collective-permute-start.22) | collective-permute-done | bytes 40992 | tf_op jit(solution)/shard_map/ppermute | solution.py:439
  60.8 0.0 collective-permute-done.21.refs_7_
  60.8 0.0 collective-permute-done.18.refs_3_
  60.8 0.0 collective-permute-done.17.refs_2_
  60.8 0.5 backward_product.3
  61.3 0.1 collective-permute-start.24
  61.4 0.7 %activations.1 = bf16[256,256]{1,0:T(8,128)(2,1)} custom-call(f32[256,256]{1,0:T(8,128)S(1)} %get-tuple-element.49.preact_ref), custom_call_target="tpu_custom_call" | custom-call | tf_op jit(solution)/shard_map/activations/pallas_call | solution.py:247
  62.1 0.6 collective-permute-done.24.refs_0_
  62.7 0.7 %finish.1 = (bf16[256,128]{1,0:T(8,128)(2,1)}, f32[128,256]{1,0:T(8,128)}, f32[1,256]{1,0:T(1,128)}) custom-call(s32[1,256]{1,0:T(1,128)S(1)} %bitcast.13, f32[128,256]{1,0:T(8,128)S(1)} %get-tuple-element.57.own_ref, bf16[208,256]{1,0:T(8,128)(2,1)S(1)} %get-tuple-element.58.sent_ref, bf16[208,256]{1,0:T(8,128)(2,1)S(1)} %collective-permute-done.24.refs_0_), custom_call_target="tpu_custom_call" | custom-call | tf_op jit(solution)/shard_map/finish/pallas_call | solution.py:395
  (10 shorter events, 0.1 us)
Async XLA Ops:
  0.6 3.8 %collective-permute-start.1 = (bf16[256,128]{1,0:T(8,128)(2,1)}, bf16[256,128]{1,0:T(8,128)(2,1)S(1)}, u32[]{:S(2)}, u32[]{:S(2)}) collective-permute-start(bf16[256,128]{1,0:T(8,128)(2,1)} %refs_2_.1), channel_id=1, source_target_pairs={{0,16},{16,0},{1,17},{17,1},{2,18},{18,2},{3,19},{19,3},{4,20},{20... | collective-permute-start | bytes 196616 | tf_op jit(solution)/shard_map/ppermute | solution.py:427
  1.1 3.3 %collective-permute-start = (s32[256]{0:T(256)}, s32[256]{0:T(256)S(1)}, u32[]{:S(2)}, u32[]{:S(2)}) collective-permute-start(s32[256]{0:T(256)} %param.12), channel_id=1, source_target_pairs={{0,16},{16,0},{1,17},{17,1},{2,18},{18,2},{3,19},{19,3},{4,20},{20... | collective-permute-start | bytes 3080 | tf_op jit(solution)/shard_map/ppermute | solution.py:427
  1.9 2.6 %copy-start.1 = (bf16[256,128]{1,0:T(8,128)(2,1)S(1)}, bf16[256,128]{1,0:T(8,128)(2,1)}, u32[]{:S(2)}) copy-start(bf16[256,128]{1,0:T(8,128)(2,1)} %refs_2_.1) | copy-start | bytes 196612
  1.9 2.6 %copy-start.3 = (s32[256]{0:T(256)S(1)}, s32[256]{0:T(256)}, u32[]{:S(2)}) copy-start(s32[256]{0:T(256)} %param.12) | copy-start | bytes 3076
  5.0 9.7 %collective-permute-start.2 = (bf16[3,256,128]{2,1,0:T(8,128)(2,1)S(1)}, bf16[3,256,128]{2,1,0:T(8,128)(2,1)S(1)}, u32[]{:S(2)}, u32[]{:S(2)}) collective-permute-start(bf16[3,256,128]{2,1,0:T(8,128)(2,1)S(1)} %get-tuple-element.35), channel_id=1, source_target_pairs={{0,3},{1,2},{2,1},{3,0},{4,7},{5,6},{6,5},{7,4},{8,11},{9,10},{10,... | collective-permute-start | bytes 589832 | tf_op jit(solution)/shard_map/ppermute | solution.py:433
  9.0 19.7 %copy-start = (bf16[256,256]{1,0:T(8,128)(2,1)S(1)}, bf16[256,256]{1,0:T(8,128)(2,1)}, u32[]{:S(2)}) copy-start(bf16[256,256]{1,0:T(8,128)(2,1)} %refs_10_.1) | copy-start | bytes 393220
  9.0 19.7 %copy-start.2 = (bf16[128,256]{1,0:T(8,128)(2,1)S(1)}, bf16[128,256]{1,0:T(8,128)(2,1)}, u32[]{:S(2)}) copy-start(bf16[128,256]{1,0:T(8,128)(2,1)} %refs_8_.1) | copy-start | bytes 196612
  9.0 19.7 %copy-start.4 = (f32[256]{0:T(256)S(1)}, f32[256]{0:T(256)}, u32[]{:S(2)}) copy-start(f32[256]{0:T(256)} %param.10) | copy-start | bytes 3076
  9.6 9.5 %collective-permute-start.6 = (bf16[3,256,128]{2,1,0:T(8,128)(2,1)S(1)}, bf16[3,256,128]{2,1,0:T(8,128)(2,1)S(1)}, u32[]{:S(2)}, u32[]{:S(2)}) collective-permute-start(bf16[3,256,128]{2,1,0:T(8,128)(2,1)S(1)} %get-tuple-element.44), channel_id=1, source_target_pairs={{0,2},{1,3},{2,0},{3,1},{4,6},{5,7},{6,4},{7,5},{8,10},{9,11},{10,... | collective-permute-start | bytes 589832 | tf_op jit(solution)/shard_map/ppermute | solution.py:433
  10.1 9.2 %collective-permute-start.7 = (bf16[3,256,128]{2,1,0:T(8,128)(2,1)S(1)}, bf16[3,256,128]{2,1,0:T(8,128)(2,1)S(1)}, u32[]{:S(2)}, u32[]{:S(2)}) collective-permute-start(bf16[3,256,128]{2,1,0:T(8,128)(2,1)S(1)} %get-tuple-element.45), channel_id=1, source_target_pairs={{0,1},{1,0},{2,3},{3,2},{4,5},{5,4},{6,7},{7,6},{8,9},{9,8},{10,11... | collective-permute-start | bytes 589832 | tf_op jit(solution)/shard_map/ppermute | solution.py:433
  15.3 7.8 %collective-permute-start.3 = (bf16[256,128]{1,0:T(8,128)(2,1)S(1)}, bf16[256,128]{1,0:T(8,128)(2,1)S(1)}, u32[]{:S(2)}, u32[]{:S(2)}) collective-permute-start(bf16[256,128]{1,0:T(8,128)(2,1)S(1)} %get-tuple-element.39), channel_id=1, source_target_pairs={{0,3},{1,2},{2,1},{3,0},{4,7},{5,6},{6,5},{7,4},{8,11},{9,10},{10,... | collective-permute-start | bytes 196616 | tf_op jit(solution)/shard_map/ppermute | solution.py:433
  18.4 5.5 %collective-permute-start.4 = (bf16[256,128]{1,0:T(8,128)(2,1)S(1)}, bf16[256,128]{1,0:T(8,128)(2,1)S(1)}, u32[]{:S(2)}, u32[]{:S(2)}) collective-permute-start(bf16[256,128]{1,0:T(8,128)(2,1)S(1)} %get-tuple-element.40), channel_id=1, source_target_pairs={{0,2},{1,3},{2,0},{3,1},{4,6},{5,7},{6,4},{7,5},{8,10},{9,11},{10,... | collective-permute-start | bytes 196616 | tf_op jit(solution)/shard_map/ppermute | solution.py:433
  18.9 5.0 %collective-permute-start.5 = (bf16[256,128]{1,0:T(8,128)(2,1)S(1)}, bf16[256,128]{1,0:T(8,128)(2,1)S(1)}, u32[]{:S(2)}, u32[]{:S(2)}) collective-permute-start(bf16[256,128]{1,0:T(8,128)(2,1)S(1)} %get-tuple-element.41), channel_id=1, source_target_pairs={{0,1},{1,0},{2,3},{3,2},{4,5},{5,4},{6,7},{7,6},{8,9},{9,8},{10,11... | collective-permute-start | bytes 196616 | tf_op jit(solution)/shard_map/ppermute | solution.py:433
  19.4 6.6 %collective-permute-start.8 = (bf16[256,128]{1,0:T(8,128)(2,1)S(1)}, bf16[256,128]{1,0:T(8,128)(2,1)S(1)}, u32[]{:S(2)}, u32[]{:S(2)}) collective-permute-start(bf16[256,128]{1,0:T(8,128)(2,1)S(1)} %get-tuple-element.46), channel_id=1, source_target_pairs={{0,12},{1,13},{2,14},{3,15},{4,8},{5,9},{6,10},{7,11},{8,4},{9,5},... | collective-permute-start | bytes 196616 | tf_op jit(solution)/shard_map/ppermute | solution.py:439
  23.2 5.6 %collective-permute-start.9 = (bf16[256,128]{1,0:T(8,128)(2,1)S(1)}, bf16[256,128]{1,0:T(8,128)(2,1)S(1)}, u32[]{:S(2)}, u32[]{:S(2)}) collective-permute-start(bf16[256,128]{1,0:T(8,128)(2,1)S(1)} %get-tuple-element.47), channel_id=1, source_target_pairs={{0,8},{1,9},{2,10},{3,11},{4,12},{5,13},{6,14},{7,15},{8,0},{9,1},... | collective-permute-start | bytes 196616 | tf_op jit(solution)/shard_map/ppermute | solution.py:439
  23.2 5.6 %collective-permute-start.10 = (bf16[256,128]{1,0:T(8,128)(2,1)S(1)}, bf16[256,128]{1,0:T(8,128)(2,1)S(1)}, u32[]{:S(2)}, u32[]{:S(2)}) collective-permute-start(bf16[256,128]{1,0:T(8,128)(2,1)S(1)} %get-tuple-element.48), channel_id=1, source_target_pairs={{0,4},{1,5},{2,6},{3,7},{4,0},{5,1},{6,2},{7,3},{8,12},{9,13},{10,... | collective-permute-start | bytes 196616 | tf_op jit(solution)/shard_map/ppermute | solution.py:439
  29.7 4.5 %collective-permute-start.11 = (f32[80,256]{1,0:T(8,128)S(1)}, f32[80,256]{1,0:T(8,128)S(1)}, u32[]{:S(2)}, u32[]{:S(2)}) collective-permute-start(f32[80,256]{1,0:T(8,128)S(1)} %get-tuple-element.54), channel_id=1, source_target_pairs={{0,16},{16,0},{1,17},{17,1},{2,18},{18,2},{3,19},{19,3},{4,20},{20... | collective-permute-start | bytes 245768 | tf_op jit(solution)/shard_map/ppermute | solution.py:427
  29.7 6.9 %collective-permute-start.16 = (bf16[128,256]{1,0:T(8,128)(2,1)S(1)}, bf16[128,256]{1,0:T(8,128)(2,1)S(1)}, u32[]{:S(2)}, u32[]{:S(2)}) collective-permute-start(bf16[128,256]{1,0:T(8,128)(2,1)S(1)} %get-tuple-element.50.outgoing_ref), channel_id=1, source_target_pairs={{0,12},{1,13},{2,14},{3,15},{4,8},{5,9},{6,10},{7,11},{8,4},{9,5},... | collective-permute-start | bytes 196616 | tf_op jit(solution)/shard_map/ppermute | solution.py:439
  32.5 6.5 %collective-permute-start.15 = (bf16[128,256]{1,0:T(8,128)(2,1)S(1)}, bf16[128,256]{1,0:T(8,128)(2,1)S(1)}, u32[]{:S(2)}, u32[]{:S(2)}) collective-permute-start(bf16[128,256]{1,0:T(8,128)(2,1)S(1)} %get-tuple-element.50.outgoing_ref), channel_id=1, source_target_pairs={{0,8},{1,9},{2,10},{3,11},{4,12},{5,13},{6,14},{7,15},{8,0},{9,1},... | collective-permute-start | bytes 196616 | tf_op jit(solution)/shard_map/ppermute | solution.py:439
  32.5 6.5 %collective-permute-start.14 = (bf16[128,256]{1,0:T(8,128)(2,1)S(1)}, bf16[128,256]{1,0:T(8,128)(2,1)S(1)}, u32[]{:S(2)}, u32[]{:S(2)}) collective-permute-start(bf16[128,256]{1,0:T(8,128)(2,1)S(1)} %get-tuple-element.50.outgoing_ref), channel_id=1, source_target_pairs={{0,4},{1,5},{2,6},{3,7},{4,0},{5,1},{6,2},{7,3},{8,12},{9,13},{10,... | collective-permute-start | bytes 196616 | tf_op jit(solution)/shard_map/ppermute | solution.py:439
  34.2 10.0 %collective-permute-start.19 = (bf16[208,256]{1,0:T(8,128)(2,1)S(1)}, bf16[208,256]{1,0:T(8,128)(2,1)S(1)}, u32[]{:S(2)}, u32[]{:S(2)}) collective-permute-start(bf16[208,256]{1,0:T(8,128)(2,1)S(1)} %pack.1.refs_0_), channel_id=1, source_target_pairs={{0,3},{1,2},{2,1},{3,0},{4,7},{5,6},{6,5},{7,4},{8,11},{9,10},{10,... | collective-permute-start | bytes 319496 | tf_op jit(solution)/shard_map/ppermute | solution.py:433
  38.9 17.0 %collective-permute-start.20 = (bf16[3,128,256]{2,1,0:T(8,128)(2,1)S(1)}, bf16[3,128,256]{2,1,0:T(8,128)(2,1)S(1)}, u32[]{:S(2)}, u32[]{:S(2)}) collective-permute-start(bf16[3,128,256]{2,1,0:T(8,128)(2,1)S(1)} %stack_line.1.refs_2_), channel_id=1, source_target_pairs={{0,3},{1,2},{2,1},{3,0},{4,7},{5,6},{6,5},{7,4},{8,11},{9,10},{10,... | collective-permute-start | bytes 589832 | tf_op jit(solution)/shard_map/ppermute | solution.py:433
  41.4 19.4 %collective-permute-start.18 = (bf16[3,128,256]{2,1,0:T(8,128)(2,1)S(1)}, bf16[3,128,256]{2,1,0:T(8,128)(2,1)S(1)}, u32[]{:S(2)}, u32[]{:S(2)}) collective-permute-start(bf16[3,128,256]{2,1,0:T(8,128)(2,1)S(1)} %stack_line.1.refs_2_), channel_id=1, source_target_pairs={{0,1},{1,0},{2,3},{3,2},{4,5},{5,4},{6,7},{7,6},{8,9},{9,8},{10,11... | collective-permute-start | bytes 589832 | tf_op jit(solution)/shard_map/ppermute | solution.py:433
  42.0 18.9 %collective-permute-start.17 = (bf16[3,128,256]{2,1,0:T(8,128)(2,1)S(1)}, bf16[3,128,256]{2,1,0:T(8,128)(2,1)S(1)}, u32[]{:S(2)}, u32[]{:S(2)}) collective-permute-start(bf16[3,128,256]{2,1,0:T(8,128)(2,1)S(1)} %stack_line.1.refs_2_), channel_id=1, source_target_pairs={{0,2},{1,3},{2,0},{3,1},{4,6},{5,7},{6,4},{7,5},{8,10},{9,11},{10,... | collective-permute-start | bytes 589832 | tf_op jit(solution)/shard_map/ppermute | solution.py:433
  42.5 11.0 %collective-permute-start.13 = (bf16[208,256]{1,0:T(8,128)(2,1)S(1)}, bf16[208,256]{1,0:T(8,128)(2,1)S(1)}, u32[]{:S(2)}, u32[]{:S(2)}) collective-permute-start(bf16[208,256]{1,0:T(8,128)(2,1)S(1)} %pack.1.refs_0_), channel_id=1, source_target_pairs={{0,1},{1,0},{2,3},{3,2},{4,5},{5,4},{6,7},{7,6},{8,9},{9,8},{10,11... | collective-permute-start | bytes 319496 | tf_op jit(solution)/shard_map/ppermute | solution.py:433
  44.2 9.2 %collective-permute-start.12 = (bf16[208,256]{1,0:T(8,128)(2,1)S(1)}, bf16[208,256]{1,0:T(8,128)(2,1)S(1)}, u32[]{:S(2)}, u32[]{:S(2)}) collective-permute-start(bf16[208,256]{1,0:T(8,128)(2,1)S(1)} %pack.1.refs_0_), channel_id=1, source_target_pairs={{0,2},{1,3},{2,0},{3,1},{4,6},{5,7},{6,4},{7,5},{8,10},{9,11},{10,... | collective-permute-start | bytes 319496 | tf_op jit(solution)/shard_map/ppermute | solution.py:433
  53.5 5.9 %collective-permute-start.23 = (bf16[80,256]{1,0:T(8,128)(2,1)S(1)}, bf16[80,256]{1,0:T(8,128)(2,1)S(1)}, u32[]{:S(2)}, u32[]{:S(2)}) collective-permute-start(bf16[80,256]{1,0:T(8,128)(2,1)S(1)} %sum_terms.1.refs_6_), channel_id=1, source_target_pairs={{0,12},{1,13},{2,14},{3,15},{4,8},{5,9},{6,10},{7,11},{8,4},{9,5},... | collective-permute-start | bytes 122888 | tf_op jit(solution)/shard_map/ppermute | solution.py:439
  55.9 4.9 %collective-permute-start.22 = (bf16[80,256]{1,0:T(8,128)(2,1)S(1)}, bf16[80,256]{1,0:T(8,128)(2,1)S(1)}, u32[]{:S(2)}, u32[]{:S(2)}) collective-permute-start(bf16[80,256]{1,0:T(8,128)(2,1)S(1)} %sum_terms.1.refs_6_), channel_id=1, source_target_pairs={{0,8},{1,9},{2,10},{3,11},{4,12},{5,13},{6,14},{7,15},{8,0},{9,1},... | collective-permute-start | bytes 122888 | tf_op jit(solution)/shard_map/ppermute | solution.py:439
  55.9 4.9 %collective-permute-start.21 = (bf16[80,256]{1,0:T(8,128)(2,1)S(1)}, bf16[80,256]{1,0:T(8,128)(2,1)S(1)}, u32[]{:S(2)}, u32[]{:S(2)}) collective-permute-start(bf16[80,256]{1,0:T(8,128)(2,1)S(1)} %sum_terms.1.refs_6_), channel_id=1, source_target_pairs={{0,4},{1,5},{2,6},{3,7},{4,0},{5,1},{6,2},{7,3},{8,12},{9,13},{10,... | collective-permute-start | bytes 122888 | tf_op jit(solution)/shard_map/ppermute | solution.py:439
  61.3 1.4 %collective-permute-start.24 = (bf16[208,256]{1,0:T(8,128)(2,1)S(1)}, bf16[208,256]{1,0:T(8,128)(2,1)S(1)}, u32[]{:S(2)}, u32[]{:S(2)}) collective-permute-start(bf16[208,256]{1,0:T(8,128)(2,1)S(1)} %get-tuple-element.58.sent_ref), channel_id=1, source_target_pairs={{0,16},{16,0},{1,17},{17,1},{2,18},{18,2},{3,19},{19,3},{4,20},{20... | collective-permute-start | bytes 319496 | tf_op jit(solution)/shard_map/ppermute | solution.py:427

commit v5 on v3

--- a/solution.py
+++ b/solution.py
@@ -332,16 +332,16 @@
     )(*items)
 
 
-def backward_kernel(steps, pieces, has_totals, dense_ref, *refs):
+def backward_kernel(steps, chosen, pieces, has_totals, dense_ref, *refs):
     count = len(steps)
     parcels, stacks = refs[:count], refs[count : 2 * count]
-    inputs, outs = refs[2 * count : -pieces], refs[-pieces:]
-    terms = inputs[pieces if has_totals else 0 :]
+    inputs, outs = refs[2 * count : -len(chosen)], refs[-len(chosen) :]
+    terms = inputs[len(chosen) if has_totals else 0 :]
     high, low, nodes, _ = dense_ref.shape
     row, line, plane = spot(low)
-    for piece in range(pieces):
+    for index, piece in enumerate(chosen):
         columns = piece_columns(other(row, piece, pieces), nodes)
-        total = inputs[piece][...] if has_totals else None
+        total = inputs[index][...] if has_totals else None
         for step, parcel_ref, stack_ref in zip(steps, parcels, stacks):
             origin = source(plane, step, low)
             depth = stack_ref.shape[1]
@@ -349,14 +349,15 @@
                 values = stack_ref[hop - 1] if hop else parcel_ref[0:depth, :]
                 term = dot(values, dense_ref[source(line, hop, high), origin, :, columns])
                 total = term if total is None else total + term
-        outs[piece][0:depth, :] = total.astype(outs[piece].dtype)
+        outs[index][0:depth, :] = total.astype(outs[index].dtype)
         if terms and piece:
-            outs[piece][depth:, :] = tree_sum([ref[...].astype(F32) for ref in terms]).astype(BF16)
-
-
-def backward(dense, parcels, stacks, totals, terms=()):
+            outs[index][depth:, :] = tree_sum([ref[...].astype(F32) for ref in terms]).astype(BF16)
+
+
+def backward(dense, parcels, stacks, totals, terms=(), chosen=None):
     nodes, slots = dense.shape[2:]
     pieces = slots // nodes
+    chosen = tuple(range(pieces)) if chosen is None else chosen
     depth = next(iter(stacks.values())).shape[1]
     inputs = list(parcels.values()) + list(stacks.values()) + list(totals) + list(terms)
 
@@ -366,8 +367,8 @@
         return jax.ShapeDtypeStruct((depth, nodes), F32)
 
     return pl.pallas_call(
-        functools.partial(backward_kernel, tuple(stacks), pieces, bool(totals)),
-        out_shape=[shape_of(piece) for piece in range(pieces)],
+        functools.partial(backward_kernel, tuple(stacks), chosen, pieces, bool(totals)),
+        out_shape=[shape_of(piece) for piece in chosen],
         in_specs=[pl.BlockSpec(memory_space=pltpu.VMEM)] * (1 + len(inputs)),
         compiler_params=params(),
         name="backward_product",
@@ -469,16 +470,14 @@
     terms = sum_terms([parcels[step] for step in range(low)], weight.shape[0])
     parts = {0: terms} | {step: over_line(terms, step) for step in far_first(high)}
     terms = [parts[step] for step in range(high)]
-    steps, totals = list(stacks), []
-    for group in (steps[: low // 2], steps[low // 2 :]):
-        if group:
-            totals = backward(
-                dense,
-                {step: parcels[step] for step in group},
-                {step: stacks[step] for step in group},
-                totals,
-                terms if group[-1] == steps[-1] else (),
-            )
+    steps = list(stacks)
+    early, late = (
+        ({step: parcels[step] for step in group}, {step: stacks[step] for step in group})
+        for group in (steps[: low // 2], steps[low // 2 :])
+    )
+    totals = backward(dense, *early, [])
+    sent = backward(dense, *late, totals[1:], terms, tuple(range(1, rows)))
+    totals = backward(dense, *late, totals[:1], (), (0,)) + sent
     returned = [over_row(totals[step], step) for step in range(1, rows)]
     grad_features, grad_weight, grad_bias = finish(degrees_row, totals[0], totals[1], returned)
     return activations, grad_features, grad_weight, grad_bias[0]

time: 57 us -> 57 us (level)
  transfers between devices with their start and end apart: 25 -> 25, of which waited for: 10 -> 11; matrix products, arithmetic and copies ran while one was open for 0% -> 0% of each run, Pallas kernels for 9% -> 9%
where the time goes in v5:
time: 57 us; the launch traced here: 56.9 us
  starting transfers between devices  30.1 us (53%)
  waiting for transfers between devices  17.5 us (31%)
  Pallas kernels  7.84 us (14%)
  between operations  1.47 us (3%)
    ppermute x12, starting transfers between devices, over_plane(): return lax.ppermute(values, 'col', pairs)  17.3 us
    ppermute x9, starting transfers between devices, over_line(): return lax.ppermute(values, 'col', pairs)  12.1 us
    ppermute x9, waiting for transfers between devices, over_line(): return lax.ppermute(values, 'col', pairs)  11.3 us
    ppermute x12, waiting for transfers between devices, over_plane(): return lax.ppermute(values, 'col', pairs)  5.95 us
    pallas_call x1, Pallas kernels, densify(): pl.pallas_call(functools.partial(densify_kernel, col_slots), out_shape=ja...  2.55 us
    pallas_call x3, Pallas kernels, forward(): pl.pallas_call(functools.partial(forward_kernel, wanted, pieces, scaling)...  1.7 us
  transfers between devices with their start and end apart: 25, of which 11 were waited for; matrix products, arithmetic and copies ran while one was open for 0% of the time, Pallas kernels for 9%

profile of v5, /device:TPU:0, one launch (start us, length us, event | category | flops | bytes accessed | tf_op | source)
XLA Modules:
  0.0 56.9 jit_solution(1192691284851301384)
XLA Ops:
  0.6 0.5 collective-permute-start.1
  1.1 0.1 collective-permute-start
  1.9 2.5 %densify.1 = bf16[32,128,512]{2,1,0:T(8,128)(2,1)S(1)} custom-call(s32[1,1,128]{2,1,0:T(1,128)} %positions_hbm.1, s32[1,1]{1,0:T(1,128)S(6)} %copy.12.counts_ref, bf16[128,128,128]{2,1,0:T(8,128)(2,1)} %bitcast.17), custom_call_target="tpu_custom_call" | custom-call | tf_op jit(solution)/shard_map/densify/pallas_call | solution.py:107
  4.5 0.0 collective-permute-done
  4.5 0.0 collective-permute-done.1.refs_3_
  4.5 0.5 forward_product.3
  5.0 3.9 %collective-permute-start.5 = (bf16[3,256,128]{2,1,0:T(8,128)(2,1)S(1)}, bf16[3,256,128]{2,1,0:T(8,128)(2,1)S(1)}, u32[]{:S(2)}, u32[]{:S(2)}) collective-permute-start(bf16[3,256,128]{2,1,0:T(8,128)(2,1)S(1)} %get-tuple-element.42), channel_id=1, source_target_pairs={{0,3},{1,2},{2,1},{3,0},{4,7},{5,6},{6,5},{7,4},{8,11},{9,10},{10,... | collective-permute-start | bytes 589832 | tf_op jit(solution)/shard_map/ppermute | solution.py:434
  9.0 0.6 forward_product.5
  9.5 0.6 %collective-permute-start.6 = (bf16[3,256,128]{2,1,0:T(8,128)(2,1)S(1)}, bf16[3,256,128]{2,1,0:T(8,128)(2,1)S(1)}, u32[]{:S(2)}, u32[]{:S(2)}) collective-permute-start(bf16[3,256,128]{2,1,0:T(8,128)(2,1)S(1)} %get-tuple-element.43), channel_id=1, source_target_pairs={{0,2},{1,3},{2,0},{3,1},{4,6},{5,7},{6,4},{7,5},{8,10},{9,11},{10,... | collective-permute-start | bytes 589832 | tf_op jit(solution)/shard_map/ppermute | solution.py:434
  10.2 0.1 collective-permute-start.7
  10.2 0.6 %forward_product.4 = (f32[3,256,128]{2,1,0:T(8,128)S(1)}, bf16[256,128]{1,0:T(8,128)(2,1)S(1)}, bf16[256,128]{1,0:T(8,128)(2,1)S(1)}, bf16[256,128]{1,0:T(8,128)(2,1)S(1)}, f32[256,128]{1,0:T(8,128)S(1)}) custom-call(bf16[4,4,256,512]{3,2,1,0:T(8,128)(2,1)S(1)} %bitcast.8, bf16[256,128]{1,0:T(8,128)(2,1)S(1)} %get-tuple-element.35.refs_0_, ...), custom_call_target="tpu_custom_call" | custom-call | tf_op jit(solution)/shard_map/forward_product/pallas_call | solution.py:177
  10.9 2.9 %collective-permute-start.2 = (bf16[256,128]{1,0:T(8,128)(2,1)S(1)}, bf16[256,128]{1,0:T(8,128)(2,1)S(1)}, u32[]{:S(2)}, u32[]{:S(2)}) collective-permute-start(bf16[256,128]{1,0:T(8,128)(2,1)S(1)} %get-tuple-element.38), channel_id=1, source_target_pairs={{0,3},{1,2},{2,1},{3,0},{4,7},{5,6},{6,5},{7,4},{8,11},{9,10},{10,... | collective-permute-start | bytes 196616 | tf_op jit(solution)/shard_map/ppermute | solution.py:434
  13.8 0.6 collective-permute-start.3
  14.3 0.4 collective-permute-done.5.refs_1_
  14.7 2.0 %collective-permute-start.4 = (bf16[256,128]{1,0:T(8,128)(2,1)S(1)}, bf16[256,128]{1,0:T(8,128)(2,1)S(1)}, u32[]{:S(2)}, u32[]{:S(2)}) collective-permute-start(bf16[256,128]{1,0:T(8,128)(2,1)S(1)} %get-tuple-element.40), channel_id=1, source_target_pairs={{0,1},{1,0},{2,3},{3,2},{4,5},{5,4},{6,7},{7,6},{8,9},{9,8},{10,11... | collective-permute-start | bytes 196616 | tf_op jit(solution)/shard_map/ppermute | solution.py:434
  16.8 2.3 %collective-permute-done.6.refs_2_ = bf16[3,256,128]{2,1,0:T(8,128)(2,1)S(1)} collective-permute-done((bf16[3,256,128]{2,1,0:T(8,128)(2,1)S(1)}, bf16[3,256,128]{2,1,0:T(8,128)(2,1)S(1)}, u32[]{:S(2)}, u32[]{:S(2)}) %collective-permute-start.6) | collective-permute-done | bytes 196640 | tf_op jit(solution)/shard_map/ppermute | solution.py:434
  19.0 0.4 collective-permute-done.7.refs_3_
  19.4 0.1 combine.1
  19.5 4.0 %collective-permute-start.8 = (bf16[256,128]{1,0:T(8,128)(2,1)S(1)}, bf16[256,128]{1,0:T(8,128)(2,1)S(1)}, u32[]{:S(2)}, u32[]{:S(2)}) collective-permute-start(bf16[256,128]{1,0:T(8,128)(2,1)S(1)} %get-tuple-element.45), channel_id=1, source_target_pairs={{0,12},{1,13},{2,14},{3,15},{4,8},{5,9},{6,10},{7,11},{8,4},{9,5},... | collective-permute-start | bytes 196616 | tf_op jit(solution)/shard_map/ppermute | solution.py:440
  23.6 0.0 collective-permute-start.9
  23.6 0.0 collective-permute-done.2.refs_1_
  23.6 0.6 %collective-permute-start.10 = (bf16[256,128]{1,0:T(8,128)(2,1)S(1)}, bf16[256,128]{1,0:T(8,128)(2,1)S(1)}, u32[]{:S(2)}, u32[]{:S(2)}) collective-permute-start(bf16[256,128]{1,0:T(8,128)(2,1)S(1)} %get-tuple-element.47), channel_id=1, source_target_pairs={{0,4},{1,5},{2,6},{3,7},{4,0},{5,1},{6,2},{7,3},{8,12},{9,13},{10,... | collective-permute-start | bytes 196616 | tf_op jit(solution)/shard_map/ppermute | solution.py:440
  24.2 0.0 collective-permute-done.3.refs_2_
  24.2 0.0 collective-permute-done.4.refs_3_
  24.2 2.3 %collective-permute-done.8.refs_4_ = bf16[256,128]{1,0:T(8,128)(2,1)S(1)} collective-permute-done((bf16[256,128]{1,0:T(8,128)(2,1)S(1)}, bf16[256,128]{1,0:T(8,128)(2,1)S(1)}, u32[]{:S(2)}, u32[]{:S(2)}) %collective-permute-start.8) | collective-permute-done | bytes 65568 | tf_op jit(solution)/shard_map/ppermute | solution.py:440
  26.5 2.3 %collective-permute-done.9.refs_5_ = bf16[256,128]{1,0:T(8,128)(2,1)S(1)} collective-permute-done((bf16[256,128]{1,0:T(8,128)(2,1)S(1)}, bf16[256,128]{1,0:T(8,128)(2,1)S(1)}, u32[]{:S(2)}, u32[]{:S(2)}) %collective-permute-start.9) | collective-permute-done | bytes 65568 | tf_op jit(solution)/shard_map/ppermute | solution.py:440
  28.8 0.3 collective-permute-done.10.refs_6_
  29.2 0.0 copy-done
  29.2 0.0 copy-done.4
  29.2 0.6 %layer.1 = (bf16[128,256]{1,0:T(8,128)(2,1)S(1)}, f32[256,128]{1,0:T(8,128)S(1)}, f32[256,256]{1,0:T(8,128)S(1)}, f32[256,256]{1,0:T(8,128)S(1)}) custom-call(f32[256,128]{1,0:T(8,128)S(1)} %get-tuple-element.37.refs_0_, bf16[256,128]{1,0:T(8,128)(2,1)S(1)} %collective-permute-done.2.refs_1_, bf16[256,128]{1,0:T(8,128)(2,1)S(1)} %collective-permute-done.3.refs_2_, ...), custom_call_target="tpu_custom_call" | custom-call | tf_op jit(solution)/shard_map/layer/pallas_call | solution.py:228
  29.8 0.3 weight_terms.1
  30.1 0.1 collective-permute-start.14
  30.2 2.4 %collective-permute-start.13 = (bf16[128,256]{1,0:T(8,128)(2,1)S(1)}, bf16[128,256]{1,0:T(8,128)(2,1)S(1)}, u32[]{:S(2)}, u32[]{:S(2)}) collective-permute-start(bf16[128,256]{1,0:T(8,128)(2,1)S(1)} %get-tuple-element.49.outgoing_ref), channel_id=1, source_target_pairs={{0,12},{1,13},{2,14},{3,15},{4,8},{5,9},{6,10},{7,11},{8,4},{9,5},... | collective-permute-start | bytes 196616 | tf_op jit(solution)/shard_map/ppermute | solution.py:440
  32.6 0.0 collective-permute-done.14.refs_1_
  32.6 2.2 %collective-permute-start.17 = (bf16[208,256]{1,0:T(8,128)(2,1)S(1)}, bf16[208,256]{1,0:T(8,128)(2,1)S(1)}, u32[]{:S(2)}, u32[]{:S(2)}) collective-permute-start(bf16[208,256]{1,0:T(8,128)(2,1)S(1)} %pack.1.refs_0_), channel_id=1, source_target_pairs={{0,3},{1,2},{2,1},{3,0},{4,7},{5,6},{6,5},{7,4},{8,11},{9,10},{10,... | collective-permute-start | bytes 319496 | tf_op jit(solution)/shard_map/ppermute | solution.py:434
  34.8 0.8 %collective-permute-start.16 = (bf16[208,256]{1,0:T(8,128)(2,1)S(1)}, bf16[208,256]{1,0:T(8,128)(2,1)S(1)}, u32[]{:S(2)}, u32[]{:S(2)}) collective-permute-start(bf16[208,256]{1,0:T(8,128)(2,1)S(1)} %pack.1.refs_0_), channel_id=1, source_target_pairs={{0,2},{1,3},{2,0},{3,1},{4,6},{5,7},{6,4},{7,5},{8,10},{9,11},{10,... | collective-permute-start | bytes 319496 | tf_op jit(solution)/shard_map/ppermute | solution.py:434
  35.6 0.6 collective-permute-start.15
  36.1 0.5 collective-permute-start.12
  36.6 0.0 collective-permute-done.13.refs_2_
  36.6 1.6 %collective-permute-start.11 = (bf16[128,256]{1,0:T(8,128)(2,1)S(1)}, bf16[128,256]{1,0:T(8,128)(2,1)S(1)}, u32[]{:S(2)}, u32[]{:S(2)}) collective-permute-start(bf16[128,256]{1,0:T(8,128)(2,1)S(1)} %get-tuple-element.49.outgoing_ref), channel_id=1, source_target_pairs={{0,4},{1,5},{2,6},{3,7},{4,0},{5,1},{6,2},{7,3},{8,12},{9,13},{10,... | collective-permute-start | bytes 196616 | tf_op jit(solution)/shard_map/ppermute | solution.py:440
  38.2 3.4 %collective-permute-done.12.refs_1_ = bf16[128,256]{1,0:T(8,128)(2,1)S(1)} collective-permute-done((bf16[128,256]{1,0:T(8,128)(2,1)S(1)}, bf16[128,256]{1,0:T(8,128)(2,1)S(1)}, u32[]{:S(2)}, u32[]{:S(2)}) %collective-permute-start.12) | collective-permute-done | bytes 65568 | tf_op jit(solution)/shard_map/ppermute | solution.py:440
  41.6 0.0 collective-permute-done.11.refs_0_
  41.6 0.0 collective-permute-done.17.refs_1_.refs_3_
  41.6 0.0 collective-permute-done.16.refs_0_.refs_2_
  41.6 0.0 collective-permute-done.15.refs_1_
  41.7 2.0 %collective-permute-start.20 = (bf16[3,128,256]{2,1,0:T(8,128)(2,1)S(1)}, bf16[3,128,256]{2,1,0:T(8,128)(2,1)S(1)}, u32[]{:S(2)}, u32[]{:S(2)}) collective-permute-start(bf16[3,128,256]{2,1,0:T(8,128)(2,1)S(1)} %stack_line.1.refs_2_), channel_id=1, source_target_pairs={{0,3},{1,2},{2,1},{3,0},{4,7},{5,6},{6,5},{7,4},{8,11},{9,10},{10,... | collective-permute-start | bytes 589832 | tf_op jit(solution)/shard_map/ppermute | solution.py:434
  43.7 0.9 %collective-permute-start.19 = (bf16[3,128,256]{2,1,0:T(8,128)(2,1)S(1)}, bf16[3,128,256]{2,1,0:T(8,128)(2,1)S(1)}, u32[]{:S(2)}, u32[]{:S(2)}) collective-permute-start(bf16[3,128,256]{2,1,0:T(8,128)(2,1)S(1)} %stack_line.1.refs_2_), channel_id=1, source_target_pairs={{0,1},{1,0},{2,3},{3,2},{4,5},{5,4},{6,7},{7,6},{8,9},{9,8},{10,11... | collective-permute-start | bytes 589832 | tf_op jit(solution)/shard_map/ppermute | solution.py:434
  44.5 0.7 %collective-permute-start.18 = (bf16[3,128,256]{2,1,0:T(8,128)(2,1)S(1)}, bf16[3,128,256]{2,1,0:T(8,128)(2,1)S(1)}, u32[]{:S(2)}, u32[]{:S(2)}) collective-permute-start(bf16[3,128,256]{2,1,0:T(8,128)(2,1)S(1)} %stack_line.1.refs_2_), channel_id=1, source_target_pairs={{0,2},{1,3},{2,0},{3,1},{4,6},{5,7},{6,4},{7,5},{8,10},{9,11},{10,... | collective-permute-start | bytes 589832 | tf_op jit(solution)/shard_map/ppermute | solution.py:434
  45.2 2.3 %collective-permute-start.23 = (bf16[80,256]{1,0:T(8,128)(2,1)S(1)}, bf16[80,256]{1,0:T(8,128)(2,1)S(1)}, u32[]{:S(2)}, u32[]{:S(2)}) collective-permute-start(bf16[80,256]{1,0:T(8,128)(2,1)S(1)} %sum_terms.1.refs_5_), channel_id=1, source_target_pairs={{0,12},{1,13},{2,14},{3,15},{4,8},{5,9},{6,10},{7,11},{8,4},{9,5},... | collective-permute-start | bytes 122888 | tf_op jit(solution)/shard_map/ppermute | solution.py:440
  47.5 0.1 collective-permute-start.22
  47.6 2.8 %collective-permute-done.20.refs_3_ = bf16[3,128,256]{2,1,0:T(8,128)(2,1)S(1)} collective-permute-done((bf16[3,128,256]{2,1,0:T(8,128)(2,1)S(1)}, bf16[3,128,256]{2,1,0:T(8,128)(2,1)S(1)}, u32[]{:S(2)}, u32[]{:S(2)}) %collective-permute-start.20) | collective-permute-done | bytes 196640 | tf_op jit(solution)/shard_map/ppermute | solution.py:434
  50.5 0.6 %collective-permute-start.21 = (bf16[80,256]{1,0:T(8,128)(2,1)S(1)}, bf16[80,256]{1,0:T(8,128)(2,1)S(1)}, u32[]{:S(2)}, u32[]{:S(2)}) collective-permute-start(bf16[80,256]{1,0:T(8,128)(2,1)S(1)} %sum_terms.1.refs_5_), channel_id=1, source_target_pairs={{0,4},{1,5},{2,6},{3,7},{4,0},{5,1},{6,2},{7,3},{8,12},{9,13},{10,... | collective-permute-start | bytes 122888 | tf_op jit(solution)/shard_map/ppermute | solution.py:440
  51.0 0.4 backward_product.3
  51.5 0.0 collective-permute-done.23.refs_8_
  51.5 0.9 %collective-permute-done.22.refs_7_ = bf16[80,256]{1,0:T(8,128)(2,1)S(1)} collective-permute-done((bf16[80,256]{1,0:T(8,128)(2,1)S(1)}, bf16[80,256]{1,0:T(8,128)(2,1)S(1)}, u32[]{:S(2)}, u32[]{:S(2)}) %collective-permute-start.22) | collective-permute-done | bytes 40992 | tf_op jit(solution)/shard_map/ppermute | solution.py:440
  52.4 2.1 %collective-permute-done.21.refs_6_ = bf16[80,256]{1,0:T(8,128)(2,1)S(1)} collective-permute-done((bf16[80,256]{1,0:T(8,128)(2,1)S(1)}, bf16[80,256]{1,0:T(8,128)(2,1)S(1)}, u32[]{:S(2)}, u32[]{:S(2)}) %collective-permute-start.21) | collective-permute-done | bytes 40992 | tf_op jit(solution)/shard_map/ppermute | solution.py:440
  54.5 0.0 collective-permute-done.19.refs_3_
  54.5 0.0 collective-permute-done.18.refs_2_
  54.5 0.3 backward_product.5.sent_ref
  54.8 0.1 collective-permute-start.24
  54.9 0.7 %activations.1 = bf16[256,256]{1,0:T(8,128)(2,1)} custom-call(f32[256,256]{1,0:T(8,128)S(1)} %get-tuple-element.48.preact_ref), custom_call_target="tpu_custom_call" | custom-call | tf_op jit(solution)/shard_map/activations/pallas_call | solution.py:247
  55.6 0.3 backward_product.4.own_ref
  55.9 0.2 collective-permute-done.24.refs_0_
  56.2 0.7 %finish.1 = (bf16[256,128]{1,0:T(8,128)(2,1)}, f32[128,256]{1,0:T(8,128)}, f32[1,256]{1,0:T(1,128)}) custom-call(s32[1,256]{1,0:T(1,128)S(1)} %bitcast.14, f32[128,256]{1,0:T(8,128)S(1)} %backward_product.4.own_ref, bf16[208,256]{1,0:T(8,128)(2,1)S(1)} %backward_product.5.sent_ref, bf16[208,256]{1,0:T(8,128)(2,1)S(1)} %collective-permute-done.24.refs_0_), custom_call_target="tpu_custom_call" | custom-call | tf_op jit(solution)/shard_map/finish/pallas_call | solution.py:396
  (11 shorter events, 0.1 us)
Async XLA Ops:
  0.6 3.8 %collective-permute-start.1 = (bf16[256,128]{1,0:T(8,128)(2,1)}, bf16[256,128]{1,0:T(8,128)(2,1)S(1)}, u32[]{:S(2)}, u32[]{:S(2)}) collective-permute-start(bf16[256,128]{1,0:T(8,128)(2,1)} %refs_2_.1), channel_id=1, source_target_pairs={{0,16},{16,0},{1,17},{17,1},{2,18},{18,2},{3,19},{19,3},{4,20},{20... | collective-permute-start | bytes 196616 | tf_op jit(solution)/shard_map/ppermute | solution.py:428
  1.1 3.3 %collective-permute-start = (s32[256]{0:T(256)}, s32[256]{0:T(256)S(1)}, u32[]{:S(2)}, u32[]{:S(2)}) collective-permute-start(s32[256]{0:T(256)} %param.12), channel_id=1, source_target_pairs={{0,16},{16,0},{1,17},{17,1},{2,18},{18,2},{3,19},{19,3},{4,20},{20... | collective-permute-start | bytes 3080 | tf_op jit(solution)/shard_map/ppermute | solution.py:428
  1.9 2.6 %copy-start.1 = (bf16[256,128]{1,0:T(8,128)(2,1)S(1)}, bf16[256,128]{1,0:T(8,128)(2,1)}, u32[]{:S(2)}) copy-start(bf16[256,128]{1,0:T(8,128)(2,1)} %refs_2_.1) | copy-start | bytes 196612
  1.9 2.6 %copy-start.3 = (s32[256]{0:T(256)S(1)}, s32[256]{0:T(256)}, u32[]{:S(2)}) copy-start(s32[256]{0:T(256)} %param.12) | copy-start | bytes 3076
  5.0 9.7 %collective-permute-start.5 = (bf16[3,256,128]{2,1,0:T(8,128)(2,1)S(1)}, bf16[3,256,128]{2,1,0:T(8,128)(2,1)S(1)}, u32[]{:S(2)}, u32[]{:S(2)}) collective-permute-start(bf16[3,256,128]{2,1,0:T(8,128)(2,1)S(1)} %get-tuple-element.42), channel_id=1, source_target_pairs={{0,3},{1,2},{2,1},{3,0},{4,7},{5,6},{6,5},{7,4},{8,11},{9,10},{10,... | collective-permute-start | bytes 589832 | tf_op jit(solution)/shard_map/ppermute | solution.py:434
  9.0 20.2 %copy-start = (bf16[256,256]{1,0:T(8,128)(2,1)S(1)}, bf16[256,256]{1,0:T(8,128)(2,1)}, u32[]{:S(2)}) copy-start(bf16[256,256]{1,0:T(8,128)(2,1)} %refs_10_.1) | copy-start | bytes 393220
  9.0 20.2 %copy-start.2 = (bf16[128,256]{1,0:T(8,128)(2,1)S(1)}, bf16[128,256]{1,0:T(8,128)(2,1)}, u32[]{:S(2)}) copy-start(bf16[128,256]{1,0:T(8,128)(2,1)} %refs_8_.1) | copy-start | bytes 196612
  9.0 20.2 %copy-start.4 = (f32[256]{0:T(256)S(1)}, f32[256]{0:T(256)}, u32[]{:S(2)}) copy-start(f32[256]{0:T(256)} %param.10) | copy-start | bytes 3076
  9.5 9.5 %collective-permute-start.6 = (bf16[3,256,128]{2,1,0:T(8,128)(2,1)S(1)}, bf16[3,256,128]{2,1,0:T(8,128)(2,1)S(1)}, u32[]{:S(2)}, u32[]{:S(2)}) collective-permute-start(bf16[3,256,128]{2,1,0:T(8,128)(2,1)S(1)} %get-tuple-element.43), channel_id=1, source_target_pairs={{0,2},{1,3},{2,0},{3,1},{4,6},{5,7},{6,4},{7,5},{8,10},{9,11},{10,... | collective-permute-start | bytes 589832 | tf_op jit(solution)/shard_map/ppermute | solution.py:434
  10.2 9.3 %collective-permute-start.7 = (bf16[3,256,128]{2,1,0:T(8,128)(2,1)S(1)}, bf16[3,256,128]{2,1,0:T(8,128)(2,1)S(1)}, u32[]{:S(2)}, u32[]{:S(2)}) collective-permute-start(bf16[3,256,128]{2,1,0:T(8,128)(2,1)S(1)} %get-tuple-element.44), channel_id=1, source_target_pairs={{0,1},{1,0},{2,3},{3,2},{4,5},{5,4},{6,7},{7,6},{8,9},{9,8},{10,11... | collective-permute-start | bytes 589832 | tf_op jit(solution)/shard_map/ppermute | solution.py:434
  10.9 12.7 %collective-permute-start.2 = (bf16[256,128]{1,0:T(8,128)(2,1)S(1)}, bf16[256,128]{1,0:T(8,128)(2,1)S(1)}, u32[]{:S(2)}, u32[]{:S(2)}) collective-permute-start(bf16[256,128]{1,0:T(8,128)(2,1)S(1)} %get-tuple-element.38), channel_id=1, source_target_pairs={{0,3},{1,2},{2,1},{3,0},{4,7},{5,6},{6,5},{7,4},{8,11},{9,10},{10,... | collective-permute-start | bytes 196616 | tf_op jit(solution)/shard_map/ppermute | solution.py:434
  13.8 10.5 %collective-permute-start.3 = (bf16[256,128]{1,0:T(8,128)(2,1)S(1)}, bf16[256,128]{1,0:T(8,128)(2,1)S(1)}, u32[]{:S(2)}, u32[]{:S(2)}) collective-permute-start(bf16[256,128]{1,0:T(8,128)(2,1)S(1)} %get-tuple-element.39), channel_id=1, source_target_pairs={{0,2},{1,3},{2,0},{3,1},{4,6},{5,7},{6,4},{7,5},{8,10},{9,11},{10,... | collective-permute-start | bytes 196616 | tf_op jit(solution)/shard_map/ppermute | solution.py:434
  14.7 9.5 %collective-permute-start.4 = (bf16[256,128]{1,0:T(8,128)(2,1)S(1)}, bf16[256,128]{1,0:T(8,128)(2,1)S(1)}, u32[]{:S(2)}, u32[]{:S(2)}) collective-permute-start(bf16[256,128]{1,0:T(8,128)(2,1)S(1)} %get-tuple-element.40), channel_id=1, source_target_pairs={{0,1},{1,0},{2,3},{3,2},{4,5},{5,4},{6,7},{7,6},{8,9},{9,8},{10,11... | collective-permute-start | bytes 196616 | tf_op jit(solution)/shard_map/ppermute | solution.py:434
  19.5 7.0 %collective-permute-start.8 = (bf16[256,128]{1,0:T(8,128)(2,1)S(1)}, bf16[256,128]{1,0:T(8,128)(2,1)S(1)}, u32[]{:S(2)}, u32[]{:S(2)}) collective-permute-start(bf16[256,128]{1,0:T(8,128)(2,1)S(1)} %get-tuple-element.45), channel_id=1, source_target_pairs={{0,12},{1,13},{2,14},{3,15},{4,8},{5,9},{6,10},{7,11},{8,4},{9,5},... | collective-permute-start | bytes 196616 | tf_op jit(solution)/shard_map/ppermute | solution.py:440
  23.6 5.2 %collective-permute-start.9 = (bf16[256,128]{1,0:T(8,128)(2,1)S(1)}, bf16[256,128]{1,0:T(8,128)(2,1)S(1)}, u32[]{:S(2)}, u32[]{:S(2)}) collective-permute-start(bf16[256,128]{1,0:T(8,128)(2,1)S(1)} %get-tuple-element.46), channel_id=1, source_target_pairs={{0,8},{1,9},{2,10},{3,11},{4,12},{5,13},{6,14},{7,15},{8,0},{9,1},... | collective-permute-start | bytes 196616 | tf_op jit(solution)/shard_map/ppermute | solution.py:440
  23.6 5.6 %collective-permute-start.10 = (bf16[256,128]{1,0:T(8,128)(2,1)S(1)}, bf16[256,128]{1,0:T(8,128)(2,1)S(1)}, u32[]{:S(2)}, u32[]{:S(2)}) collective-permute-start(bf16[256,128]{1,0:T(8,128)(2,1)S(1)} %get-tuple-element.47), channel_id=1, source_target_pairs={{0,4},{1,5},{2,6},{3,7},{4,0},{5,1},{6,2},{7,3},{8,12},{9,13},{10,... | collective-permute-start | bytes 196616 | tf_op jit(solution)/shard_map/ppermute | solution.py:440
  30.1 2.5 %collective-permute-start.14 = (f32[80,256]{1,0:T(8,128)S(1)}, f32[80,256]{1,0:T(8,128)S(1)}, u32[]{:S(2)}, u32[]{:S(2)}) collective-permute-start(f32[80,256]{1,0:T(8,128)S(1)} %get-tuple-element.53), channel_id=1, source_target_pairs={{0,16},{16,0},{1,17},{17,1},{2,18},{18,2},{3,19},{19,3},{4,20},{20... | collective-permute-start | bytes 245768 | tf_op jit(solution)/shard_map/ppermute | solution.py:428
  30.2 6.5 %collective-permute-start.13 = (bf16[128,256]{1,0:T(8,128)(2,1)S(1)}, bf16[128,256]{1,0:T(8,128)(2,1)S(1)}, u32[]{:S(2)}, u32[]{:S(2)}) collective-permute-start(bf16[128,256]{1,0:T(8,128)(2,1)S(1)} %get-tuple-element.49.outgoing_ref), channel_id=1, source_target_pairs={{0,12},{1,13},{2,14},{3,15},{4,8},{5,9},{6,10},{7,11},{8,4},{9,5},... | collective-permute-start | bytes 196616 | tf_op jit(solution)/shard_map/ppermute | solution.py:440
  32.6 9.0 %collective-permute-start.17 = (bf16[208,256]{1,0:T(8,128)(2,1)S(1)}, bf16[208,256]{1,0:T(8,128)(2,1)S(1)}, u32[]{:S(2)}, u32[]{:S(2)}) collective-permute-start(bf16[208,256]{1,0:T(8,128)(2,1)S(1)} %pack.1.refs_0_), channel_id=1, source_target_pairs={{0,3},{1,2},{2,1},{3,0},{4,7},{5,6},{6,5},{7,4},{8,11},{9,10},{10,... | collective-permute-start | bytes 319496 | tf_op jit(solution)/shard_map/ppermute | solution.py:434
  34.8 6.8 %collective-permute-start.16 = (bf16[208,256]{1,0:T(8,128)(2,1)S(1)}, bf16[208,256]{1,0:T(8,128)(2,1)S(1)}, u32[]{:S(2)}, u32[]{:S(2)}) collective-permute-start(bf16[208,256]{1,0:T(8,128)(2,1)S(1)} %pack.1.refs_0_), channel_id=1, source_target_pairs={{0,2},{1,3},{2,0},{3,1},{4,6},{5,7},{6,4},{7,5},{8,10},{9,11},{10,... | collective-permute-start | bytes 319496 | tf_op jit(solution)/shard_map/ppermute | solution.py:434
  35.6 6.0 %collective-permute-start.15 = (bf16[208,256]{1,0:T(8,128)(2,1)S(1)}, bf16[208,256]{1,0:T(8,128)(2,1)S(1)}, u32[]{:S(2)}, u32[]{:S(2)}) collective-permute-start(bf16[208,256]{1,0:T(8,128)(2,1)S(1)} %pack.1.refs_0_), channel_id=1, source_target_pairs={{0,1},{1,0},{2,3},{3,2},{4,5},{5,4},{6,7},{7,6},{8,9},{9,8},{10,11... | collective-permute-start | bytes 319496 | tf_op jit(solution)/shard_map/ppermute | solution.py:434
  36.1 5.5 %collective-permute-start.12 = (bf16[128,256]{1,0:T(8,128)(2,1)S(1)}, bf16[128,256]{1,0:T(8,128)(2,1)S(1)}, u32[]{:S(2)}, u32[]{:S(2)}) collective-permute-start(bf16[128,256]{1,0:T(8,128)(2,1)S(1)} %get-tuple-element.49.outgoing_ref), channel_id=1, source_target_pairs={{0,8},{1,9},{2,10},{3,11},{4,12},{5,13},{6,14},{7,15},{8,0},{9,1},... | collective-permute-start | bytes 196616 | tf_op jit(solution)/shard_map/ppermute | solution.py:440
  36.6 5.0 %collective-permute-start.11 = (bf16[128,256]{1,0:T(8,128)(2,1)S(1)}, bf16[128,256]{1,0:T(8,128)(2,1)S(1)}, u32[]{:S(2)}, u32[]{:S(2)}) collective-permute-start(bf16[128,256]{1,0:T(8,128)(2,1)S(1)} %get-tuple-element.49.outgoing_ref), channel_id=1, source_target_pairs={{0,4},{1,5},{2,6},{3,7},{4,0},{5,1},{6,2},{7,3},{8,12},{9,13},{10,... | collective-permute-start | bytes 196616 | tf_op jit(solution)/shard_map/ppermute | solution.py:440
  41.7 8.8 %collective-permute-start.20 = (bf16[3,128,256]{2,1,0:T(8,128)(2,1)S(1)}, bf16[3,128,256]{2,1,0:T(8,128)(2,1)S(1)}, u32[]{:S(2)}, u32[]{:S(2)}) collective-permute-start(bf16[3,128,256]{2,1,0:T(8,128)(2,1)S(1)} %stack_line.1.refs_2_), channel_id=1, source_target_pairs={{0,3},{1,2},{2,1},{3,0},{4,7},{5,6},{6,5},{7,4},{8,11},{9,10},{10,... | collective-permute-start | bytes 589832 | tf_op jit(solution)/shard_map/ppermute | solution.py:434
  43.7 10.8 %collective-permute-start.19 = (bf16[3,128,256]{2,1,0:T(8,128)(2,1)S(1)}, bf16[3,128,256]{2,1,0:T(8,128)(2,1)S(1)}, u32[]{:S(2)}, u32[]{:S(2)}) collective-permute-start(bf16[3,128,256]{2,1,0:T(8,128)(2,1)S(1)} %stack_line.1.refs_2_), channel_id=1, source_target_pairs={{0,1},{1,0},{2,3},{3,2},{4,5},{5,4},{6,7},{7,6},{8,9},{9,8},{10,11... | collective-permute-start | bytes 589832 | tf_op jit(solution)/shard_map/ppermute | solution.py:434
  44.5 9.9 %collective-permute-start.18 = (bf16[3,128,256]{2,1,0:T(8,128)(2,1)S(1)}, bf16[3,128,256]{2,1,0:T(8,128)(2,1)S(1)}, u32[]{:S(2)}, u32[]{:S(2)}) collective-permute-start(bf16[3,128,256]{2,1,0:T(8,128)(2,1)S(1)} %stack_line.1.refs_2_), channel_id=1, source_target_pairs={{0,2},{1,3},{2,0},{3,1},{4,6},{5,7},{6,4},{7,5},{8,10},{9,11},{10,... | collective-permute-start | bytes 589832 | tf_op jit(solution)/shard_map/ppermute | solution.py:434
  45.2 6.3 %collective-permute-start.23 = (bf16[80,256]{1,0:T(8,128)(2,1)S(1)}, bf16[80,256]{1,0:T(8,128)(2,1)S(1)}, u32[]{:S(2)}, u32[]{:S(2)}) collective-permute-start(bf16[80,256]{1,0:T(8,128)(2,1)S(1)} %sum_terms.1.refs_5_), channel_id=1, source_target_pairs={{0,12},{1,13},{2,14},{3,15},{4,8},{5,9},{6,10},{7,11},{8,4},{9,5},... | collective-permute-start | bytes 122888 | tf_op jit(solution)/shard_map/ppermute | solution.py:440
  47.5 4.9 %collective-permute-start.22 = (bf16[80,256]{1,0:T(8,128)(2,1)S(1)}, bf16[80,256]{1,0:T(8,128)(2,1)S(1)}, u32[]{:S(2)}, u32[]{:S(2)}) collective-permute-start(bf16[80,256]{1,0:T(8,128)(2,1)S(1)} %sum_terms.1.refs_5_), channel_id=1, source_target_pairs={{0,8},{1,9},{2,10},{3,11},{4,12},{5,13},{6,14},{7,15},{8,0},{9,1},... | collective-permute-start | bytes 122888 | tf_op jit(solution)/shard_map/ppermute | solution.py:440
  50.5 4.0 %collective-permute-start.21 = (bf16[80,256]{1,0:T(8,128)(2,1)S(1)}, bf16[80,256]{1,0:T(8,128)(2,1)S(1)}, u32[]{:S(2)}, u32[]{:S(2)}) collective-permute-start(bf16[80,256]{1,0:T(8,128)(2,1)S(1)} %sum_terms.1.refs_5_), channel_id=1, source_target_pairs={{0,4},{1,5},{2,6},{3,7},{4,0},{5,1},{6,2},{7,3},{8,12},{9,13},{10,... | collective-permute-start | bytes 122888 | tf_op jit(solution)/shard_map/ppermute | solution.py:440
  54.8 1.4 %collective-permute-start.24 = (bf16[208,256]{1,0:T(8,128)(2,1)S(1)}, bf16[208,256]{1,0:T(8,128)(2,1)S(1)}, u32[]{:S(2)}, u32[]{:S(2)}) collective-permute-start(bf16[208,256]{1,0:T(8,128)(2,1)S(1)} %backward_product.5.sent_ref), channel_id=1, source_target_pairs={{0,16},{16,0},{1,17},{17,1},{2,18},{18,2},{3,19},{19,3},{4,20},{20... | collective-permute-start | bytes 319496 | tf_op jit(solution)/shard_map/ppermute | solution.py:428
